TPU v7x, 32 devices: a whole 2x2x4 slice. The times are simulated.
32 devices in a mesh: blk: 32 (over z, y, x, core).
Axes of the slice: x: 2, y: 2, z: 4, core: 2. Of those that a mesh axis runs over, the one named last changes fastest.
Arguments:
- images: bfloat16 [12800, 768], P('blk'), may hold values from -6 to 6
- captions: bfloat16 [20480, 768], P('blk'), may hold values from -6 to 6
- img_gain1: bfloat16 [768], replicated, may hold values from 0.5 to 1.5
- img_bias1: bfloat16 [768], replicated, may hold values from -3 to 3
- img_qkv: bfloat16 [1769472], P('blk'), may hold values from -0.21875 to 0.21875
- img_out: bfloat16 [589824], P('blk'), may hold values from -0.5 to 0.5
- img_gain2: bfloat16 [768], replicated, may hold values from 0.5 to 1.5
- img_bias2: bfloat16 [768], replicated, may hold values from -3 to 3
- img_up: bfloat16 [2359296], P('blk'), may hold values from -0.21875 to 0.21875
- img_down: bfloat16 [2359296], P('blk'), may hold values from -0.109375 to 0.109375
- txt_gain1: float32 [768], replicated, may hold values from 0.5 to 1.5
- txt_bias1: float32 [768], replicated, may hold values from -3 to 3
- txt_qkv: bfloat16 [768, 2304], replicated, may hold values from -0.21875 to 0.21875
- txt_out: bfloat16 [768, 768], replicated, may hold values from -0.4375 to 0.4375
- txt_gain2: float32 [768], replicated, may hold values from 0.5 to 1.5
- txt_bias2: float32 [768], replicated, may hold values from -3 to 3
- txt_up: bfloat16 [768, 3072], replicated, may hold values from -0.21875 to 0.21875
- txt_down: bfloat16 [3072, 768], replicated, may hold values from -0.109375 to 0.109375
- counts: int32 [256], P('blk'), may hold values from 1 to 5, as said below
- matches: int32 [1280, 256], P('blk'), may hold values 0 or 1
Outputs:
- loss: float32 [], replicated
- caption_grad: float32 [20480, 768], P('blk')
- grad_gain1: float32 [768], replicated
- grad_bias1: float32 [768], replicated
- grad_qkv: float32 [1769472], P('blk')
- grad_out: float32 [589824], P('blk')
- grad_gain2: float32 [768], replicated
- grad_bias2: float32 [768], replicated
- grad_up: float32 [2359296], P('blk')
- grad_down: float32 [2359296], P('blk')
Inputs may be any that keep to these rules, and one draw needn't show every extreme that they name: `counts`: each image has 1 to 5 captions; in every draw all 8 images of one block have 5, so that block's 40 caption slots are all live.
All inputs are finite; a program needn't handle non-finite values. No bound on the sum of `matches` on one device may be relied on, other than what follows from the above.
Results may differ from a plain program's by a relative error of at most 0.015.
Values may be sent and summed in bfloat16 or wider, within the bound.
No kernel may reach another device: no remote copies, remote signals or barrier semaphores. Data moves between devices by JAX's collectives and lax.ppermute only.
A program may use at most 192 MiB of HBM per device.

v0:
```python
import functools

import jax
import jax.numpy as jnp
from jax import lax
from jax.experimental import pallas as pl
from jax.experimental.pallas import tpu as pltpu
from jax.sharding import PartitionSpec as P

D = 768
FF = 3072
HEAD = 64
HEADS = D // HEAD
IMG_LEN = 50
TXT_LEN = 16
AXIS = "blk"

norm_eps = 1e-06
logit_scale = 50.0
f32 = jnp.float32
bf16 = jnp.bfloat16


def swapped(value, mask):
    peers = lax.axis_size(AXIS)
    return lax.ppermute(value, AXIS, [(i, i ^ mask) for i in range(peers)])


def bit_masks():
    peers = lax.axis_size(AXIS)
    return [1 << k for k in range(peers.bit_length() - 1)]


def joined(held, other, mask):
    upper = (lax.axis_index(AXIS) & mask) > 0
    first = jnp.where(upper, other, held)
    second = jnp.where(upper, held, other)
    return jnp.stack([first, second], axis=1).reshape((-1,) + held.shape[1:])


def spread(block):
    peers = lax.axis_size(AXIS)
    copies = jnp.broadcast_to(block[None], (peers,) + block.shape)
    return lax.all_to_all(copies, AXIS, split_axis=0, concat_axis=0, tiled=True)


def stage_orders():
    masks = bit_masks()
    head, tail = masks[:-2], masks[-2:]
    order_a = list(head)
    order_b = list(head)
    for k in range(1, len(head) - 1, 2):
        order_b[k], order_b[k + 1] = order_b[k + 1], order_b[k]
    return order_a, order_b, tail


def row_order(bits):
    peers = lax.axis_size(AXIS)
    own = lax.axis_index(AXIS)
    per = D // peers
    places = lax.iota(jnp.int32, D)
    block = places // per
    target = jnp.zeros_like(block) + own
    for k, mask in enumerate(bits):
        target = target ^ (((block >> (len(bits) - 1 - k)) & 1) * mask)
    source = target * per + places % per
    return (source[:, None] == lax.iota(jnp.int32, D)[None, :]).astype(bf16)


def gathered_line(shard):
    return jnp.concatenate([shard] + [swapped(shard, mask) for mask in (8, 16, 24)], axis=0)


def gathered_rows(line, beside, above):
    half = line.shape[0] // 2
    pieces = [line, beside, above, swapped(beside[:half], 4), swapped(above[half:], 2)]
    return pieces + [swapped(piece, 1) for piece in pieces]


def in_turn(first, then):
    return lax.optimization_barrier((first, then))


def placed(order, values):
    return mul_bt(order, values).astype(bf16)


def hand_on(parts, stage):
    order_a, order_b, _ = stage_orders()
    keep_a, send_a, keep_b, send_b = parts
    return keep_a, swapped(send_a, order_a[stage]), keep_b, swapped(send_b, order_b[stage])


def hand_on_last(blocks):
    low, high = stage_orders()[2]
    own, *others = blocks
    return own, [swapped(block, mask) for block, mask in zip(others, (low, high, low | high))]


def sum_last(own, others):
    total = own
    for other in others:
        total = total + other.astype(f32)
    return total


VMEM_BYTES = 56 << 20
TILE = 512


def norm_parts(values):
    average = jnp.mean(values, axis=-1, keepdims=True)
    centred = values - average
    variance = jnp.mean(centred * centred, axis=-1, keepdims=True)
    scale = lax.rsqrt(variance + norm_eps)
    return centred * scale, scale


def norm_back(unit, scale, gain, grad):
    inner = grad * gain
    shift = jnp.mean(inner, axis=-1, keepdims=True)
    along = jnp.mean(inner * unit, axis=-1, keepdims=True)
    return scale * (inner - shift - unit * along)


def mul(lhs, rhs):
    return jnp.dot(lhs, rhs, preferred_element_type=f32)


def mul_bt(lhs, rhs):
    return lax.dot_general(lhs, rhs, (((1,), (1,)), ((), ())), preferred_element_type=f32)


def mul_at(lhs, rhs):
    return lax.dot_general(lhs, rhs, (((0,), (0,)), ((), ())), preferred_element_type=f32)


def params(**more):
    return pltpu.CompilerParams(vmem_limit_bytes=VMEM_BYTES, **more)


def cost(flops, moved, transcendentals=0):
    return pl.CostEstimate(flops=flops, bytes_accessed=moved, transcendentals=transcendentals)


def lane_halves(dtype):
    lane = lax.broadcasted_iota(jnp.int32, (1, 2 * HEAD), 1)
    low = jnp.where(lane < HEAD, 1.0, 0.0)
    return low.astype(dtype), (1.0 - low).astype(dtype)


def two_heads(pair):
    low, high = lane_halves(bf16)
    return jnp.concatenate([pair * low, pair * high], axis=0)


def same_sequence(rows, row0, cols, col0, seq_len):
    row = (lax.broadcasted_iota(jnp.int32, (rows, cols), 0) + row0) // seq_len
    col = (lax.broadcasted_iota(jnp.int32, (rows, cols), 1) + col0) // seq_len
    return row == col


def masked_softmax(scores, mask):
    scores = jnp.where(mask, scores, -1e30)
    raised = jnp.exp(scores - jnp.max(scores, axis=-1, keepdims=True))
    return raised * (1.0 / jnp.sum(raised, axis=-1, keepdims=True))


def fold_kernel(keep_a, got_a, keep_b, got_b, *refs):
    outs = refs[-4:]
    half = outs[0].shape[0]
    for k, (kept, got) in enumerate(((keep_a, got_a), (keep_b, got_b))):
        for j in range(2):
            at = slice(j * half, (j + 1) * half)
            outs[2 * k + j][...] = (kept[at, :].astype(f32) + got[at, :].astype(f32)).astype(bf16)


def fold(parts, after=()):
    rows, cols = parts[0].shape
    if rows % 32:
        whole = [
            (kept.astype(f32) + got.astype(f32)).astype(bf16)
            for kept, got in (parts[:2], parts[2:])
        ]
        return [part for one in whole for part in (one[: rows // 2], one[rows // 2 :])]
    tile = 512
    return pl.pallas_call(
        fold_kernel,
        grid=(cols // tile,),
        out_shape=[jax.ShapeDtypeStruct((rows // 2, cols), bf16)] * 4,
        in_specs=[pl.BlockSpec((rows, tile), lambda i: (0, i))] * 4 + anywhere(after),
        out_specs=[pl.BlockSpec((rows // 2, tile), lambda i: (0, i))] * 4,
        compiler_params=params(),
        cost_estimate=cost(2 * rows * cols, 12 * rows * cols),
        name="fold",
    )(*parts, *after)


def fold_last_kernel(keep_a, got_a, keep_b, got_b, *refs):
    own_ref, *outs = refs[-4:]
    rows = own_ref.shape[0]
    cols = keep_a.shape[1]
    for k, (kept, got) in enumerate(((keep_a, got_a), (keep_b, got_b))):
        total = kept[...].astype(f32) + got[...].astype(f32)
        at = slice(k * cols, (k + 1) * cols)
        own_ref[:, at] = total[:rows]
        for j, out in enumerate(outs):
            out[:, at] = total[(j + 1) * rows : (j + 2) * rows].astype(bf16)


def fold_last(parts, after=()):
    rows, cols = parts[0].shape
    shape = (rows // 4, 2 * cols)
    if rows % 32:
        pairs = (parts[:2], parts[2:])
        both = [kept.astype(f32) + got.astype(f32) for kept, got in pairs]
        own, *others = jnp.split(jnp.concatenate(both, axis=1), 4)
        return [own] + [other.astype(bf16) for other in others]
    return pl.pallas_call(
        fold_last_kernel,
        out_shape=[jax.ShapeDtypeStruct(shape, f32)] + [jax.ShapeDtypeStruct(shape, bf16)] * 3,
        in_specs=[pl.BlockSpec(memory_space=pltpu.VMEM)] * 4 + anywhere(after),
        compiler_params=params(),
        cost_estimate=cost(2 * rows * cols, 12 * rows * cols),
        name="fold_last",
    )(*parts, *after)


def anywhere(after):
    return [pl.BlockSpec(memory_space=pl.ANY)] * len(after)


def pair_cols(part, pair):
    start = part * D + pair * 2 * HEAD
    return slice(start, start + 2 * HEAD)


def norm_rows(src, dst, gain, bias, step_rows):
    @pl.loop(0, src.shape[0] // step_rows)
    def _(step):
        at = pl.ds(pl.multiple_of(step * step_rows, step_rows), step_rows)
        unit, _ = norm_parts(src[at, :].astype(f32))
        dst[at, :] = (unit * gain + bias).astype(bf16)


def attend(qkv_ref, att_ref, q_rows, k_rows, mask):
    low, high = lane_halves(f32)
    for pair in range(HEADS // 2):
        queries = two_heads(qkv_ref[q_rows, pair_cols(0, pair)] * bf16(HEAD ** (-0.5)))
        scores = mul_bt(queries, qkv_ref[k_rows, pair_cols(1, pair)])
        probs = masked_softmax(scores, mask).astype(bf16)
        half = probs.shape[0] // 2
        mixed = mul(probs, qkv_ref[k_rows, pair_cols(2, pair)])
        att_ref[q_rows, pair_cols(0, pair)] = (mixed[:half] * low + mixed[half:] * high).astype(bf16)


def twice(mask):
    return jnp.concatenate([mask, mask], axis=0)


def text_front_kernel(
    x_ref, g1_ref, b1_ref, wqkv_ref, wo_ref, g2_ref, b2_ref, h1_ref, qkv_ref, att_ref, mid_ref,
    h2_ref, sum_ref
):
    rows, chunk = x_ref.shape[0], 128
    norm_rows(x_ref, h1_ref, g1_ref[...], b1_ref[...], chunk)

    @pl.loop(0, 3 * D // 256)
    def _(step):
        at = pl.ds(pl.multiple_of(step * 256, 256), 256)
        qkv_ref[:, at] = mul(h1_ref[...], wqkv_ref[:, at]).astype(bf16)

    mask = twice(same_sequence(chunk, 0, chunk, 0, TXT_LEN))

    @pl.loop(0, rows // chunk)
    def _(step):
        at = pl.ds(pl.multiple_of(step * chunk, chunk), chunk)
        attend(qkv_ref, att_ref, at, at, mask)

    @pl.loop(0, D // 256)
    def _(step):
        at = pl.ds(pl.multiple_of(step * 256, 256), 256)
        mid_ref[:, at] = x_ref[:, at].astype(f32) + mul(att_ref[...], wo_ref[:, at])

    norm_rows(mid_ref, h2_ref, g2_ref[...], b2_ref[...], chunk)
    per = chunk // TXT_LEN

    @pl.loop(0, rows // chunk)
    def _(step):
        values = mid_ref[pl.ds(pl.multiple_of(step * chunk, chunk), chunk), :]
        sum_ref[pl.ds(pl.multiple_of(step * per, per), per), :] = jnp.sum(
            values.reshape(per, TXT_LEN, D), axis=1
        )


def text_front(rows_in, gain1, bias1, wqkv, wo, gain2, bias2):
    rows = rows_in.shape[0]
    shapes = [
        ((rows, D), bf16),
        ((rows, 3 * D), bf16),
        ((rows, D), bf16),
        ((rows, D), f32),
        ((rows, D), bf16),
        ((rows // TXT_LEN, D), f32),
    ]
    return pl.pallas_call(
        text_front_kernel,
        out_shape=[jax.ShapeDtypeStruct(*item) for item in shapes],
        compiler_params=params(),
        cost_estimate=cost(rows * D * D * 8, 14 * D * rows + 8 * D * D, rows * 128 * HEADS),
        name="text_front",
    )(rows_in, gain1[None], bias1[None], wqkv, wo, gain2[None], bias2[None])


def image_front_kernel(
    windows, x_ref, perm_ref, g1_ref, b1_ref, g2_ref, b2_ref, *refs
):
    h2_ref, sum_ref, w_ref, h1_ref, placed_ref, qkv_ref, att_ref, mid_ref, sems = refs[-9:]
    rows, chunk = x_ref.shape[0], 80
    copies, row = [], 0
    for k, piece in enumerate(refs[:-9]):
        place = w_ref.at[pl.ds(row, piece.shape[0]), :]
        copies.append(pltpu.make_async_copy(piece, place, sems.at[k]))
        row += piece.shape[0]
    for copy in copies:
        copy.start()

    def place_columns(src):
        @pl.loop(0, D // 256)
        def _(step):
            at = pl.ds(pl.multiple_of(step * 256, 256), 256)
            placed_ref[:, at] = mul_bt(src[...], perm_ref[at, :]).astype(bf16)

    norm_rows(x_ref, h1_ref, g1_ref[...].astype(f32), b1_ref[...].astype(f32), chunk)
    place_columns(h1_ref)
    for copy in copies:
        copy.wait()

    @pl.loop(0, 3 * D // 256)
    def _(step):
        at = pl.ds(pl.multiple_of(step * 256, 256), 256)
        qkv_ref[:, at] = mul(placed_ref[...], w_ref[:, at]).astype(bf16)

    for row0, count, key0, keys in windows:
        mask = twice(same_sequence(count, row0, keys, key0, IMG_LEN))
        attend(qkv_ref, att_ref, pl.ds(row0, count), pl.ds(key0, keys), mask)
    place_columns(att_ref)

    @pl.loop(0, D // 256)
    def _(step):
        at = pl.ds(pl.multiple_of(step * 256, 256), 256)
        there = pl.ds(pl.multiple_of(step * 256 + 3 * D, 256), 256)
        mid_ref[:, at] = x_ref[:, at].astype(f32) + mul(placed_ref[...], w_ref[:, there])

    norm_rows(mid_ref, h2_ref, g2_ref[...].astype(f32), b2_ref[...].astype(f32), chunk)
    for k in range(rows // IMG_LEN):
        first, last = k * IMG_LEN, (k + 1) * IMG_LEN
        start, end = first // 8 * 8, -(-last // 8) * 8
        values = mid_ref[start:end, :]
        place = lax.broadcasted_iota(jnp.int32, values.shape, 0) + start
        inside = (place >= first) & (place < last)
        sum_ref[k : k + 1, :] = jnp.sum(jnp.where(inside, values, 0.0), axis=0, keepdims=True)


def image_front(rows_in, pieces, perm, gain1, bias1, gain2, bias2):
    rows = rows_in.shape[0]
    windows = ((0, 208, 0, 256), (208, 192, 192, 208))
    vmem = pl.BlockSpec(memory_space=pltpu.VMEM)
    return pl.pallas_call(
        functools.partial(image_front_kernel, windows),
        out_shape=[
            jax.ShapeDtypeStruct((rows, D), bf16),
            jax.ShapeDtypeStruct((rows // IMG_LEN, D), f32),
        ],
        in_specs=[vmem] * 6 + anywhere(pieces),
        out_specs=[vmem] * 2,
        scratch_shapes=[
            pltpu.VMEM((D, 4 * D), bf16),
            pltpu.VMEM((rows, D), bf16),
            pltpu.VMEM((rows, D), bf16),
            pltpu.VMEM((rows, 3 * D), bf16),
            pltpu.VMEM((rows, D), bf16),
            pltpu.VMEM((rows, D), f32),
            pltpu.SemaphoreType.DMA((len(pieces),)),
        ],
        compiler_params=params(),
        cost_estimate=cost(rows * D * D * 12, 8 * D * D, rows * 256 * HEADS),
        name="image_front",
    )(rows_in, perm, gain1[None], bias1[None], gain2[None], bias2[None], *pieces)


def gelu_parts(inner):
    half = 0.5 * (1.0 + lax.erf(inner * (0.5**0.5)))
    return inner * half, half


def pack_kernel(unit_ref, pos_ref, *refs):
    refs[-1][:, :D] = unit_ref[...].astype(bf16)
    refs[-1][:, D:] = pos_ref[...]


def packed(unit, positive, after):
    shape = (unit.shape[0], D + positive.shape[1])
    return pl.pallas_call(
        pack_kernel,
        out_shape=jax.ShapeDtypeStruct(shape, bf16),
        in_specs=[pl.BlockSpec(memory_space=pltpu.VMEM)] * 2 + anywhere(after),
        compiler_params=params(),
        cost_estimate=cost(shape[0] * shape[1], 4 * shape[0] * shape[1]),
        name="packed",
    )(unit, positive, *after)


def pool_matrix(count, rows, row0, seq_len):
    row = (lax.broadcasted_iota(jnp.int32, (count, rows), 1) + row0) // seq_len
    return jnp.where(row == lax.broadcasted_iota(jnp.int32, (count, rows), 0), 1.0, 0.0).astype(bf16)


def two_terms(mean):
    high = mean.astype(bf16)
    low = (mean - high.astype(f32)).astype(bf16)
    return jnp.concatenate([high, low], axis=0)


def unit_rows(pooled):
    inverse = lax.rsqrt(jnp.sum(pooled * pooled, axis=-1, keepdims=True) + norm_eps)
    return pooled * inverse, inverse


def text_up_kernel(h2_ref, wu_ref, wd_ref, sum_ref, *refs):
    slope_ref, hid_ref, unit_ref, inv_ref, acc = refs[-5:]
    step = pl.program_id(0)
    chunk = 128
    per = chunk // TXT_LEN
    pool = pool_matrix(per, chunk, 0, TXT_LEN)
    for k in range(h2_ref.shape[0] // chunk):
        inner = mul(h2_ref[k * chunk : (k + 1) * chunk, :], wu_ref[...])
        value, half = gelu_parts(inner)
        slope = half + inner * (jnp.exp(-0.5 * inner * inner) * 0.3989422804014327)
        slope_ref[k * chunk : (k + 1) * chunk, :] = slope.astype(bf16)
        hid_ref[k * per : (k + 1) * per, :] = mul(pool, value.astype(bf16))
    terms = mul(two_terms(hid_ref[...] * (1.0 / TXT_LEN)), wd_ref[...])
    count = hid_ref.shape[0]
    added = terms[:count] + terms[count:]

    @pl.when(step == 0)
    def _():
        acc[...] = sum_ref[...] * (1.0 / TXT_LEN) + added

    @pl.when(step > 0)
    def _():
        acc[...] += added

    @pl.when(step == pl.num_programs(0) - 1)
    def _():
        unit, inverse = unit_rows(acc[...])
        unit_ref[...] = unit
        inv_ref[...] = jnp.broadcast_to(inverse, inv_ref.shape)


def text_up(normed2, weight_up, weight_down, middle_sum, after=()):
    rows, count = normed2.shape[0], middle_sum.shape[0]
    fixed = lambda shape: pl.BlockSpec(shape, lambda i: (0, 0))
    return pl.pallas_call(
        text_up_kernel,
        grid=(FF // TILE,),
        out_shape=[
            jax.ShapeDtypeStruct((rows, FF), bf16),
            jax.ShapeDtypeStruct((count, FF), f32),
            jax.ShapeDtypeStruct((count, D), f32),
            jax.ShapeDtypeStruct((count, 128), f32),
        ],
        in_specs=[
            fixed((rows, D)),
            pl.BlockSpec((D, TILE), lambda i: (0, i)),
            pl.BlockSpec((TILE, D), lambda i: (i, 0)),
            fixed((count, D)),
        ]
        + anywhere(after),
        out_specs=[
            pl.BlockSpec((rows, TILE), lambda i: (0, i)),
            pl.BlockSpec((count, TILE), lambda i: (0, i)),
            fixed((count, D)),
            fixed((count, 128)),
        ],
        scratch_shapes=[pltpu.VMEM((count, D), f32)],
        compiler_params=params(),
        cost_estimate=cost(2 * rows * D * FF, 4 * D * FF + 2 * rows * FF, 20 * rows * FF),
        name="text_up",
    )(normed2, weight_up, weight_down, middle_sum, *after)


def image_up_kernel(fold, h2_ref, wu_ref, wd_ref, sum_ref, *refs):
    out_ref, acc = refs[-2:]
    step = pl.program_id(0)
    rows, count = h2_ref.shape[0], sum_ref.shape[0]
    chunk = 80
    summed = jnp.zeros((count, TILE), f32)
    for k in range(rows // chunk):
        inner = mul(h2_ref[k * chunk : (k + 1) * chunk, :], wu_ref[...])
        value, _ = gelu_parts(inner)
        pool = pool_matrix(count, chunk, k * chunk, IMG_LEN)
        summed = summed + mul(pool, value.astype(bf16))
    mean = two_terms(summed * (1.0 / IMG_LEN))
    place = lax.broadcasted_iota(jnp.int32, (TILE, TILE // fold), 0)
    picked = lax.broadcasted_iota(jnp.int32, (TILE, TILE // fold), 1) * fold
    terms = jnp.zeros((2 * count, D), f32)
    for k in range(fold):
        chosen = jnp.where(place == picked + k, 1.0, 0.0).astype(bf16)
        part = mul(mean, chosen).astype(bf16)
        terms = terms + mul(part, wd_ref[:, k * D : (k + 1) * D])
    added = terms[:count] + terms[count:]

    @pl.when(step == 0)
    def _():
        acc[...] = sum_ref[...] * (1.0 / IMG_LEN) + added

    @pl.when(step > 0)
    def _():
        acc[...] += added

    @pl.when(step == pl.num_programs(0) - 1)
    def _():
        out_ref[...] = unit_rows(acc[...])[0].astype(bf16)


def image_up(normed2, whole, up_col, down_col, middle_sum, after=()):
    rows, count = normed2.shape[0], middle_sum.shape[0]
    fold = FF // D
    fixed = lambda shape: pl.BlockSpec(shape, lambda i: (0, 0))
    return pl.pallas_call(
        functools.partial(image_up_kernel, fold),
        grid=(FF // TILE,),
        out_shape=jax.ShapeDtypeStruct((count, D), bf16),
        in_specs=[
            fixed((rows, D)),
            pl.BlockSpec((D, TILE), lambda i: (0, up_col // TILE + i)),
            pl.BlockSpec((TILE // fold, fold * D), lambda i: (i, down_col // (fold * D))),
            fixed((count, D)),
        ]
        + anywhere(after),
        out_specs=fixed((count, D)),
        scratch_shapes=[pltpu.VMEM((count, D), f32)],
        compiler_params=params(),
        cost_estimate=cost(2 * rows * D * FF, 4 * D * FF, 15 * rows * FF),
        name="image_up",
    )(normed2, whole, whole, middle_sum, *after)


def loss_parts(text_rows, pos, image_all):
    similar = mul_bt(text_rows, image_all) * logit_scale
    shifted = jnp.exp(similar - logit_scale)
    alive = jnp.max(pos, axis=1, keepdims=True)
    row_sum = jnp.sum(shifted, axis=1, keepdims=True)
    row_count = jnp.maximum(jnp.sum(pos, axis=1, keepdims=True), 1.0)
    return similar, shifted, alive, row_sum, row_count


def sums_over_captions(text_rows, pos, image_all):
    similar, shifted, alive, row_sum, row_count = loss_parts(text_rows, pos, image_all)
    pos_similar = pos * similar
    cap_term = alive * (
        logit_scale + jnp.log(row_sum) - jnp.sum(pos_similar, axis=1, keepdims=True) / row_count
    )
    return (
        jnp.sum(alive * shifted, axis=0, keepdims=True),
        jnp.sum(pos, axis=0, keepdims=True),
        jnp.sum(pos_similar, axis=0, keepdims=True),
        jnp.sum(cap_term, axis=0, keepdims=True),
        jnp.sum(alive, axis=0, keepdims=True),
    )


def loss_from(sums):
    col_sum, col_count, col_pos, cap_total, live_total = sums
    img_term = logit_scale + jnp.log(col_sum) - col_pos / col_count
    return 0.5 * cap_total / live_total + 0.5 * jnp.mean(img_term, axis=1, keepdims=True)


def grad_of_unit(text_rows, pos, image_all, col_sum, col_count, live_total):
    _, shifted, alive, row_sum, row_count = loss_parts(text_rows, pos, image_all)
    cap_share, img_share = 0.5 / live_total, 0.5 / image_all.shape[0]
    grad_sims = alive * shifted * (cap_share / row_sum + img_share / col_sum) - pos * (
        cap_share / row_count + img_share / col_count
    )
    return mul(grad_sims.astype(bf16), image_all) * logit_scale


def turned(grad, unit):
    return grad - unit * jnp.sum(grad * unit, axis=-1, keepdims=True)


def loss_kernel(
    pack_ref, image_ref, own_ref, unit_ref, inv_ref, loss_ref, row_ref, low_ref, col_sum_ref,
    col_count_ref, live_ref
):
    image_all = image_ref[...]
    chunk = 256
    total = None
    for k in range(pack_ref.shape[0] // chunk):
        at = slice(k * chunk, (k + 1) * chunk)
        part = sums_over_captions(pack_ref[at, :D], pack_ref[at, D:].astype(f32), image_all)
        total = part if total is None else [a + b for a, b in zip(total, part)]
    loss_ref[...] = jnp.broadcast_to(loss_from(total), loss_ref.shape)
    col_sum, col_count, _, _, live_total = total
    col_sum_ref[...] = col_sum
    col_count_ref[...] = col_count
    live_ref[...] = jnp.broadcast_to(live_total, live_ref.shape)
    grad = grad_of_unit(
        own_ref[:, :D], own_ref[:, D:].astype(f32), image_all, col_sum, col_count, live_total
    )
    row = inv_ref[:, :1] * turned(grad, unit_ref[...]) * (1.0 / TXT_LEN)
    row_ref[...] = row
    low_ref[...] = row.astype(bf16)


def loss_and_rows(pack, image_all, own_pack, unit, inverse):
    images, count = image_all.shape[0], own_pack.shape[0]
    shapes = [(1, 128), (count, D), (count, D), (1, images), (1, images), (1, 128)]
    kinds = [f32, f32, bf16, f32, f32, f32]
    return pl.pallas_call(
        loss_kernel,
        out_shape=[jax.ShapeDtypeStruct(*item) for item in zip(shapes, kinds)],
        compiler_params=params(),
        cost_estimate=cost(2 * pack.shape[0] * images * D, 2 * pack.size, pack.shape[0] * images),
        name="loss_and_rows",
    )(pack, image_all, own_pack, unit, inverse)


def down_kernel(pack_ref, image_ref, col_sum_ref, col_count_ref, live_ref, hid_ref, *refs):
    step, out_ref = pl.program_id(0), refs[-1]
    text_rows = pack_ref[:, :D]
    grad = grad_of_unit(
        text_rows, pack_ref[:, D:].astype(f32), image_ref[...], col_sum_ref[...],
        col_count_ref[...], live_ref[:, :1]
    )
    rows = (turned(grad, text_rows.astype(f32)) * (1.0 / TXT_LEN)).astype(bf16)
    part = mul_at(hid_ref[...], rows)

    @pl.when(step == 0)
    def _():
        out_ref[...] = part

    @pl.when(step > 0)
    def _():
        out_ref[...] += part


def grad_of_down(pack, image_all, col_sum, col_count, live_total, hidden_cols, after):
    images, chunk = image_all.shape[0], 256
    fixed = lambda shape: pl.BlockSpec(shape, lambda i: (0, 0))
    per = hidden_cols.shape[1]
    return pl.pallas_call(
        down_kernel,
        grid=(pack.shape[0] // chunk,),
        out_shape=jax.ShapeDtypeStruct((per, D), f32),
        in_specs=[
            pl.BlockSpec((chunk, pack.shape[1]), lambda i: (i, 0)),
            fixed((images, D)), fixed((1, images)), fixed((1, images)), fixed((1, 128)),
            pl.BlockSpec((chunk, per), lambda i: (i, 0)),
        ]
        + anywhere(after),
        out_specs=fixed((per, D)),
        compiler_params=params(),
        cost_estimate=cost(4 * pack.shape[0] * images * D, 2 * pack.size, pack.shape[0] * images),
        name="grad_of_down",
    )(pack, image_all, col_sum, col_count, live_total, hidden_cols, *after)


def mlp_back_kernel(
    low_ref, wd_ref, slope_ref, wu_ref, lhs_ref, mid_ref, gain_ref, row_ref, keep_a, send_a, keep_b,
    send_b, out_ref, gain_out, bias_out, acc
):
    step = pl.program_id(0)
    count, rows = low_ref.shape[0], slope_ref.shape[0]
    half = D // 2
    hidden = mul_bt(low_ref[...], wd_ref[...])
    wide = jnp.broadcast_to(hidden[:, None, :], (count, TXT_LEN, TILE)).reshape(rows, TILE)
    inner = (wide * slope_ref[...].astype(f32)).astype(bf16)
    weight = mul(lhs_ref[0], inner).astype(bf16)

    @pl.when(step < pl.num_programs(0) // 2)
    def _():
        keep_a[...] = weight[:half]
        send_a[...] = weight[half:]

    @pl.when(step >= pl.num_programs(0) // 2)
    def _():
        keep_b[...] = weight[:half]
        send_b[...] = weight[half:]

    added = mul_bt(inner, wu_ref[...])

    @pl.when(step == 0)
    def _():
        acc[...] = added

    @pl.when(step > 0)
    def _():
        acc[...] += added

    @pl.when(step == pl.num_programs(0) - 1)
    def _():
        chunk = 128
        per = chunk // TXT_LEN
        gain = gain_ref[...]
        gain_out[...] = jnp.zeros_like(gain_out)
        bias_out[...] = jnp.zeros_like(bias_out)

        @pl.loop(0, rows // chunk)
        def _(k):
            at = pl.ds(pl.multiple_of(k * chunk, chunk), chunk)
            unit, scale = norm_parts(mid_ref[at, :])
            grad = acc[at, :]
            gain_out[...] += jnp.sum(grad * unit, axis=0, keepdims=True)
            bias_out[...] += jnp.sum(grad, axis=0, keepdims=True)
            row = row_ref[pl.ds(pl.multiple_of(k * per, per), per), :]
            row = jnp.broadcast_to(row[:, None, :], (per, TXT_LEN, D)).reshape(chunk, D)
            out_ref[at, :] = row + norm_back(unit, scale, gain, grad)


def mlp_back(grad_row, grad_low, weight_down, slope, weight_up, lhs, middle, gain):
    rows, count = slope.shape[0], grad_row.shape[0]
    steps = FF // TILE
    fixed = lambda shape: pl.BlockSpec(shape, lambda i: (0, 0))
    first = pl.BlockSpec((D // 2, TILE), lambda i: (0, jnp.minimum(i, steps // 2 - 1)))
    second = pl.BlockSpec((D // 2, TILE), lambda i: (0, jnp.maximum(i - steps // 2, 0)))
    part = jax.ShapeDtypeStruct((D // 2, FF // 2), bf16)
    line = jax.ShapeDtypeStruct((1, D), f32)
    return pl.pallas_call(
        mlp_back_kernel,
        grid=(steps,),
        out_shape=[part] * 4 + [jax.ShapeDtypeStruct((rows, D), f32), line, line],
        in_specs=[
            fixed((count, D)),
            pl.BlockSpec((TILE, D), lambda i: (i, 0)),
            pl.BlockSpec((rows, TILE), lambda i: (0, i)),
            pl.BlockSpec((D, TILE), lambda i: (0, i)),
            pl.BlockSpec((1, D, rows), lambda i: (i // (steps // 2), 0, 0)),
            fixed((rows, D)),
            fixed((1, D)),
            fixed((count, D)),
        ],
        out_specs=[first, first, second, second, fixed((rows, D)), fixed((1, D)), fixed((1, D))],
        scratch_shapes=[pltpu.VMEM((rows, D), f32)],
        compiler_params=params(),
        cost_estimate=cost(4 * rows * D * FF, 4 * D * FF + 2 * rows * FF + 2 * D * FF, rows * FF),
        name="mlp_back",
    )(grad_low, weight_down, slope, weight_up, lhs, middle, gain[None], grad_row)


def attention_back_kernel(grad_ref, wo_ref, qkv_ref, *refs):
    low_ref, out_ref = refs[-2:]
    chunk = grad_ref.shape[0]
    one = same_sequence(chunk, 0, chunk, 0, TXT_LEN)
    mask = jnp.concatenate([one, one], axis=0)
    low = grad_ref[...].astype(bf16)
    low_ref[...] = low
    grad_att = mul_bt(low, wo_ref[...]).astype(bf16)
    for pair in range(HEADS // 2):
        queries = two_heads(qkv_ref[:, pair_cols(0, pair)] * bf16(HEAD ** (-0.5)))
        keys = qkv_ref[:, pair_cols(1, pair)]
        vals = qkv_ref[:, pair_cols(2, pair)]
        grads = two_heads(grad_att[:, pair_cols(0, pair)])
        probs = masked_softmax(mul_bt(queries, keys), mask)
        grad_probs = mul_bt(grads, vals)
        along = jnp.sum(grad_probs * probs, axis=-1, keepdims=True)
        grad_scores = (probs * (grad_probs - along)).astype(bf16)
        side = jnp.concatenate([grad_scores[:chunk], grad_scores[chunk:]], axis=1)
        grad_q = mul(side, two_heads(keys)) * HEAD ** (-0.5)
        grad_k = mul_at(grad_scores, queries)
        grad_v = mul_at(probs.astype(bf16), grads)
        out_ref[:, pair_cols(0, pair)] = grad_q.astype(bf16)
        out_ref[:, pair_cols(1, pair)] = grad_k.astype(bf16)
        out_ref[:, pair_cols(2, pair)] = grad_v.astype(bf16)


def attention_back(grad_middle, weight_out, project, first, count, after=()):
    chunk = 128
    rows = count * chunk
    return pl.pallas_call(
        attention_back_kernel,
        grid=(count,),
        out_shape=[
            jax.ShapeDtypeStruct((rows, D), bf16),
            jax.ShapeDtypeStruct((rows, 3 * D), bf16),
        ],
        in_specs=[
            pl.BlockSpec((chunk, D), lambda i: (i + first, 0)),
            pl.BlockSpec((D, D), lambda i: (0, 0)),
            pl.BlockSpec((chunk, 3 * D), lambda i: (i + first, 0)),
        ]
        + anywhere(after),
        out_specs=[
            pl.BlockSpec((chunk, D), lambda i: (i, 0)),
            pl.BlockSpec((chunk, 3 * D), lambda i: (i, 0)),
        ],
        compiler_params=params(),
        cost_estimate=cost(10 * rows * D * D, 16 * rows * D + 2 * D * D, rows * 128 * HEADS),
        name="attention_back",
    )(grad_middle, weight_out, project, *after)


def mul_rows(lhs, parts):
    total, row = 0.0, 0
    for part in parts:
        total = total + mul(lhs[:, row : row + part.shape[0]], part[...])
        row += part.shape[0]
    return total


def weight_back_kernel(counts, lhs_ref, *refs):
    step, half = pl.program_id(0), D // 2
    keep, send = refs[-2:]
    row = 0
    for k, count in enumerate(counts):
        parts = refs[row : row + count]
        row += count

        @pl.when(step == k if len(counts) > 1 else step >= 0)
        def _(parts=parts):
            weight = mul_rows(lhs_ref[0], parts).astype(bf16)
            keep[...] = weight[:half]
            send[...] = weight[half:]


def weight_back(lhs, first, groups, blocks, after=()):
    rows = lhs.shape[2]
    steps = 2
    many = len(groups) > 1
    given = [part for group in groups for part in group]
    return pl.pallas_call(
        functools.partial(weight_back_kernel, [len(group) for group in groups]),
        grid=(steps,),
        out_shape=[jax.ShapeDtypeStruct((D // 2, steps * D), bf16)] * 2,
        in_specs=[pl.BlockSpec((1, D, rows), lambda i: (first + (i if many else 0), 0, 0))]
        + [
            pl.BlockSpec((part.shape[0], D), lambda i, col=col: (0, col + (0 if many else i)))
            for group, col in zip(groups, blocks)
            for part in group
        ]
        + anywhere(after),
        out_specs=[pl.BlockSpec((D // 2, D), lambda i: (0, i))] * 2,
        compiler_params=params(),
        cost_estimate=cost(4 * rows * D * D, 4 * rows * D + 7 * D * D),
        name="weight_back",
    )(lhs, *given, *after)


def input_back_kernel(count, *refs):
    projs = refs[:count]
    w_ref, x_ref, gain_ref, mid_ref = refs[count : count + 4]
    out_ref, gain_out, bias_out, acc = refs[-4:]
    step = pl.program_id(0)
    rows, chunk = x_ref.shape[0], 128
    row = 0
    for part in projs:
        at = slice(row, row + part.shape[0])
        row += part.shape[0]
        added = mul_bt(part[...], w_ref[...])

        @pl.when(step == 0)
        def _(at=at, added=added):
            acc[at, :] = added

        @pl.when(step > 0)
        def _(at=at, added=added):
            acc[at, :] += added

    @pl.when(step == pl.num_programs(0) - 1)
    def _():
        gain = gain_ref[...]
        gain_out[...] = jnp.zeros_like(gain_out)
        bias_out[...] = jnp.zeros_like(bias_out)

        @pl.loop(0, rows // chunk)
        def _(k):
            at = pl.ds(pl.multiple_of(k * chunk, chunk), chunk)
            unit, scale = norm_parts(x_ref[at, :].astype(f32))
            grad = acc[at, :]
            gain_out[...] += jnp.sum(grad * unit, axis=0, keepdims=True)
            bias_out[...] += jnp.sum(grad, axis=0, keepdims=True)
            out_ref[at, :] = mid_ref[at, :] + norm_back(unit, scale, gain, grad)


def input_back(grad_projs, weight, rows_in, gain, grad_middle, after=()):
    rows = rows_in.shape[0]
    fixed = lambda shape: pl.BlockSpec(shape, lambda i: (0, 0))
    line = jax.ShapeDtypeStruct((1, D), f32)
    return pl.pallas_call(
        functools.partial(input_back_kernel, len(grad_projs)),
        grid=(3,),
        out_shape=[jax.ShapeDtypeStruct((rows, D), f32), line, line],
        in_specs=[pl.BlockSpec((part.shape[0], D), lambda i: (0, i)) for part in grad_projs]
        + [
            pl.BlockSpec((D, D), lambda i: (0, i)),
            fixed((rows, D)), fixed((1, D)), fixed((rows, D)),
        ]
        + anywhere(after),
        out_specs=[fixed((rows, D)), fixed((1, D)), fixed((1, D))],
        scratch_shapes=[pltpu.VMEM((rows, D), f32)],
        compiler_params=params(),
        cost_estimate=cost(6 * rows * D * D, 14 * rows * D + 6 * D * D),
        name="input_back",
    )(*grad_projs, weight, rows_in, gain[None], grad_middle, *after)


def local(
    images,
    captions,
    img_gain1,
    img_bias1,
    img_qkv,
    img_out,
    img_gain2,
    img_bias2,
    img_up,
    img_down,
    txt_gain1,
    txt_bias1,
    txt_qkv,
    txt_out,
    txt_gain2,
    txt_bias2,
    txt_up,
    txt_down,
    counts,
    matches,
):
    peers = lax.axis_size(AXIS)
    own = lax.axis_index(AXIS)
    per = D // peers
    img_local = counts.shape[0]
    cap_local = matches.shape[0]
    total_images = matches.shape[1]

    whole = lax.all_gather(
        jnp.concatenate([img_up.reshape(per, FF), img_down.reshape(per, FF)], axis=1),
        AXIS,
        axis=0,
        tiled=True,
    )
    small = peers == 32
    shard = jnp.concatenate([img_qkv.reshape(per, 3 * D), img_out.reshape(per, D)], axis=1)
    if small:
        line, perm = gathered_line(shard), row_order((1, 4, 2, 16, 8))
    else:
        line, perm = lax.all_gather(shard, AXIS, axis=0, tiled=True), jnp.eye(D, dtype=bf16)

    normed1, project, attended, middle, normed2, middle_sum = text_front(
        captions, txt_gain1, txt_bias1, txt_qkv, txt_out, txt_gain2, txt_bias2
    )
    middle_sum, line = in_turn(middle_sum, line)
    beside, above = (swapped(line, 2), swapped(line, 4)) if small else (line, line)
    slope, hidden_sum, text_unit, inverse = text_up(
        normed2, txt_up, txt_down, middle_sum, (line,)
    )
    text_unit, (beside, above) = in_turn(text_unit, (beside, above))
    pieces = gathered_rows(line, beside, above) if small else [line]

    ends_at = jnp.cumsum(counts)
    slot_ids = lax.iota(jnp.int32, cap_local)
    owner = jnp.sum((ends_at[None, :] <= slot_ids[:, None]).astype(jnp.int32), axis=1)
    owner = owner + own * img_local
    live = slot_ids < ends_at[-1]
    columns = lax.iota(jnp.int32, total_images)
    positive = ((matches > 0) | (owner[:, None] == columns[None, :])) & live[:, None]

    own_pack = packed(text_unit, positive.astype(bf16), pieces[1:5] if small else ())

    normed_img, middle_img = image_front(
        images, pieces, perm, img_gain1, img_bias1, img_gain2, img_bias2
    )
    if small:
        held = own_pack[None]
        scaled_sum = (hidden_sum * inverse[:, :1]).astype(bf16)
        normed_img, scaled_sum, other = lax.optimization_barrier(
            (normed_img, scaled_sum, swapped(held, 16))
        )
        held = joined(held, other, 16)
        hidden_cols = lax.all_to_all(scaled_sum, AXIS, split_axis=1, concat_axis=0, tiled=True)
        held = joined(held, swapped(held, 8), 8)
        whole, other = in_turn(whole, swapped(held, 4))
        held = joined(held, other, 4)
        other = swapped(held, 2)
    image_low = image_up(normed_img, whole, 0, FF, middle_img)
    if small:
        image_low, other, hidden_cols = lax.optimization_barrier((image_low, other, hidden_cols))
        held = joined(held, other, 2)
        text_pack = joined(held, swapped(held, 1), 1).reshape(-1, D + total_images)
    image_all = spread(image_low).reshape(total_images, D)

    order_a, order_b, tail = stage_orders()
    matrix_a, matrix_b = row_order(order_a + tail[::-1]), row_order(order_b + tail[::-1])
    lhs_up = jnp.stack([placed(matrix_a, normed2), placed(matrix_b, normed2)])
    lhs_rest = jnp.stack(
        [placed(matrix_a, normed1), placed(matrix_b, normed1), placed(matrix_b, attended)]
    )

    if small:
        loss_value, grad_row, row_low, col_sum, col_count, live_total = loss_and_rows(
            text_pack, image_all, own_pack, text_unit, inverse
        )
        loss_value = loss_value[0, 0]
    else:
        text_low, pos = own_pack[:, :D], own_pack[:, D:].astype(f32)
        sums = lax.psum(sums_over_captions(text_low, pos, image_all), AXIS)
        loss_value = loss_from(sums)[0, 0]
        grad = grad_of_unit(text_low, pos, image_all, sums[0], sums[1], sums[4])
        grad_row = inverse[:, :1] * turned(grad, text_unit) * (1.0 / TXT_LEN)
        row_low = grad_row.astype(bf16)

    *up, grad_middle, gain_two, bias_two = mlp_back(
        grad_row, row_low, txt_down, slope, txt_up, lhs_up, middle, txt_gain2
    )
    stages = len(order_a)
    low_one, proj_one = attention_back(grad_middle, txt_out, project, 0, 2)
    for stage in range(stages - 2):
        up = fold(hand_on(up, stage), (proj_one,))
    low_two, proj_two = attention_back(grad_middle, txt_out, project, 2, 3, up)
    up = fold(hand_on(up, stages - 2), (proj_two,))
    projs, lows = (proj_one, proj_two), (low_one, low_two)
    rest_a = weight_back(lhs_rest, 0, [projs], [0], up)
    up = hand_on_last(fold_last(hand_on(up, stages - 1), rest_a[1:]))
    rest_b = weight_back(lhs_rest, 1, [projs, lows], [2, 0], up[:1])
    rest = [*rest_a, *rest_b]
    for stage in range(stages - 2):
        rest = fold(hand_on(rest, stage), up[1])
    caption_grad, gain_one, bias_one = input_back(
        projs, txt_qkv, captions, txt_gain1, grad_middle, rest[:1]
    )
    rest = fold(hand_on(rest, stages - 2), (caption_grad,))
    if small:
        grad_down = grad_of_down(
            text_pack, image_all, col_sum, col_count, live_total, hidden_cols, rest
        )
        rest = fold_last(hand_on(rest, stages - 1), (grad_down,))
    else:
        grad_down = lax.psum_scatter(
            mul_at(hidden_sum.astype(bf16), row_low), AXIS, scatter_dimension=0, tiled=True
        )
        rest = fold_last(hand_on(rest, stages - 1))
    up_share = sum_last(*up)
    rest_share = sum_last(*hand_on_last(rest))
    norms = jnp.concatenate([gain_one, bias_one, gain_two, bias_two], axis=0)
    norms = jnp.sum(spread(norms[None]), axis=0).reshape(4, D)
    return (
        loss_value,
        caption_grad,
        norms[0],
        norms[1],
        rest_share[:, : 3 * D].reshape(-1),
        rest_share[:, 3 * D :].reshape(-1),
        norms[2],
        norms[3],
        up_share.reshape(-1),
        grad_down.reshape(-1),
    )


def solution(mesh):
    split, flat, whole = P("blk", None), P("blk"), P()
    image_block = (whole, whole, flat, flat, whole, whole, flat, flat)
    return jax.shard_map(
        local,
        mesh=mesh,
        in_specs=(split, split) + image_block + (whole,) * 8 + (flat, split),
        out_specs=(whole, split, whole, whole, flat, flat, whole, whole, flat, flat),
        check_vma=False,
    )
```

profile of v0, /device:TPU:0, one launch (start us, length us, event | category | flops | bytes accessed | tf_op | source)
XLA Modules:
  0.0 336.2 jit_solution(15703712480437349934)
XLA Ops:
  11.9 5.1 %collective-permute-start.2 = (bf16[24,3072]{1,0:T(8,128)(2,1)S(1)}, bf16[24,3072]{1,0:T(8,128)(2,1)S(1)}, u32[]{:S(2)}, u32[]{:S(2)}) collective-permute-start(bf16[24,3072]{1,0:T(8,128)(2,1)S(1)} %constant_dynamic-update-slice_fusion), channel_id=1, source_target_pairs={{0,24},{1,25},{2,26},{3,27},{4,28},{5,29},{6,30},{7,31},{8,16},{9,... | collective-permute-start | bytes 442376 | tf_op jit(solution)/shard_map/ppermute | solution.py:26
  20.3 19.0 %text_front.1 = (bf16[640,768]{1,0:T(8,128)(2,1)}, bf16[640,2304]{1,0:T(8,128)(2,1)}, bf16[640,768]{1,0:T(8,128)(2,1)}, f32[640,768]{1,0:T(8,128)}, bf16[640,768]{1,0:T(8,128)(2,1)}, /*index=5*/f32[40,768]{1,0:T(8,128)}) custom-call(bf16[640,768]{1,0:T(8,128)(2,1)} %refs_3_.1, f32[1,768]{1,0:T(1,128)} %broadcast_in_dim.26.g1_ref.refs_4_, ...), custom_call_target="tpu_custom_call" | custom-call | flops 3019898880 | bytes 11599872 | tf_op jit(solution)/shard_map/text_front/pallas_call | solution.py:306
  47.5 13.7 %text_up.1 = (bf16[640,3072]{1,0:T(8,128)(2,1)}, f32[40,3072]{1,0:T(8,128)}, f32[40,768]{1,0:T(8,128)}, f32[40,128]{1,0:T(8,128)}) custom-call(bf16[640,768]{1,0:T(8,128)(2,1)} %get-tuple-element.85.h2_ref, bf16[768,3072]{1,0:T(8,128)(2,1)} %wu_ref.3, bf16[3072,768]{1,0:T(8,128)(2,1)} %wd_ref.3, f32[40,768]{1,0:T(8,128)} %get-tuple-element.86.sum_ref, ...), custom_call_target="tpu_custom_call" | custom-call | flops 3019898880 | bytes 13369344 | tf_op jit(solution)/shard_map/text_up/pallas_call | solution.py:464
  78.8 13.8 %image_front.1 = (bf16[400,768]{1,0:T(8,128)(2,1)}, f32[8,768]{1,0:T(8,128)}) custom-call(bf16[400,768]{1,0:T(8,128)(2,1)} %x_ref.3, bf16[768,768]{1,0:T(8,128)(2,1)} %fusion.5.perm_ref, bf16[1,768]{1,0:T(2,128)(2,1)} %broadcast_in_dim.22.g1_ref, bf16[1,768]{1,0:T(2,128)(2,1)} %broadcast_in_dim.23.b1_ref, bf16[1,768]{1,0:T(2,128)(2,1)} %broadcast_in_dim.24.g2_ref, ...), custom_call_target="tpu_custom_call" | custom-call | flops 2831155200 | bytes 4718592 | tf_op jit(solution)/shard_map/image_front/pallas_call | solution.py:369
  94.6 12.8 %collective-permute-done.13 = bf16[2,40,1024]{2,1,0:T(8,128)(2,1)S(1)} collective-permute-done((bf16[2,40,1024]{2,1,0:T(8,128)(2,1)S(1)}, bf16[2,40,1024]{2,1,0:T(8,128)(2,1)S(1)}, u32[]{:S(2)}, u32[]{:S(2)}) %collective-permute-start.13) | collective-permute-done | bytes 163872 | tf_op jit(solution)/shard_map/ppermute | solution.py:26
  109.0 8.4 %collective-permute-done.14 = bf16[4,40,1024]{2,1,0:T(8,128)(2,1)S(1)} collective-permute-done((bf16[4,40,1024]{2,1,0:T(8,128)(2,1)S(1)}, bf16[4,40,1024]{2,1,0:T(8,128)(2,1)S(1)}, u32[]{:S(2)}, u32[]{:S(2)}) %collective-permute-start.14) | collective-permute-done | bytes 327712 | tf_op jit(solution)/shard_map/ppermute | solution.py:26
  123.5 14.1 %image_up.1 = bf16[8,768]{1,0:T(8,128)(2,1)} custom-call(bf16[400,768]{1,0:T(8,128)(2,1)} %get-tuple-element.94.h2_ref, bf16[768,6144]{1,0:T(8,128)(2,1)} %all-gather.2.cloned.1.call-done.wu_ref.wd_ref, bf16[768,6144]{1,0:T(8,128)(2,1)} %all-gather.2.cloned.1.call-done.wu_ref.wd_ref, f32[8,768]{1,0:T(8,128)} %get-tuple-element.97.sum_ref), custom_call_target="tpu_custom_call" | custom-call | flops 1887436800 | bytes 9437184 | tf_op jit(solution)/shard_map/image_up/pallas_call | solution.py:531
  143.1 5.4 %all-to-all-start.1 = ((bf16[32,8,768]{2,1,0:T(8,128)(2,1)}), bf16[32,8,768]{2,1,0:T(8,128)(2,1)S(1)}, u32[]{:S(2)}, u32[]{:S(2)}) async-start(bf16[32,8,768]{2,1,0:T(8,128)(2,1)} %broadcast_in_dim.60), calls=%async_computation.1 | async-start | bytes 786432 | tf_op jit(solution)/shard_map/all_to_all | solution.py:44
  157.1 4.5 %all-to-all-done.1 = bf16[32,8,768]{2,1,0:T(8,128)(2,1)S(1)} async-done(((bf16[32,8,768]{2,1,0:T(8,128)(2,1)}), bf16[32,8,768]{2,1,0:T(8,128)(2,1)S(1)}, u32[]{:S(2)}, u32[]{:S(2)}) %all-to-all-start.1) | async-done | bytes 393248 | tf_op jit(solution)/shard_map/all_to_all | solution.py:44
  162.4 4.0 %loss_and_rows.1 = (f32[1,128]{1,0:T(1,128)}, f32[40,768]{1,0:T(8,128)}, bf16[40,768]{1,0:T(8,128)(2,1)}, f32[1,256]{1,0:T(1,128)}, f32[1,256]{1,0:T(1,128)}, /*index=5*/f32[1,128]{1,0:T(1,128)}) custom-call(bf16[1280,1024]{1,0:T(8,128)(2,1)} %bitcast.67, bf16[256,768]{1,0:T(8,128)(2,1)} %bitcast.70, bf16[40,1024]{1,0:T(8,128)(2,1)} %packed.1.own_ref, ...), custom_call_target="tpu_custom_call" | custom-call | flops 503316480 | bytes 2621440 | tf_op jit(solution)/shard_map/loss_and_rows/pallas_call | solution.py:621
  166.5 21.5 %mlp_back.1 = (bf16[384,1536]{1,0:T(8,128)(2,1)}, bf16[384,1536]{1,0:T(8,128)(2,1)}, bf16[384,1536]{1,0:T(8,128)(2,1)}, bf16[384,1536]{1,0:T(8,128)(2,1)}, f32[6...) custom-call(bf16[40,768]{1,0:T(8,128)(2,1)} %get-tuple-element.103.low_ref, bf16[3072,768]{1,0:T(8,128)(2,1)} %wd_ref.3, ...), custom_call_target="tpu_custom_call" | custom-call | flops 6039797760 | bytes 18087936 | tf_op jit(solution)/shard_map/mlp_back/pallas_call | solution.py:730
  189.8 9.2 %attention_back.2 = (bf16[256,768]{1,0:T(8,128)(2,1)}, bf16[256,2304]{1,0:T(8,128)(2,1)}) custom-call(f32[640,768]{1,0:T(8,128)} %get-tuple-element.107.grad_ref.refs_5_, bf16[768,768]{1,0:T(8,128)(2,1)} %wo_ref.5, bf16[640,2304]{1,0:T(8,128)(2,1)} %get-tuple-element.108.qkv_ref), custom_call_target="tpu_custom_call" | custom-call | flops 1509949440 | bytes 4325376 | tf_op jit(solution)/shard_map/attention_back/pallas_call | solution.py:781
  200.5 13.7 %fold.4 = (bf16[192,1536]{1,0:T(8,128)(2,1)}, bf16[192,1536]{1,0:T(8,128)(2,1)}, bf16[192,1536]{1,0:T(8,128)(2,1)}, bf16[192,1536]{1,0:T(8,128)(2,1)}) custom-call(bf16[384,1536]{1,0:T(8,128)(2,1)} %get-tuple-element.110.keep_a, bf16[384,1536]{1,0:T(8,128)(2,1)} %copy-done.8, bf16[384,1536]{1,0:T(8,128)(2,1)} %get-tuple-element.112.keep_b, ...), custom_call_target="tpu_custom_call" | custom-call | flops 1179648 | bytes 7077888 | tf_op jit(solution)/shard_map/fold/pallas_call | solution.py:187
  218.6 12.6 %attention_back.3 = (bf16[384,768]{1,0:T(8,128)(2,1)}, bf16[384,2304]{1,0:T(8,128)(2,1)}) custom-call(f32[640,768]{1,0:T(8,128)} %get-tuple-element.107.grad_ref.refs_5_, bf16[768,768]{1,0:T(8,128)(2,1)} %wo_ref.5, bf16[640,2304]{1,0:T(8,128)(2,1)} %get-tuple-element.108.qkv_ref, bf16[192,1536]{1,0:T(8,128)(2,1)} %get-tuple-element.114.refs_0_.keep_a, ...), custom_call_target="tpu_custom_call" | custom-call | flops 2264924160 | bytes 5898240 | tf_op jit(solution)/shard_map/attention_back/pallas_call | solution.py:781
  232.3 3.5 %fold.5 = (bf16[96,1536]{1,0:T(8,128)(2,1)}, bf16[96,1536]{1,0:T(8,128)(2,1)}, bf16[96,1536]{1,0:T(8,128)(2,1)}, bf16[96,1536]{1,0:T(8,128)(2,1)}) custom-call(bf16[192,1536]{1,0:T(8,128)(2,1)} %get-tuple-element.114.refs_0_.keep_a, bf16[192,1536]{1,0:T(8,128)(2,1)} %copy-done.20, bf16[192,1536]{1,0:T(8,128)(2,1)} %get-tuple-element.116.refs_2_.keep_b, ...), custom_call_target="tpu_custom_call" | custom-call | flops 589824 | bytes 3538944 | tf_op jit(solution)/shard_map/fold/pallas_call | solution.py:187
  239.8 4.7 %weight_back.2 = (bf16[384,1536]{1,0:T(8,128)(2,1)}, bf16[384,1536]{1,0:T(8,128)(2,1)}) custom-call(bf16[3,768,640]{2,1,0:T(8,128)(2,1)} %pad_maximum_fusion.lhs_ref, bf16[256,2304]{1,0:T(8,128)(2,1)} %get-tuple-element.109.refs_0_, bf16[384,2304]{1,0:T(8,128)(2,1)} %get-tuple-element.118.refs_0_.refs_1_, ...), custom_call_target="tpu_custom_call" | custom-call | flops 1509949440 | bytes 6094848 | tf_op jit(solution)/shard_map/weight_back/pallas_call | solution.py:832
  248.1 5.1 %weight_back.3 = (bf16[384,1536]{1,0:T(8,128)(2,1)}, bf16[384,1536]{1,0:T(8,128)(2,1)}) custom-call(bf16[3,768,640]{2,1,0:T(8,128)(2,1)} %pad_maximum_fusion.lhs_ref, bf16[256,2304]{1,0:T(8,128)(2,1)} %get-tuple-element.109.refs_0_, bf16[384,2304]{1,0:T(8,128)(2,1)} %get-tuple-element.118.refs_0_.refs_1_, bf16[256,768]{1,0:T(8,128)(2,1)} %get-tuple-element.127.refs_2_, ...), custom_call_target="tpu_custom_call" | custom-call | flops 1509949440 | bytes 6094848 | tf_op jit(solution)/shard_map/weight_back/pallas_call | solution.py:832
  261.2 7.2 %collective-permute-done.26.refs_1_ = bf16[24,3072]{1,0:T(8,128)(2,1)S(1)} collective-permute-done((bf16[24,3072]{1,0:T(8,128)(2,1)S(1)}, bf16[24,3072]{1,0:T(8,128)(2,1)S(1)}, u32[]{:S(2)}, u32[]{:S(2)}) %collective-permute-start.26) | collective-permute-done | bytes 147488 | tf_op jit(solution)/shard_map/ppermute | solution.py:26
  269.9 4.5 %fold.6 = (bf16[192,1536]{1,0:T(8,128)(2,1)}, bf16[192,1536]{1,0:T(8,128)(2,1)}, bf16[192,1536]{1,0:T(8,128)(2,1)}, bf16[192,1536]{1,0:T(8,128)(2,1)}) custom-call(bf16[384,1536]{1,0:T(8,128)(2,1)} %get-tuple-element.125.keep_a, bf16[384,1536]{1,0:T(8,128)(2,1)} %copy-done.6, bf16[384,1536]{1,0:T(8,128)(2,1)} %get-tuple-element.130.keep_b, ...), custom_call_target="tpu_custom_call" | custom-call | flops 1179648 | bytes 7077888 | tf_op jit(solution)/shard_map/fold/pallas_call | solution.py:187
  276.2 10.4 %input_back.1 = (f32[640,768]{1,0:T(8,128)}, f32[1,768]{1,0:T(1,128)}, f32[1,768]{1,0:T(1,128)}) custom-call(bf16[256,2304]{1,0:T(8,128)(2,1)} %get-tuple-element.109.refs_0_, bf16[384,2304]{1,0:T(8,128)(2,1)} %get-tuple-element.118.refs_0_.refs_1_, bf16[768,2304]{1,0:T(8,128)(2,1)} %refs_2_.1, bf16[640,768]{1,0:T(8,128)(2,1)} %refs_3_.1, ...), custom_call_target="tpu_custom_call" | custom-call | flops 2264924160 | bytes 10420224 | tf_op jit(solution)/shard_map/input_back/pallas_call | solution.py:890
  288.1 4.3 %all-to-all-start.2 = ((f32[32,1,4,768]{3,2,1,0:T(4,128)}), f32[32,1,4,768]{3,2,1,0:T(4,128)S(1)}, u32[]{:S(2)}, u32[]{:S(2)}) async-start(f32[32,1,4,768]{3,2,1,0:T(4,128)} %broadcast_in_dim.61), calls=%async_computation.2 | async-start | bytes 786432 | tf_op jit(solution)/shard_map/all_to_all | solution.py:44
  293.5 3.5 %fold.7 = (bf16[96,1536]{1,0:T(8,128)(2,1)}, bf16[96,1536]{1,0:T(8,128)(2,1)}, bf16[96,1536]{1,0:T(8,128)(2,1)}, bf16[96,1536]{1,0:T(8,128)(2,1)}) custom-call(bf16[192,1536]{1,0:T(8,128)(2,1)} %get-tuple-element.135.refs_6_.keep_a, bf16[192,1536]{1,0:T(8,128)(2,1)} %copy-done.18, bf16[192,1536]{1,0:T(8,128)(2,1)} %get-tuple-element.142.keep_b, ...), custom_call_target="tpu_custom_call" | custom-call | flops 589824 | bytes 3538944 | tf_op jit(solution)/shard_map/fold/pallas_call | solution.py:187
  300.2 7.9 %grad_of_down.1.refs_0_ = f32[96,768]{1,0:T(8,128)} custom-call(bf16[1280,1024]{1,0:T(8,128)(2,1)} %bitcast.68, bf16[256,768]{1,0:T(8,128)(2,1)} %bitcast.71, f32[1,256]{1,0:T(1,128)} %get-tuple-element.148.col_sum_ref, f32[1,256]{1,0:T(1,128)} %get-tuple-element.149.col_count_ref, f32[1,128]{1,0:T(1,128)} %get-tuple-element.150.live_ref, ...), custom_call_target="tpu_custom_call" | custom-call | flops 1006632960 | bytes 2621440 | tf_op jit(solution)/shard_map/grad_of_down/pallas_call | solution.py:653
  320.5 7.2 %collective-permute-done.33 = bf16[24,3072]{1,0:T(8,128)(2,1)S(1)} collective-permute-done((bf16[24,3072]{1,0:T(8,128)(2,1)}, bf16[24,3072]{1,0:T(8,128)(2,1)S(1)}, u32[]{:S(2)}, u32[]{:S(2)}) %collective-permute-start.33) | collective-permute-done | bytes 147488 | tf_op jit(solution)/shard_map/ppermute | solution.py:26
  (245 shorter events, 105.0 us)
Async XLA Ops:
  7.2 110.2 %all-gather.2.cloned.1.call-start = ((), (), s32[]{:S(2)}) async-start(), calls=%async_computation.3 | async-start | bytes 9732096 | tf_op jit(solution)/shard_map/all_gather | solution.py:937
  11.9 28.0 %collective-permute-start.2 = (bf16[24,3072]{1,0:T(8,128)(2,1)S(1)}, bf16[24,3072]{1,0:T(8,128)(2,1)S(1)}, u32[]{:S(2)}, u32[]{:S(2)}) collective-permute-start(bf16[24,3072]{1,0:T(8,128)(2,1)S(1)} %constant_dynamic-update-slice_fusion), channel_id=1, source_target_pairs={{0,24},{1,25},{2,26},{3,27},{4,28},{5,29},{6,30},{7,31},{8,16},{9,... | collective-permute-start | bytes 442376 | tf_op jit(solution)/shard_map/ppermute | solution.py:26
  17.0 22.9 %collective-permute-start.1 = (bf16[24,3072]{1,0:T(8,128)(2,1)S(1)}, bf16[24,3072]{1,0:T(8,128)(2,1)S(1)}, u32[]{:S(2)}, u32[]{:S(2)}) collective-permute-start(bf16[24,3072]{1,0:T(8,128)(2,1)S(1)} %constant_dynamic-update-slice_fusion), channel_id=1, source_target_pairs={{0,16},{1,17},{2,18},{3,19},{4,20},{5,21},{6,22},{7,23},{8,24},{9,... | collective-permute-start | bytes 442376 | tf_op jit(solution)/shard_map/ppermute | solution.py:26
  17.0 22.9 %collective-permute-start = (bf16[24,3072]{1,0:T(8,128)(2,1)S(1)}, bf16[24,3072]{1,0:T(8,128)(2,1)S(1)}, u32[]{:S(2)}, u32[]{:S(2)}) collective-permute-start(bf16[24,3072]{1,0:T(8,128)(2,1)S(1)} %constant_dynamic-update-slice_fusion), channel_id=1, source_target_pairs={{0,8},{1,9},{2,10},{3,11},{4,12},{5,13},{6,14},{7,15},{8,0},{9,1},... | collective-permute-start | bytes 442376 | tf_op jit(solution)/shard_map/ppermute | solution.py:26
  40.0 22.9 %collective-permute-start.3 = (bf16[96,3072]{1,0:T(8,128)(2,1)S(1)}, bf16[96,3072]{1,0:T(8,128)(2,1)S(1)}, u32[]{:S(2)}, u32[]{:S(2)}) collective-permute-start(bf16[96,3072]{1,0:T(8,128)(2,1)S(1)} %pad_maximum_fusion.5.refs_0_), channel_id=1, source_target_pairs={{0,2},{1,3},{2,0},{3,1},{4,6},{5,7},{6,4},{7,5},{8,10},{9,11},{10,... | collective-permute-start | bytes 1769480 | tf_op jit(solution)/shard_map/ppermute | solution.py:26
  41.6 21.2 %collective-permute-start.4 = (bf16[96,3072]{1,0:T(8,128)(2,1)S(1)}, bf16[96,3072]{1,0:T(8,128)(2,1)S(1)}, u32[]{:S(2)}, u32[]{:S(2)}) collective-permute-start(bf16[96,3072]{1,0:T(8,128)(2,1)S(1)} %pad_maximum_fusion.5.refs_0_), channel_id=1, source_target_pairs={{0,4},{1,5},{2,6},{3,7},{4,0},{5,1},{6,2},{7,3},{8,12},{9,13},{10,... | collective-permute-start | bytes 1769480 | tf_op jit(solution)/shard_map/ppermute | solution.py:26
  74.7 17.9 %collective-permute-start.12 = (bf16[1,40,1024]{2,1,0:T(8,128)(2,1)}, bf16[1,40,1024]{2,1,0:T(8,128)(2,1)S(1)}, u32[]{:S(2)}, u32[]{:S(2)}) collective-permute-start(bf16[1,40,1024]{2,1,0:T(8,128)(2,1)} %bitcast.75), channel_id=1, source_target_pairs={{0,16},{1,17},{2,18},{3,19},{4,20},{5,21},{6,22},{7,23},{8,24},{9,... | collective-permute-start | bytes 245768 | tf_op jit(solution)/shard_map/ppermute | solution.py:26
  92.7 14.7 %collective-permute-start.13 = (bf16[2,40,1024]{2,1,0:T(8,128)(2,1)S(1)}, bf16[2,40,1024]{2,1,0:T(8,128)(2,1)S(1)}, u32[]{:S(2)}, u32[]{:S(2)}) collective-permute-start(bf16[2,40,1024]{2,1,0:T(8,128)(2,1)S(1)} %maximum_bitcast_fusion), channel_id=1, source_target_pairs={{0,8},{1,9},{2,10},{3,11},{4,12},{5,13},{6,14},{7,15},{8,0},{9,1},... | collective-permute-start | bytes 491528 | tf_op jit(solution)/shard_map/ppermute | solution.py:26
  117.6 20.5 %collective-permute-start.15 = (bf16[8,40,1024]{2,1,0:T(8,128)(2,1)S(1)}, bf16[8,40,1024]{2,1,0:T(8,128)(2,1)S(1)}, u32[]{:S(2)}, u32[]{:S(2)}) collective-permute-start(bf16[8,40,1024]{2,1,0:T(8,128)(2,1)S(1)} %bitcast.72), channel_id=1, source_target_pairs={{0,2},{1,3},{2,0},{3,1},{4,6},{5,7},{6,4},{7,5},{8,10},{9,11},{10,... | collective-permute-start | bytes 1966088 | tf_op jit(solution)/shard_map/ppermute | solution.py:26
  120.3 17.9 %all-to-all-start = ((bf16[40,32,96]{2,0,1:T(8,128)(2,1)}), bf16[40,32,96]{2,0,1:T(8,128)(2,1)S(1)}, u32[]{:S(2)}, u32[]{:S(2)}) async-start(bf16[40,32,96]{2,0,1:T(8,128)(2,1)} %copy.54), calls=%async_computation | async-start | bytes 655360 | tf_op jit(solution)/shard_map/all_to_all | solution.py:981
  139.0 15.8 %collective-permute-start.16 = (bf16[16,40,1024]{2,1,0:T(8,128)(2,1)S(1)}, bf16[16,40,1024]{2,1,0:T(8,128)(2,1)S(1)}, u32[]{:S(2)}, u32[]{:S(2)}) collective-permute-start(bf16[16,40,1024]{2,1,0:T(8,128)(2,1)S(1)} %bitcast.69), channel_id=1, source_target_pairs={{0,1},{1,0},{2,3},{3,2},{4,5},{5,4},{6,7},{7,6},{8,9},{9,8},{10,11... | collective-permute-start | bytes 3932168 | tf_op jit(solution)/shard_map/ppermute | solution.py:26
  143.1 18.6 %all-to-all-start.1 = ((bf16[32,8,768]{2,1,0:T(8,128)(2,1)}), bf16[32,8,768]{2,1,0:T(8,128)(2,1)S(1)}, u32[]{:S(2)}, u32[]{:S(2)}) async-start(bf16[32,8,768]{2,1,0:T(8,128)(2,1)} %broadcast_in_dim.60), calls=%async_computation.1 | async-start | bytes 786432 | tf_op jit(solution)/shard_map/all_to_all | solution.py:44
  214.2 17.1 %collective-permute-start.19 = (bf16[192,1536]{1,0:T(8,128)(2,1)}, bf16[192,1536]{1,0:T(8,128)(2,1)S(1)}, u32[]{:S(2)}, u32[]{:S(2)}) collective-permute-start(bf16[192,1536]{1,0:T(8,128)(2,1)} %get-tuple-element.115.refs_1_), channel_id=1, source_target_pairs={{0,2},{1,3},{2,0},{3,1},{4,6},{5,7},{6,4},{7,5},{8,10},{9,11},{10,... | collective-permute-start | bytes 1769480 | tf_op jit(solution)/shard_map/ppermute | solution.py:26
  214.8 16.5 %collective-permute-start.20 = (bf16[192,1536]{1,0:T(8,128)(2,1)}, bf16[192,1536]{1,0:T(8,128)(2,1)S(1)}, u32[]{:S(2)}, u32[]{:S(2)}) collective-permute-start(bf16[192,1536]{1,0:T(8,128)(2,1)} %get-tuple-element.117.refs_3_), channel_id=1, source_target_pairs={{0,4},{1,5},{2,6},{3,7},{4,0},{5,1},{6,2},{7,3},{8,12},{9,13},{10,... | collective-permute-start | bytes 1769480 | tf_op jit(solution)/shard_map/ppermute | solution.py:26
  244.5 23.9 %collective-permute-start.21 = (bf16[384,1536]{1,0:T(8,128)(2,1)}, bf16[384,1536]{1,0:T(8,128)(2,1)S(1)}, u32[]{:S(2)}, u32[]{:S(2)}) collective-permute-start(bf16[384,1536]{1,0:T(8,128)(2,1)} %get-tuple-element.126.refs_0_), channel_id=1, source_target_pairs={{0,1},{1,0},{2,3},{3,2},{4,5},{5,4},{6,7},{7,6},{8,9},{9,8},{10,11... | collective-permute-start | bytes 3538952 | tf_op jit(solution)/shard_map/ppermute | solution.py:26
  253.2 15.3 %collective-permute-start.24 = (bf16[384,1536]{1,0:T(8,128)(2,1)}, bf16[384,1536]{1,0:T(8,128)(2,1)S(1)}, u32[]{:S(2)}, u32[]{:S(2)}) collective-permute-start(bf16[384,1536]{1,0:T(8,128)(2,1)} %get-tuple-element.131), channel_id=1, source_target_pairs={{0,1},{1,0},{2,3},{3,2},{4,5},{5,4},{6,7},{7,6},{8,9},{9,8},{10,11... | collective-permute-start | bytes 3538952 | tf_op jit(solution)/shard_map/ppermute | solution.py:26
  254.7 13.7 %collective-permute-start.26 = (bf16[24,3072]{1,0:T(8,128)(2,1)S(1)}, bf16[24,3072]{1,0:T(8,128)(2,1)S(1)}, u32[]{:S(2)}, u32[]{:S(2)}) collective-permute-start(bf16[24,3072]{1,0:T(8,128)(2,1)S(1)} %copy-done.47), channel_id=1, source_target_pairs={{0,16},{1,17},{2,18},{3,19},{4,20},{5,21},{6,22},{7,23},{8,24},{9,... | collective-permute-start | bytes 442376 | tf_op jit(solution)/shard_map/ppermute | solution.py:26
  255.4 13.1 %collective-permute-start.27 = (bf16[24,3072]{1,0:T(8,128)(2,1)S(1)}, bf16[24,3072]{1,0:T(8,128)(2,1)S(1)}, u32[]{:S(2)}, u32[]{:S(2)}) collective-permute-start(bf16[24,3072]{1,0:T(8,128)(2,1)S(1)} %copy-done.46), channel_id=1, source_target_pairs={{0,24},{1,25},{2,26},{3,27},{4,28},{5,29},{6,30},{7,31},{8,16},{9,... | collective-permute-start | bytes 442376 | tf_op jit(solution)/shard_map/ppermute | solution.py:26
  274.5 18.0 %collective-permute-start.28 = (bf16[192,1536]{1,0:T(8,128)(2,1)}, bf16[192,1536]{1,0:T(8,128)(2,1)S(1)}, u32[]{:S(2)}, u32[]{:S(2)}) collective-permute-start(bf16[192,1536]{1,0:T(8,128)(2,1)} %get-tuple-element.141), channel_id=1, source_target_pairs={{0,2},{1,3},{2,0},{3,1},{4,6},{5,7},{6,4},{7,5},{8,10},{9,11},{10,... | collective-permute-start | bytes 1769480 | tf_op jit(solution)/shard_map/ppermute | solution.py:26
  275.2 17.3 %collective-permute-start.29 = (bf16[192,1536]{1,0:T(8,128)(2,1)}, bf16[192,1536]{1,0:T(8,128)(2,1)S(1)}, u32[]{:S(2)}, u32[]{:S(2)}) collective-permute-start(bf16[192,1536]{1,0:T(8,128)(2,1)} %get-tuple-element.143), channel_id=1, source_target_pairs={{0,4},{1,5},{2,6},{3,7},{4,0},{5,1},{6,2},{7,3},{8,12},{9,13},{10,... | collective-permute-start | bytes 1769480 | tf_op jit(solution)/shard_map/ppermute | solution.py:26
  288.1 29.6 %all-to-all-start.2 = ((f32[32,1,4,768]{3,2,1,0:T(4,128)}), f32[32,1,4,768]{3,2,1,0:T(4,128)S(1)}, u32[]{:S(2)}, u32[]{:S(2)}) async-start(f32[32,1,4,768]{3,2,1,0:T(4,128)} %broadcast_in_dim.61), calls=%async_computation.2 | async-start | bytes 786432 | tf_op jit(solution)/shard_map/all_to_all | solution.py:44
  296.9 11.2 %collective-permute-start.30 = (bf16[96,1536]{1,0:T(8,128)(2,1)}, bf16[96,1536]{1,0:T(8,128)(2,1)S(1)}, u32[]{:S(2)}, u32[]{:S(2)}) collective-permute-start(bf16[96,1536]{1,0:T(8,128)(2,1)} %get-tuple-element.145.refs_1_), channel_id=1, source_target_pairs={{0,4},{1,5},{2,6},{3,7},{4,0},{5,1},{6,2},{7,3},{8,12},{9,13},{10,... | collective-permute-start | bytes 884744 | tf_op jit(solution)/shard_map/ppermute | solution.py:26
  315.1 12.7 %collective-permute-start.33 = (bf16[24,3072]{1,0:T(8,128)(2,1)}, bf16[24,3072]{1,0:T(8,128)(2,1)S(1)}, u32[]{:S(2)}, u32[]{:S(2)}) collective-permute-start(bf16[24,3072]{1,0:T(8,128)(2,1)} %get-tuple-element.154), channel_id=1, source_target_pairs={{0,16},{1,17},{2,18},{3,19},{4,20},{5,21},{6,22},{7,23},{8,24},{9,... | collective-permute-start | bytes 442376 | tf_op jit(solution)/shard_map/ppermute | solution.py:26
  315.1 12.7 %collective-permute-start.32 = (bf16[24,3072]{1,0:T(8,128)(2,1)}, bf16[24,3072]{1,0:T(8,128)(2,1)S(1)}, u32[]{:S(2)}, u32[]{:S(2)}) collective-permute-start(bf16[24,3072]{1,0:T(8,128)(2,1)} %get-tuple-element.153), channel_id=1, source_target_pairs={{0,8},{1,9},{2,10},{3,11},{4,12},{5,13},{6,14},{7,15},{8,0},{9,1},... | collective-permute-start | bytes 442376 | tf_op jit(solution)/shard_map/ppermute | solution.py:26
  (68 other events, 538.3 us)
Sparse Core Ops, SparseCore 0:
  11.0 99.3 all-gather.1
where the time goes:
time: 341 us; the launch traced here: 336 us
  Pallas kernels  167 us (49%)
  waiting for transfers between devices  52.3 us (15%)
  starting transfers between devices  51.9 us (15%)
  local copies, waits for them, and re-layouts  28.9 us (8%)
  between operations  14.9 us (4%)
  other arithmetic  11.8 us (3%)
  matrix products  9.16 us (3%)
    ppermute x35, waiting for transfers between devices, swapped(): return lax.ppermute(value, AXIS, [(i, i ^ mask) for i in range(peers)])  47.2 us
    ppermute x35, starting transfers between devices, swapped(): return lax.ppermute(value, AXIS, [(i, i ^ mask) for i in range(peers)])  38.9 us
    pallas_call x4, Pallas kernels, fold(): pl.pallas_call(fold_kernel, grid=(cols // tile,), out_shape=[jax.ShapeDty...  25.2 us
    pallas_call x2, Pallas kernels, attention_back(): pl.pallas_call(attention_back_kernel, grid=(count,), out_shape=[jax.Shape...  21.8 us
    pallas_call x1, Pallas kernels, mlp_back(): pl.pallas_call(mlp_back_kernel, grid=(steps,), out_shape=[part] * 4 + [ja...  21.5 us
    pallas_call x1, Pallas kernels, text_front(): pl.pallas_call(text_front_kernel, out_shape=[jax.ShapeDtypeStruct(*item)...  19 us
    pallas_call x1, Pallas kernels, image_up(): pl.pallas_call(functools.partial(image_up_kernel, fold), grid=(FF // TILE...  14.1 us
    pallas_call x1, Pallas kernels, image_front(): pl.pallas_call(functools.partial(image_front_kernel, windows), out_shape=...  13.8 us
  transfers between devices with their start and end apart: 39, of which 13 were waited for; matrix products, arithmetic and copies ran while one was open for 10% of the time, Pallas kernels for 36%

commit v1 on v0

--- a/solution.py
+++ b/solution.py
@@ -160,10 +160,17 @@
     return row == col
 
 
-def masked_softmax(scores, mask):
-    scores = jnp.where(mask, scores, -1e30)
-    raised = jnp.exp(scores - jnp.max(scores, axis=-1, keepdims=True))
-    return raised * (1.0 / jnp.sum(raised, axis=-1, keepdims=True))
+def softmax_down(scores, mask):
+    keys = mask.shape[0]
+    parts, sums = [], []
+    for k in range(2):
+        part = jnp.where(mask, scores[k * keys : (k + 1) * keys], -1e30)
+        most = jnp.max(part, axis=0, keepdims=True)
+        raised = jnp.exp(part - most)
+        total = jnp.sum(raised, axis=0, keepdims=True)
+        parts.append(raised * (1.0 / total))
+        sums.append(most + jnp.log(total))
+    return parts, sums
 
 
 def fold_kernel(keep_a, got_a, keep_b, got_b, *refs):
@@ -243,24 +250,34 @@
         dst[at, :] = (unit * gain + bias).astype(bf16)
 
 
-def attend(qkv_ref, att_ref, q_rows, k_rows, mask):
+def attend_along(qkv_ref, att_ref, q_rows, k_rows, mask):
     low, high = lane_halves(f32)
     for pair in range(HEADS // 2):
         queries = two_heads(qkv_ref[q_rows, pair_cols(0, pair)] * bf16(HEAD ** (-0.5)))
         scores = mul_bt(queries, qkv_ref[k_rows, pair_cols(1, pair)])
-        probs = masked_softmax(scores, mask).astype(bf16)
+        scores = jnp.where(mask, scores, -1e30)
+        raised = jnp.exp(scores - jnp.max(scores, axis=-1, keepdims=True))
+        probs = (raised * (1.0 / jnp.sum(raised, axis=-1, keepdims=True))).astype(bf16)
         half = probs.shape[0] // 2
         mixed = mul(probs, qkv_ref[k_rows, pair_cols(2, pair)])
         att_ref[q_rows, pair_cols(0, pair)] = (mixed[:half] * low + mixed[half:] * high).astype(bf16)
 
 
-def twice(mask):
-    return jnp.concatenate([mask, mask], axis=0)
+def attend(qkv_ref, att_ref, q_rows, k_rows, mask, keep_sums):
+    for pair in range(HEADS // 2):
+        queries = qkv_ref[q_rows, pair_cols(0, pair)] * bf16(HEAD ** (-0.5))
+        scores = mul_bt(two_heads(qkv_ref[k_rows, pair_cols(1, pair)]), queries)
+        probs, sums = softmax_down(scores, mask)
+        vals = two_heads(qkv_ref[k_rows, pair_cols(2, pair)])
+        mixed = mul_at(jnp.concatenate(probs, axis=0).astype(bf16), vals)
+        att_ref[q_rows, pair_cols(0, pair)] = mixed.astype(bf16)
+        for k in range(2):
+            keep_sums(2 * pair + k, sums[k])
 
 
 def text_front_kernel(
     x_ref, g1_ref, b1_ref, wqkv_ref, wo_ref, g2_ref, b2_ref, h1_ref, qkv_ref, att_ref, mid_ref,
-    h2_ref, sum_ref
+    h2_ref, sum_ref, lse_ref
 ):
     rows, chunk = x_ref.shape[0], 128
     norm_rows(x_ref, h1_ref, g1_ref[...], b1_ref[...], chunk)
@@ -270,12 +287,16 @@
         at = pl.ds(pl.multiple_of(step * 256, 256), 256)
         qkv_ref[:, at] = mul(h1_ref[...], wqkv_ref[:, at]).astype(bf16)
 
-    mask = twice(same_sequence(chunk, 0, chunk, 0, TXT_LEN))
+    mask = same_sequence(chunk, 0, chunk, 0, TXT_LEN)
 
     @pl.loop(0, rows // chunk)
     def _(step):
         at = pl.ds(pl.multiple_of(step * chunk, chunk), chunk)
-        attend(qkv_ref, att_ref, at, at, mask)
+
+        def keep_sums(head, value):
+            lse_ref[pl.ds(step * 16 + head, 1), :] = value
+
+        attend(qkv_ref, att_ref, at, at, mask, keep_sums)
 
     @pl.loop(0, D // 256)
     def _(step):
@@ -302,6 +323,7 @@
         ((rows, D), f32),
         ((rows, D), bf16),
         ((rows // TXT_LEN, D), f32),
+        ((rows // 128 * 16, 128), f32),
     ]
     return pl.pallas_call(
         text_front_kernel,
@@ -342,8 +364,9 @@
         qkv_ref[:, at] = mul(placed_ref[...], w_ref[:, at]).astype(bf16)
 
     for row0, count, key0, keys in windows:
-        mask = twice(same_sequence(count, row0, keys, key0, IMG_LEN))
-        attend(qkv_ref, att_ref, pl.ds(row0, count), pl.ds(key0, keys), mask)
+        one = same_sequence(count, row0, keys, key0, IMG_LEN)
+        mask = jnp.concatenate([one, one], axis=0)
+        attend_along(qkv_ref, att_ref, pl.ds(row0, count), pl.ds(key0, keys), mask)
     place_columns(att_ref)
 
     @pl.loop(0, D // 256)
@@ -749,33 +772,37 @@
     )(grad_low, weight_down, slope, weight_up, lhs, middle, gain[None], grad_row)
 
 
-def attention_back_kernel(grad_ref, wo_ref, qkv_ref, *refs):
+def attention_back_kernel(grad_ref, wo_ref, qkv_ref, lse_ref, *refs):
     low_ref, out_ref = refs[-2:]
     chunk = grad_ref.shape[0]
-    one = same_sequence(chunk, 0, chunk, 0, TXT_LEN)
-    mask = jnp.concatenate([one, one], axis=0)
+    mask = same_sequence(chunk, 0, chunk, 0, TXT_LEN)
     low = grad_ref[...].astype(bf16)
     low_ref[...] = low
     grad_att = mul_bt(low, wo_ref[...]).astype(bf16)
     for pair in range(HEADS // 2):
-        queries = two_heads(qkv_ref[:, pair_cols(0, pair)] * bf16(HEAD ** (-0.5)))
-        keys = qkv_ref[:, pair_cols(1, pair)]
-        vals = qkv_ref[:, pair_cols(2, pair)]
-        grads = two_heads(grad_att[:, pair_cols(0, pair)])
-        probs = masked_softmax(mul_bt(queries, keys), mask)
-        grad_probs = mul_bt(grads, vals)
-        along = jnp.sum(grad_probs * probs, axis=-1, keepdims=True)
-        grad_scores = (probs * (grad_probs - along)).astype(bf16)
-        side = jnp.concatenate([grad_scores[:chunk], grad_scores[chunk:]], axis=1)
-        grad_q = mul(side, two_heads(keys)) * HEAD ** (-0.5)
-        grad_k = mul_at(grad_scores, queries)
-        grad_v = mul_at(probs.astype(bf16), grads)
+        queries = qkv_ref[:, pair_cols(0, pair)] * bf16(HEAD ** (-0.5))
+        keys = two_heads(qkv_ref[:, pair_cols(1, pair)])
+        vals = two_heads(qkv_ref[:, pair_cols(2, pair)])
+        grads = grad_att[:, pair_cols(0, pair)]
+        scores, grad_probs = mul_bt(keys, queries), mul_bt(vals, grads)
+        probs, grad_scores = [], []
+        for k in range(2):
+            at = slice(k * chunk, (k + 1) * chunk)
+            head = 2 * pair + k
+            shifted = scores[at] - lse_ref[head : head + 1, :]
+            prob = jnp.where(mask, jnp.exp(jnp.where(mask, shifted, 0.0)), 0.0)
+            along = jnp.sum(grad_probs[at] * prob, axis=0, keepdims=True)
+            grad_scores.append((prob * (grad_probs[at] - along)).astype(bf16))
+            probs.append(prob.astype(bf16))
+        grad_q = mul_at(jnp.concatenate(grad_scores, axis=0), keys) * HEAD ** (-0.5)
+        grad_k = mul(jnp.concatenate(grad_scores, axis=1), two_heads(queries))
+        grad_v = mul(jnp.concatenate(probs, axis=1), two_heads(grads))
         out_ref[:, pair_cols(0, pair)] = grad_q.astype(bf16)
         out_ref[:, pair_cols(1, pair)] = grad_k.astype(bf16)
         out_ref[:, pair_cols(2, pair)] = grad_v.astype(bf16)
 
 
-def attention_back(grad_middle, weight_out, project, first, count, after=()):
+def attention_back(grad_middle, weight_out, project, log_sums, first, count, after=()):
     chunk = 128
     rows = count * chunk
     return pl.pallas_call(
@@ -789,6 +816,7 @@
             pl.BlockSpec((chunk, D), lambda i: (i + first, 0)),
             pl.BlockSpec((D, D), lambda i: (0, 0)),
             pl.BlockSpec((chunk, 3 * D), lambda i: (i + first, 0)),
+            pl.BlockSpec((16, chunk), lambda i: (i + first, 0)),
         ]
         + anywhere(after),
         out_specs=[
@@ -798,7 +826,7 @@
         compiler_params=params(),
         cost_estimate=cost(10 * rows * D * D, 16 * rows * D + 2 * D * D, rows * 128 * HEADS),
         name="attention_back",
-    )(grad_middle, weight_out, project, *after)
+    )(grad_middle, weight_out, project, log_sums, *after)
 
 
 def mul_rows(lhs, parts):
@@ -947,7 +975,7 @@
     else:
         line, perm = lax.all_gather(shard, AXIS, axis=0, tiled=True), jnp.eye(D, dtype=bf16)
 
-    normed1, project, attended, middle, normed2, middle_sum = text_front(
+    normed1, project, attended, middle, normed2, middle_sum, log_sums = text_front(
         captions, txt_gain1, txt_bias1, txt_qkv, txt_out, txt_gain2, txt_bias2
     )
     middle_sum, line = in_turn(middle_sum, line)
@@ -979,14 +1007,14 @@
         )
         held = joined(held, other, 16)
         hidden_cols = lax.all_to_all(scaled_sum, AXIS, split_axis=1, concat_axis=0, tiled=True)
-        held = joined(held, swapped(held, 8), 8)
-        whole, other = in_turn(whole, swapped(held, 4))
-        held = joined(held, other, 4)
-        other = swapped(held, 2)
+        whole, other = in_turn(whole, swapped(held, 8))
+        held = joined(held, other, 8)
+        other = swapped(held, 4)
     image_low = image_up(normed_img, whole, 0, FF, middle_img)
     if small:
         image_low, other, hidden_cols = lax.optimization_barrier((image_low, other, hidden_cols))
-        held = joined(held, other, 2)
+        held = joined(held, other, 4)
+        held = joined(held, swapped(held, 2), 2)
         text_pack = joined(held, swapped(held, 1), 1).reshape(-1, D + total_images)
     image_all = spread(image_low).reshape(total_images, D)
 
@@ -1014,10 +1042,10 @@
         grad_row, row_low, txt_down, slope, txt_up, lhs_up, middle, txt_gain2
     )
     stages = len(order_a)
-    low_one, proj_one = attention_back(grad_middle, txt_out, project, 0, 2)
+    low_one, proj_one = attention_back(grad_middle, txt_out, project, log_sums, 0, 2)
     for stage in range(stages - 2):
         up = fold(hand_on(up, stage), (proj_one,))
-    low_two, proj_two = attention_back(grad_middle, txt_out, project, 2, 3, up)
+    low_two, proj_two = attention_back(grad_middle, txt_out, project, log_sums, 2, 3, up)
     up = fold(hand_on(up, stages - 2), (proj_two,))
     projs, lows = (proj_one, proj_two), (low_one, low_two)
     rest_a = weight_back(lhs_rest, 0, [projs], [0], up)
@@ -1025,11 +1053,14 @@
     rest_b = weight_back(lhs_rest, 1, [projs, lows], [2, 0], up[:1])
     rest = [*rest_a, *rest_b]
     for stage in range(stages - 2):
-        rest = fold(hand_on(rest, stage), up[1])
+        rest = fold(hand_on(rest, stage))
     caption_grad, gain_one, bias_one = input_back(
         projs, txt_qkv, captions, txt_gain1, grad_middle, rest[:1]
     )
+    caption_grad, up = in_turn(caption_grad, up)
     rest = fold(hand_on(rest, stages - 2), (caption_grad,))
+    norms = jnp.concatenate([gain_one, bias_one, gain_two, bias_two], axis=0)
+    norms, rest = in_turn(norms, rest)
     if small:
         grad_down = grad_of_down(
             text_pack, image_all, col_sum, col_count, live_total, hidden_cols, rest
@@ -1042,7 +1073,6 @@
         rest = fold_last(hand_on(rest, stages - 1))
     up_share = sum_last(*up)
     rest_share = sum_last(*hand_on_last(rest))
-    norms = jnp.concatenate([gain_one, bias_one, gain_two, bias_two], axis=0)
     norms = jnp.sum(spread(norms[None]), axis=0).reshape(4, D)
     return (
         loss_value,

time: 341 us -> 323 us (0.947)
  Pallas kernels: 167 us -> 153 us
  starting transfers between devices: 51.9 us -> 46.4 us
  waiting for transfers between devices: 52.3 us -> 57.6 us
    pallas_call x4, Pallas kernels: 25.2 us -> 16.1 us  [fold(): pl.pallas_call(fold_kernel, grid=(cols // tile,), out_shape=[jax.ShapeDty...]
    pallas_call x2, Pallas kernels: 21.8 us -> 17 us  [attention_back(): pl.pallas_call(attention_back_kernel, grid=(count,), out_shape=[jax.Shape...]
    all_gather x1, waiting for transfers between devices: 0.01 us -> 4.52 us  [local(): lax.all_gather(jnp.concatenate([img_up.reshape(per, FF), img_down.reshape...]
    unnamed x108 -> x96, local copies, waits for them, and re-layouts: 11.5 us -> 12 us
  transfers between devices with their start and end apart: 39 -> 39, of which waited for: 13 -> 12; matrix products, arithmetic and copies ran while one was open for 10% -> 11% of each run, Pallas kernels for 36% -> 34%
where the time goes in v1:
time: 323 us; the launch traced here: 322 us
  Pallas kernels  153 us (47%)
  waiting for transfers between devices  57.6 us (18%)
  starting transfers between devices  46.4 us (14%)
  local copies, waits for them, and re-layouts  29.5 us (9%)
  between operations  14.7 us (5%)
  other arithmetic  11.8 us (4%)
  matrix products  9.13 us (3%)
    ppermute x35, waiting for transfers between devices, swapped(): return lax.ppermute(value, AXIS, [(i, i ^ mask) for i in range(peers)])  48.6 us
    ppermute x35, starting transfers between devices, swapped(): return lax.ppermute(value, AXIS, [(i, i ^ mask) for i in range(peers)])  37.2 us
    pallas_call x1, Pallas kernels, mlp_back(): pl.pallas_call(mlp_back_kernel, grid=(steps,), out_shape=[part] * 4 + [ja...  21.5 us
    pallas_call x1, Pallas kernels, text_front(): pl.pallas_call(text_front_kernel, out_shape=[jax.ShapeDtypeStruct(*item)...  18.3 us
    pallas_call x2, Pallas kernels, attention_back(): pl.pallas_call(attention_back_kernel, grid=(count,), out_shape=[jax.Shape...  17 us
    pallas_call x4, Pallas kernels, fold(): pl.pallas_call(fold_kernel, grid=(cols // tile,), out_shape=[jax.ShapeDty...  16.1 us
    pallas_call x1, Pallas kernels, image_up(): pl.pallas_call(functools.partial(image_up_kernel, fold), grid=(FF // TILE...  14 us
    pallas_call x1, Pallas kernels, image_front(): pl.pallas_call(functools.partial(image_front_kernel, windows), out_shape=...  13.8 us
  transfers between devices with their start and end apart: 39, of which 12 were waited for; matrix products, arithmetic and copies ran while one was open for 11% of the time, Pallas kernels for 34%

profile of v1, /device:TPU:0, one launch (start us, length us, event | category | flops | bytes accessed | tf_op | source)
XLA Modules:
  0.0 321.6 jit_solution(5492446342392561287)
XLA Ops:
  11.9 5.1 %collective-permute-start.2 = (bf16[24,3072]{1,0:T(8,128)(2,1)S(1)}, bf16[24,3072]{1,0:T(8,128)(2,1)S(1)}, u32[]{:S(2)}, u32[]{:S(2)}) collective-permute-start(bf16[24,3072]{1,0:T(8,128)(2,1)S(1)} %constant_dynamic-update-slice_fusion), channel_id=1, source_target_pairs={{0,24},{1,25},{2,26},{3,27},{4,28},{5,29},{6,30},{7,31},{8,16},{9,... | collective-permute-start | bytes 442376 | tf_op jit(solution)/shard_map/ppermute | solution.py:26
  20.3 18.3 %text_front.1 = (bf16[640,768]{1,0:T(8,128)(2,1)}, bf16[640,2304]{1,0:T(8,128)(2,1)}, bf16[640,768]{1,0:T(8,128)(2,1)}, f32[640,768]{1,0:T(8,128)}, bf16[640,768...) custom-call(bf16[640,768]{1,0:T(8,128)(2,1)} %refs_3_.1, f32[1,768]{1,0:T(1,128)} %broadcast_in_dim.26.g1_ref.refs_4_, ...), custom_call_target="tpu_custom_call" | custom-call | flops 3019898880 | bytes 11599872 | tf_op jit(solution)/shard_map/text_front/pallas_call | solution.py:328
  46.8 13.8 %text_up.1 = (bf16[640,3072]{1,0:T(8,128)(2,1)}, f32[40,3072]{1,0:T(8,128)}, f32[40,768]{1,0:T(8,128)}, f32[40,128]{1,0:T(8,128)}) custom-call(bf16[640,768]{1,0:T(8,128)(2,1)} %get-tuple-element.96.h2_ref, bf16[768,3072]{1,0:T(8,128)(2,1)} %wu_ref.3, bf16[3072,768]{1,0:T(8,128)(2,1)} %wd_ref.3, f32[40,768]{1,0:T(8,128)} %get-tuple-element.97.sum_ref, ...), custom_call_target="tpu_custom_call" | custom-call | flops 3019898880 | bytes 13369344 | tf_op jit(solution)/shard_map/text_up/pallas_call | solution.py:487
  77.6 13.8 %image_front.1 = (bf16[400,768]{1,0:T(8,128)(2,1)}, f32[8,768]{1,0:T(8,128)}) custom-call(bf16[400,768]{1,0:T(8,128)(2,1)} %x_ref.3, bf16[768,768]{1,0:T(8,128)(2,1)} %fusion.5.perm_ref, bf16[1,768]{1,0:T(2,128)(2,1)} %broadcast_in_dim.22.g1_ref, bf16[1,768]{1,0:T(2,128)(2,1)} %broadcast_in_dim.23.b1_ref, bf16[1,768]{1,0:T(2,128)(2,1)} %broadcast_in_dim.24.g2_ref, ...), custom_call_target="tpu_custom_call" | custom-call | flops 2831155200 | bytes 4718592 | tf_op jit(solution)/shard_map/image_front/pallas_call | solution.py:392
  97.4 12.6 %collective-permute-done.13 = bf16[2,40,1024]{2,1,0:T(8,128)(2,1)S(1)} collective-permute-done((bf16[2,40,1024]{2,1,0:T(8,128)(2,1)S(1)}, bf16[2,40,1024]{2,1,0:T(8,128)(2,1)S(1)}, u32[]{:S(2)}, u32[]{:S(2)}) %collective-permute-start.13) | collective-permute-done | bytes 163872 | tf_op jit(solution)/shard_map/ppermute | solution.py:26
  110.0 4.5 %all-gather.2.cloned.1.call-done.wu_ref.wd_ref = bf16[768,6144]{1,0:T(8,128)(2,1)} async-done(((bf16[24,6144]{1,0:T(8,128)(2,1)}), bf16[768,6144]{1,0:T(8,128)(2,1)}) %all-gather.2.cloned.1.call-update) | async-done | bytes 9437200 | tf_op jit(solution)/shard_map/all_gather | solution.py:965
  116.0 14.0 %image_up.1 = bf16[8,768]{1,0:T(8,128)(2,1)} custom-call(bf16[400,768]{1,0:T(8,128)(2,1)} %get-tuple-element.105.h2_ref, bf16[768,6144]{1,0:T(8,128)(2,1)} %all-gather.2.cloned.1.call-done.wu_ref.wd_ref, bf16[768,6144]{1,0:T(8,128)(2,1)} %all-gather.2.cloned.1.call-done.wu_ref.wd_ref, f32[8,768]{1,0:T(8,128)} %get-tuple-element.108.sum_ref), custom_call_target="tpu_custom_call" | custom-call | flops 1887436800 | bytes 9437184 | tf_op jit(solution)/shard_map/image_up/pallas_call | solution.py:554
  131.6 15.8 %collective-permute-done.15 = bf16[8,40,1024]{2,1,0:T(8,128)(2,1)S(1)} collective-permute-done((bf16[8,40,1024]{2,1,0:T(8,128)(2,1)S(1)}, bf16[8,40,1024]{2,1,0:T(8,128)(2,1)S(1)}, u32[]{:S(2)}, u32[]{:S(2)}) %collective-permute-start.15) | collective-permute-done | bytes 655392 | tf_op jit(solution)/shard_map/ppermute | solution.py:26
  154.9 3.4 %fusion.12 = bf16[1,768,640]{2,1,0:T(8,128)(2,1)} fusion(bf16[640,768]{1,0:T(8,128)(2,1)} %get-tuple-element.96.h2_ref, s32[768]{0:T(1024)S(1)} %fusion.30), kind=kOutput, calls=%fused_computation.17 | convolution fusion | flops 756056064 | bytes 1969152 | tf_op jit(solution)/shard_map/dot_general | solution.py:131
  163.5 4.5 %all-to-all-done.1 = bf16[32,8,768]{2,1,0:T(8,128)(2,1)S(1)} async-done(((bf16[32,8,768]{2,1,0:T(8,128)(2,1)}), bf16[32,8,768]{2,1,0:T(8,128)(2,1)S(1)}, u32[]{:S(2)}, u32[]{:S(2)}) %all-to-all-start.1) | async-done | bytes 393248 | tf_op jit(solution)/shard_map/all_to_all | solution.py:44
  168.8 4.0 %loss_and_rows.1 = (f32[1,128]{1,0:T(1,128)}, f32[40,768]{1,0:T(8,128)}, bf16[40,768]{1,0:T(8,128)(2,1)}, f32[1,256]{1,0:T(1,128)}, f32[1,256]{1,0:T(1,128)}, /*index=5*/f32[1,128]{1,0:T(1,128)}) custom-call(bf16[1280,1024]{1,0:T(8,128)(2,1)} %bitcast.67, bf16[256,768]{1,0:T(8,128)(2,1)} %bitcast.70, bf16[40,1024]{1,0:T(8,128)(2,1)} %packed.1.own_ref, ...), custom_call_target="tpu_custom_call" | custom-call | flops 503316480 | bytes 2621440 | tf_op jit(solution)/shard_map/loss_and_rows/pallas_call | solution.py:644
  172.9 21.5 %mlp_back.1 = (bf16[384,1536]{1,0:T(8,128)(2,1)}, bf16[384,1536]{1,0:T(8,128)(2,1)}, bf16[384,1536]{1,0:T(8,128)(2,1)}, bf16[384,1536]{1,0:T(8,128)(2,1)}, f32[6...) custom-call(bf16[40,768]{1,0:T(8,128)(2,1)} %get-tuple-element.114.low_ref, bf16[3072,768]{1,0:T(8,128)(2,1)} %wd_ref.3, ...), custom_call_target="tpu_custom_call" | custom-call | flops 6039797760 | bytes 18087936 | tf_op jit(solution)/shard_map/mlp_back/pallas_call | solution.py:753
  196.2 7.2 %attention_back.2 = (bf16[256,768]{1,0:T(8,128)(2,1)}, bf16[256,2304]{1,0:T(8,128)(2,1)}) custom-call(f32[640,768]{1,0:T(8,128)} %get-tuple-element.118.grad_ref.refs_5_, bf16[768,768]{1,0:T(8,128)(2,1)} %wo_ref.5, bf16[640,2304]{1,0:T(8,128)(2,1)} %get-tuple-element.119.qkv_ref, f32[80,128]{1,0:T(8,128)} %get-tuple-element.120.lse_ref), custom_call_target="tpu_custom_call" | custom-call | flops 1509949440 | bytes 4325376 | tf_op jit(solution)/shard_map/attention_back/pallas_call | solution.py:808
  204.9 4.5 %fold.4 = (bf16[192,1536]{1,0:T(8,128)(2,1)}, bf16[192,1536]{1,0:T(8,128)(2,1)}, bf16[192,1536]{1,0:T(8,128)(2,1)}, bf16[192,1536]{1,0:T(8,128)(2,1)}) custom-call(bf16[384,1536]{1,0:T(8,128)(2,1)} %get-tuple-element.122.keep_a, bf16[384,1536]{1,0:T(8,128)(2,1)} %copy-done.7, bf16[384,1536]{1,0:T(8,128)(2,1)} %get-tuple-element.124.keep_b, ...), custom_call_target="tpu_custom_call" | custom-call | flops 1179648 | bytes 7077888 | tf_op jit(solution)/shard_map/fold/pallas_call | solution.py:194
  213.8 9.8 %attention_back.3 = (bf16[384,768]{1,0:T(8,128)(2,1)}, bf16[384,2304]{1,0:T(8,128)(2,1)}) custom-call(f32[640,768]{1,0:T(8,128)} %get-tuple-element.118.grad_ref.refs_5_, bf16[768,768]{1,0:T(8,128)(2,1)} %wo_ref.5, bf16[640,2304]{1,0:T(8,128)(2,1)} %get-tuple-element.119.qkv_ref, f32[80,128]{1,0:T(8,128)} %get-tuple-element.120.lse_ref, ...), custom_call_target="tpu_custom_call" | custom-call | flops 2264924160 | bytes 5898240 | tf_op jit(solution)/shard_map/attention_back/pallas_call | solution.py:808
  226.4 3.5 %fold.5 = (bf16[96,1536]{1,0:T(8,128)(2,1)}, bf16[96,1536]{1,0:T(8,128)(2,1)}, bf16[96,1536]{1,0:T(8,128)(2,1)}, bf16[96,1536]{1,0:T(8,128)(2,1)}) custom-call(bf16[192,1536]{1,0:T(8,128)(2,1)} %get-tuple-element.126.refs_0_.keep_a, bf16[192,1536]{1,0:T(8,128)(2,1)} %copy-done.14, bf16[192,1536]{1,0:T(8,128)(2,1)} %get-tuple-element.128.refs_2_.keep_b, ...), custom_call_target="tpu_custom_call" | custom-call | flops 589824 | bytes 3538944 | tf_op jit(solution)/shard_map/fold/pallas_call | solution.py:194
  233.9 4.8 %weight_back.2 = (bf16[384,1536]{1,0:T(8,128)(2,1)}, bf16[384,1536]{1,0:T(8,128)(2,1)}) custom-call(bf16[3,768,640]{2,1,0:T(8,128)(2,1)} %pad_maximum_fusion.lhs_ref, bf16[256,2304]{1,0:T(8,128)(2,1)} %get-tuple-element.121.refs_0_, bf16[384,2304]{1,0:T(8,128)(2,1)} %get-tuple-element.130.refs_0_.refs_1_, ...), custom_call_target="tpu_custom_call" | custom-call | flops 1509949440 | bytes 6094848 | tf_op jit(solution)/shard_map/weight_back/pallas_call | solution.py:860
  242.2 5.0 %weight_back.3 = (bf16[384,1536]{1,0:T(8,128)(2,1)}, bf16[384,1536]{1,0:T(8,128)(2,1)}) custom-call(bf16[3,768,640]{2,1,0:T(8,128)(2,1)} %pad_maximum_fusion.lhs_ref, bf16[256,2304]{1,0:T(8,128)(2,1)} %get-tuple-element.121.refs_0_, bf16[384,2304]{1,0:T(8,128)(2,1)} %get-tuple-element.130.refs_0_.refs_1_, bf16[256,768]{1,0:T(8,128)(2,1)} %get-tuple-element.139.refs_2_, ...), custom_call_target="tpu_custom_call" | custom-call | flops 1509949440 | bytes 6094848 | tf_op jit(solution)/shard_map/weight_back/pallas_call | solution.py:860
  251.5 4.6 %fold.6 = (bf16[192,1536]{1,0:T(8,128)(2,1)}, bf16[192,1536]{1,0:T(8,128)(2,1)}, bf16[192,1536]{1,0:T(8,128)(2,1)}, bf16[192,1536]{1,0:T(8,128)(2,1)}) custom-call(bf16[384,1536]{1,0:T(8,128)(2,1)} %get-tuple-element.137.keep_a, bf16[384,1536]{1,0:T(8,128)(2,1)} %copy-done.6, bf16[384,1536]{1,0:T(8,128)(2,1)} %get-tuple-element.142.keep_b, ...), custom_call_target="tpu_custom_call" | custom-call | flops 1179648 | bytes 7077888 | tf_op jit(solution)/shard_map/fold/pallas_call | solution.py:194
  262.4 10.4 %input_back.1 = (f32[640,768]{1,0:T(8,128)}, f32[1,768]{1,0:T(1,128)}, f32[1,768]{1,0:T(1,128)}) custom-call(bf16[256,2304]{1,0:T(8,128)(2,1)} %get-tuple-element.121.refs_0_, bf16[384,2304]{1,0:T(8,128)(2,1)} %get-tuple-element.130.refs_0_.refs_1_, bf16[768,2304]{1,0:T(8,128)(2,1)} %refs_2_.1, bf16[640,768]{1,0:T(8,128)(2,1)} %refs_3_.1, ...), custom_call_target="tpu_custom_call" | custom-call | flops 2264924160 | bytes 10420224 | tf_op jit(solution)/shard_map/input_back/pallas_call | solution.py:918
  274.6 3.5 %fold.7 = (bf16[96,1536]{1,0:T(8,128)(2,1)}, bf16[96,1536]{1,0:T(8,128)(2,1)}, bf16[96,1536]{1,0:T(8,128)(2,1)}, bf16[96,1536]{1,0:T(8,128)(2,1)}) custom-call(bf16[192,1536]{1,0:T(8,128)(2,1)} %get-tuple-element.144.refs_6_.keep_a, bf16[192,1536]{1,0:T(8,128)(2,1)} %copy-done.12, bf16[192,1536]{1,0:T(8,128)(2,1)} %get-tuple-element.155.keep_b, ...), custom_call_target="tpu_custom_call" | custom-call | flops 589824 | bytes 3538944 | tf_op jit(solution)/shard_map/fold/pallas_call | solution.py:194
  284.3 7.9 %grad_of_down.1.refs_0_ = f32[96,768]{1,0:T(8,128)} custom-call(bf16[1280,1024]{1,0:T(8,128)(2,1)} %bitcast.68, bf16[256,768]{1,0:T(8,128)(2,1)} %bitcast.71, f32[1,256]{1,0:T(1,128)} %get-tuple-element.166.col_sum_ref, f32[1,256]{1,0:T(1,128)} %get-tuple-element.167.col_count_ref, f32[1,128]{1,0:T(1,128)} %get-tuple-element.168.live_ref, ...), custom_call_target="tpu_custom_call" | custom-call | flops 1006632960 | bytes 2621440 | tf_op jit(solution)/shard_map/grad_of_down/pallas_call | solution.py:676
  295.8 3.6 %collective-permute-start.34 = (bf16[24,3072]{1,0:T(8,128)(2,1)}, bf16[24,3072]{1,0:T(8,128)(2,1)S(1)}, u32[]{:S(2)}, u32[]{:S(2)}) collective-permute-start(bf16[24,3072]{1,0:T(8,128)(2,1)} %get-tuple-element.173), channel_id=1, source_target_pairs={{0,24},{1,25},{2,26},{3,27},{4,28},{5,29},{6,30},{7,31},{8,16},{9,... | collective-permute-start | bytes 442376 | tf_op jit(solution)/shard_map/ppermute | solution.py:26
  304.6 8.0 %collective-permute-done.33 = bf16[24,3072]{1,0:T(8,128)(2,1)S(1)} collective-permute-done((bf16[24,3072]{1,0:T(8,128)(2,1)}, bf16[24,3072]{1,0:T(8,128)(2,1)S(1)}, u32[]{:S(2)}, u32[]{:S(2)}) %collective-permute-start.33) | collective-permute-done | bytes 147488 | tf_op jit(solution)/shard_map/ppermute | solution.py:26
  (233 shorter events, 102.6 us)
Async XLA Ops:
  7.2 107.3 %all-gather.2.cloned.1.call-start = ((), (), s32[]{:S(2)}) async-start(), calls=%async_computation.3 | async-start | bytes 9732096 | tf_op jit(solution)/shard_map/all_gather | solution.py:965
  11.9 27.3 %collective-permute-start.2 = (bf16[24,3072]{1,0:T(8,128)(2,1)S(1)}, bf16[24,3072]{1,0:T(8,128)(2,1)S(1)}, u32[]{:S(2)}, u32[]{:S(2)}) collective-permute-start(bf16[24,3072]{1,0:T(8,128)(2,1)S(1)} %constant_dynamic-update-slice_fusion), channel_id=1, source_target_pairs={{0,24},{1,25},{2,26},{3,27},{4,28},{5,29},{6,30},{7,31},{8,16},{9,... | collective-permute-start | bytes 442376 | tf_op jit(solution)/shard_map/ppermute | solution.py:26
  17.0 22.2 %collective-permute-start.1 = (bf16[24,3072]{1,0:T(8,128)(2,1)S(1)}, bf16[24,3072]{1,0:T(8,128)(2,1)S(1)}, u32[]{:S(2)}, u32[]{:S(2)}) collective-permute-start(bf16[24,3072]{1,0:T(8,128)(2,1)S(1)} %constant_dynamic-update-slice_fusion), channel_id=1, source_target_pairs={{0,16},{1,17},{2,18},{3,19},{4,20},{5,21},{6,22},{7,23},{8,24},{9,... | collective-permute-start | bytes 442376 | tf_op jit(solution)/shard_map/ppermute | solution.py:26
  17.0 22.2 %collective-permute-start = (bf16[24,3072]{1,0:T(8,128)(2,1)S(1)}, bf16[24,3072]{1,0:T(8,128)(2,1)S(1)}, u32[]{:S(2)}, u32[]{:S(2)}) collective-permute-start(bf16[24,3072]{1,0:T(8,128)(2,1)S(1)} %constant_dynamic-update-slice_fusion), channel_id=1, source_target_pairs={{0,8},{1,9},{2,10},{3,11},{4,12},{5,13},{6,14},{7,15},{8,0},{9,1},... | collective-permute-start | bytes 442376 | tf_op jit(solution)/shard_map/ppermute | solution.py:26
  39.3 22.9 %collective-permute-start.3 = (bf16[96,3072]{1,0:T(8,128)(2,1)S(1)}, bf16[96,3072]{1,0:T(8,128)(2,1)S(1)}, u32[]{:S(2)}, u32[]{:S(2)}) collective-permute-start(bf16[96,3072]{1,0:T(8,128)(2,1)S(1)} %pad_maximum_fusion.5.refs_0_), channel_id=1, source_target_pairs={{0,2},{1,3},{2,0},{3,1},{4,6},{5,7},{6,4},{7,5},{8,10},{9,11},{10,... | collective-permute-start | bytes 1769480 | tf_op jit(solution)/shard_map/ppermute | solution.py:26
  41.0 21.2 %collective-permute-start.4 = (bf16[96,3072]{1,0:T(8,128)(2,1)S(1)}, bf16[96,3072]{1,0:T(8,128)(2,1)S(1)}, u32[]{:S(2)}, u32[]{:S(2)}) collective-permute-start(bf16[96,3072]{1,0:T(8,128)(2,1)S(1)} %pad_maximum_fusion.5.refs_0_), channel_id=1, source_target_pairs={{0,4},{1,5},{2,6},{3,7},{4,0},{5,1},{6,2},{7,3},{8,12},{9,13},{10,... | collective-permute-start | bytes 1769480 | tf_op jit(solution)/shard_map/ppermute | solution.py:26
  73.4 18.1 %collective-permute-start.12 = (bf16[1,40,1024]{2,1,0:T(8,128)(2,1)}, bf16[1,40,1024]{2,1,0:T(8,128)(2,1)S(1)}, u32[]{:S(2)}, u32[]{:S(2)}) collective-permute-start(bf16[1,40,1024]{2,1,0:T(8,128)(2,1)} %bitcast.75), channel_id=1, source_target_pairs={{0,16},{1,17},{2,18},{3,19},{4,20},{5,21},{6,22},{7,23},{8,24},{9,... | collective-permute-start | bytes 245768 | tf_op jit(solution)/shard_map/ppermute | solution.py:26
  91.5 18.5 %collective-permute-start.13 = (bf16[2,40,1024]{2,1,0:T(8,128)(2,1)S(1)}, bf16[2,40,1024]{2,1,0:T(8,128)(2,1)S(1)}, u32[]{:S(2)}, u32[]{:S(2)}) collective-permute-start(bf16[2,40,1024]{2,1,0:T(8,128)(2,1)S(1)} %maximum_bitcast_fusion), channel_id=1, source_target_pairs={{0,8},{1,9},{2,10},{3,11},{4,12},{5,13},{6,14},{7,15},{8,0},{9,1},... | collective-permute-start | bytes 491528 | tf_op jit(solution)/shard_map/ppermute | solution.py:26
  94.6 35.4 %all-to-all-start = ((bf16[40,32,96]{2,0,1:T(8,128)(2,1)}), bf16[40,32,96]{2,0,1:T(8,128)(2,1)S(1)}, u32[]{:S(2)}, u32[]{:S(2)}) async-start(bf16[40,32,96]{2,0,1:T(8,128)(2,1)} %copy.53), calls=%async_computation | async-start | bytes 655360 | tf_op jit(solution)/shard_map/all_to_all | solution.py:1009
  114.6 15.4 %collective-permute-start.14 = (bf16[4,40,1024]{2,1,0:T(8,128)(2,1)S(1)}, bf16[4,40,1024]{2,1,0:T(8,128)(2,1)S(1)}, u32[]{:S(2)}, u32[]{:S(2)}) collective-permute-start(bf16[4,40,1024]{2,1,0:T(8,128)(2,1)S(1)} %bitcast.74), channel_id=1, source_target_pairs={{0,4},{1,5},{2,6},{3,7},{4,0},{5,1},{6,2},{7,3},{8,12},{9,13},{10,... | collective-permute-start | bytes 983048 | tf_op jit(solution)/shard_map/ppermute | solution.py:26
  130.8 16.6 %collective-permute-start.15 = (bf16[8,40,1024]{2,1,0:T(8,128)(2,1)S(1)}, bf16[8,40,1024]{2,1,0:T(8,128)(2,1)S(1)}, u32[]{:S(2)}, u32[]{:S(2)}) collective-permute-start(bf16[8,40,1024]{2,1,0:T(8,128)(2,1)S(1)} %bitcast.72), channel_id=1, source_target_pairs={{0,2},{1,3},{2,0},{3,1},{4,6},{5,7},{6,4},{7,5},{8,10},{9,11},{10,... | collective-permute-start | bytes 1966088 | tf_op jit(solution)/shard_map/ppermute | solution.py:26
  147.8 13.4 %collective-permute-start.16 = (bf16[16,40,1024]{2,1,0:T(8,128)(2,1)S(1)}, bf16[16,40,1024]{2,1,0:T(8,128)(2,1)S(1)}, u32[]{:S(2)}, u32[]{:S(2)}) collective-permute-start(bf16[16,40,1024]{2,1,0:T(8,128)(2,1)S(1)} %bitcast.69), channel_id=1, source_target_pairs={{0,1},{1,0},{2,3},{3,2},{4,5},{5,4},{6,7},{7,6},{8,9},{9,8},{10,11... | collective-permute-start | bytes 3932168 | tf_op jit(solution)/shard_map/ppermute | solution.py:26
  151.8 16.3 %all-to-all-start.1 = ((bf16[32,8,768]{2,1,0:T(8,128)(2,1)}), bf16[32,8,768]{2,1,0:T(8,128)(2,1)S(1)}, u32[]{:S(2)}, u32[]{:S(2)}) async-start(bf16[32,8,768]{2,1,0:T(8,128)(2,1)} %broadcast_in_dim.60), calls=%async_computation.1 | async-start | bytes 786432 | tf_op jit(solution)/shard_map/all_to_all | solution.py:44
  209.4 15.5 %collective-permute-start.19 = (bf16[192,1536]{1,0:T(8,128)(2,1)}, bf16[192,1536]{1,0:T(8,128)(2,1)S(1)}, u32[]{:S(2)}, u32[]{:S(2)}) collective-permute-start(bf16[192,1536]{1,0:T(8,128)(2,1)} %get-tuple-element.127.refs_1_), channel_id=1, source_target_pairs={{0,2},{1,3},{2,0},{3,1},{4,6},{5,7},{6,4},{7,5},{8,10},{9,11},{10,... | collective-permute-start | bytes 1769480 | tf_op jit(solution)/shard_map/ppermute | solution.py:26
  209.9 15.6 %collective-permute-start.20 = (bf16[192,1536]{1,0:T(8,128)(2,1)}, bf16[192,1536]{1,0:T(8,128)(2,1)S(1)}, u32[]{:S(2)}, u32[]{:S(2)}) collective-permute-start(bf16[192,1536]{1,0:T(8,128)(2,1)} %get-tuple-element.129.refs_3_), channel_id=1, source_target_pairs={{0,4},{1,5},{2,6},{3,7},{4,0},{5,1},{6,2},{7,3},{8,12},{9,13},{10,... | collective-permute-start | bytes 1769480 | tf_op jit(solution)/shard_map/ppermute | solution.py:26
  256.1 17.5 %collective-permute-start.28 = (bf16[192,1536]{1,0:T(8,128)(2,1)}, bf16[192,1536]{1,0:T(8,128)(2,1)S(1)}, u32[]{:S(2)}, u32[]{:S(2)}) collective-permute-start(bf16[192,1536]{1,0:T(8,128)(2,1)} %get-tuple-element.154), channel_id=1, source_target_pairs={{0,2},{1,3},{2,0},{3,1},{4,6},{5,7},{6,4},{7,5},{8,10},{9,11},{10,... | collective-permute-start | bytes 1769480 | tf_op jit(solution)/shard_map/ppermute | solution.py:26
  257.1 16.5 %collective-permute-start.29 = (bf16[192,1536]{1,0:T(8,128)(2,1)}, bf16[192,1536]{1,0:T(8,128)(2,1)S(1)}, u32[]{:S(2)}, u32[]{:S(2)}) collective-permute-start(bf16[192,1536]{1,0:T(8,128)(2,1)} %get-tuple-element.156), channel_id=1, source_target_pairs={{0,4},{1,5},{2,6},{3,7},{4,0},{5,1},{6,2},{7,3},{8,12},{9,13},{10,... | collective-permute-start | bytes 1769480 | tf_op jit(solution)/shard_map/ppermute | solution.py:26
  258.0 14.8 %collective-permute-start.25 = (bf16[24,3072]{1,0:T(8,128)(2,1)S(1)}, bf16[24,3072]{1,0:T(8,128)(2,1)S(1)}, u32[]{:S(2)}, u32[]{:S(2)}) collective-permute-start(bf16[24,3072]{1,0:T(8,128)(2,1)S(1)} %copy-done.42), channel_id=1, source_target_pairs={{0,8},{1,9},{2,10},{3,11},{4,12},{5,13},{6,14},{7,15},{8,0},{9,1},... | collective-permute-start | bytes 442376 | tf_op jit(solution)/shard_map/ppermute | solution.py:26
  258.7 14.1 %collective-permute-start.26 = (bf16[24,3072]{1,0:T(8,128)(2,1)S(1)}, bf16[24,3072]{1,0:T(8,128)(2,1)S(1)}, u32[]{:S(2)}, u32[]{:S(2)}) collective-permute-start(bf16[24,3072]{1,0:T(8,128)(2,1)S(1)} %copy-done.41), channel_id=1, source_target_pairs={{0,16},{1,17},{2,18},{3,19},{4,20},{5,21},{6,22},{7,23},{8,24},{9,... | collective-permute-start | bytes 442376 | tf_op jit(solution)/shard_map/ppermute | solution.py:26
  259.7 13.2 %collective-permute-start.27 = (bf16[24,3072]{1,0:T(8,128)(2,1)S(1)}, bf16[24,3072]{1,0:T(8,128)(2,1)S(1)}, u32[]{:S(2)}, u32[]{:S(2)}) collective-permute-start(bf16[24,3072]{1,0:T(8,128)(2,1)S(1)} %copy-done.40), channel_id=1, source_target_pairs={{0,24},{1,25},{2,26},{3,27},{4,28},{5,29},{6,30},{7,31},{8,16},{9,... | collective-permute-start | bytes 442376 | tf_op jit(solution)/shard_map/ppermute | solution.py:26
  278.1 14.1 %collective-permute-start.30 = (bf16[96,1536]{1,0:T(8,128)(2,1)}, bf16[96,1536]{1,0:T(8,128)(2,1)S(1)}, u32[]{:S(2)}, u32[]{:S(2)}) collective-permute-start(bf16[96,1536]{1,0:T(8,128)(2,1)} %get-tuple-element.163.refs_1_), channel_id=1, source_target_pairs={{0,4},{1,5},{2,6},{3,7},{4,0},{5,1},{6,2},{7,3},{8,12},{9,13},{10,... | collective-permute-start | bytes 884744 | tf_op jit(solution)/shard_map/ppermute | solution.py:26
  281.0 33.0 %all-to-all-start.2 = ((f32[32,1,4,768]{3,2,1,0:T(4,128)}), f32[32,1,4,768]{3,2,1,0:T(4,128)S(1)}, u32[]{:S(2)}, u32[]{:S(2)}) async-start(f32[32,1,4,768]{3,2,1,0:T(4,128)} %broadcast_in_dim.61), calls=%async_computation.2 | async-start | bytes 786432 | tf_op jit(solution)/shard_map/all_to_all | solution.py:44
  299.4 13.2 %collective-permute-start.33 = (bf16[24,3072]{1,0:T(8,128)(2,1)}, bf16[24,3072]{1,0:T(8,128)(2,1)S(1)}, u32[]{:S(2)}, u32[]{:S(2)}) collective-permute-start(bf16[24,3072]{1,0:T(8,128)(2,1)} %get-tuple-element.172), channel_id=1, source_target_pairs={{0,16},{1,17},{2,18},{3,19},{4,20},{5,21},{6,22},{7,23},{8,24},{9,... | collective-permute-start | bytes 442376 | tf_op jit(solution)/shard_map/ppermute | solution.py:26
  299.4 13.2 %collective-permute-start.32 = (bf16[24,3072]{1,0:T(8,128)(2,1)}, bf16[24,3072]{1,0:T(8,128)(2,1)S(1)}, u32[]{:S(2)}, u32[]{:S(2)}) collective-permute-start(bf16[24,3072]{1,0:T(8,128)(2,1)} %get-tuple-element.171), channel_id=1, source_target_pairs={{0,8},{1,9},{2,10},{3,11},{4,12},{5,13},{6,14},{7,15},{8,0},{9,1},... | collective-permute-start | bytes 442376 | tf_op jit(solution)/shard_map/ppermute | solution.py:26
  (62 other events, 472.2 us)
Sparse Core Ops, SparseCore 0:
  11.0 103.5 all-gather.1

commit v2 on v1

--- a/solution.py
+++ b/solution.py
@@ -71,10 +71,9 @@
     return jnp.concatenate([shard] + [swapped(shard, mask) for mask in (8, 16, 24)], axis=0)
 
 
-def gathered_rows(line, beside, above):
-    half = line.shape[0] // 2
-    pieces = [line, beside, above, swapped(beside[:half], 4), swapped(above[half:], 2)]
-    return pieces + [swapped(piece, 1) for piece in pieces]
+def diagonal(beside, above):
+    half = beside.shape[0] // 2
+    return swapped(beside[:half], 4), swapped(above[half:], 2)
 
 
 def in_turn(first, then):
@@ -342,19 +341,19 @@
     copies, row = [], 0
     for k, piece in enumerate(refs[:-9]):
         place = w_ref.at[pl.ds(row, piece.shape[0]), :]
-        copies.append(pltpu.make_async_copy(piece, place, sems.at[k]))
+        copies.append(pltpu.make_async_copy(piece.at[:, : 4 * D], place, sems.at[k]))
         row += piece.shape[0]
     for copy in copies:
         copy.start()
 
-    def place_columns(src):
+    def place_columns(src, dst):
         @pl.loop(0, D // 256)
         def _(step):
             at = pl.ds(pl.multiple_of(step * 256, 256), 256)
-            placed_ref[:, at] = mul_bt(src[...], perm_ref[at, :]).astype(bf16)
+            dst[:, at] = mul_bt(src[...], perm_ref[at, :]).astype(bf16)
 
     norm_rows(x_ref, h1_ref, g1_ref[...].astype(f32), b1_ref[...].astype(f32), chunk)
-    place_columns(h1_ref)
+    place_columns(h1_ref, placed_ref)
     for copy in copies:
         copy.wait()
 
@@ -367,7 +366,7 @@
         one = same_sequence(count, row0, keys, key0, IMG_LEN)
         mask = jnp.concatenate([one, one], axis=0)
         attend_along(qkv_ref, att_ref, pl.ds(row0, count), pl.ds(key0, keys), mask)
-    place_columns(att_ref)
+    place_columns(att_ref, placed_ref)
 
     @pl.loop(0, D // 256)
     def _(step):
@@ -375,7 +374,8 @@
         there = pl.ds(pl.multiple_of(step * 256 + 3 * D, 256), 256)
         mid_ref[:, at] = x_ref[:, at].astype(f32) + mul(placed_ref[...], w_ref[:, there])
 
-    norm_rows(mid_ref, h2_ref, g2_ref[...].astype(f32), b2_ref[...].astype(f32), chunk)
+    norm_rows(mid_ref, h1_ref, g2_ref[...].astype(f32), b2_ref[...].astype(f32), chunk)
+    place_columns(h1_ref, h2_ref)
     for k in range(rows // IMG_LEN):
         first, last = k * IMG_LEN, (k + 1) * IMG_LEN
         start, end = first // 8 * 8, -(-last // 8) * 8
@@ -513,26 +513,45 @@
     )(normed2, weight_up, weight_down, middle_sum, *after)
 
 
-def image_up_kernel(fold, h2_ref, wu_ref, wd_ref, sum_ref, *refs):
-    out_ref, acc = refs[-2:]
+def image_up_kernel(fold, count, h2_ref, wd_ref, sum_ref, *refs):
+    pieces = refs[:count]
+    out_ref, acc, wu_ref, sems = refs[-4:]
     step = pl.program_id(0)
-    rows, count = h2_ref.shape[0], sum_ref.shape[0]
+    rows, images = h2_ref.shape[0], sum_ref.shape[0]
     chunk = 80
-    summed = jnp.zeros((count, TILE), f32)
+
+    def copies(tile):
+        row = 0
+        for k, piece in enumerate(pieces):
+            cols = pl.ds(pl.multiple_of(4 * D + tile * TILE, TILE), TILE)
+            there = wu_ref.at[tile, pl.ds(row, piece.shape[0]), :]
+            yield pltpu.make_async_copy(piece.at[:, cols], there, sems.at[tile, k])
+            row += piece.shape[0]
+
+    @pl.when(step == 0)
+    def _():
+        for tile in range(FF // TILE):
+            for copy in copies(tile):
+                copy.start()
+
+    for copy in copies(step):
+        copy.wait()
+    weight = wu_ref[step]
+    summed = jnp.zeros((images, TILE), f32)
     for k in range(rows // chunk):
-        inner = mul(h2_ref[k * chunk : (k + 1) * chunk, :], wu_ref[...])
+        inner = mul(h2_ref[k * chunk : (k + 1) * chunk, :], weight)
         value, _ = gelu_parts(inner)
-        pool = pool_matrix(count, chunk, k * chunk, IMG_LEN)
+        pool = pool_matrix(images, chunk, k * chunk, IMG_LEN)
         summed = summed + mul(pool, value.astype(bf16))
     mean = two_terms(summed * (1.0 / IMG_LEN))
     place = lax.broadcasted_iota(jnp.int32, (TILE, TILE // fold), 0)
     picked = lax.broadcasted_iota(jnp.int32, (TILE, TILE // fold), 1) * fold
-    terms = jnp.zeros((2 * count, D), f32)
+    terms = jnp.zeros((2 * images, D), f32)
     for k in range(fold):
         chosen = jnp.where(place == picked + k, 1.0, 0.0).astype(bf16)
         part = mul(mean, chosen).astype(bf16)
         terms = terms + mul(part, wd_ref[:, k * D : (k + 1) * D])
-    added = terms[:count] + terms[count:]
+    added = terms[:images] + terms[images:]
 
     @pl.when(step == 0)
     def _():
@@ -547,27 +566,31 @@
         out_ref[...] = unit_rows(acc[...])[0].astype(bf16)
 
 
-def image_up(normed2, whole, up_col, down_col, middle_sum, after=()):
-    rows, count = normed2.shape[0], middle_sum.shape[0]
+def image_up(normed2, pieces, whole, middle_sum, after=()):
+    rows, images = normed2.shape[0], middle_sum.shape[0]
     fold = FF // D
     fixed = lambda shape: pl.BlockSpec(shape, lambda i: (0, 0))
     return pl.pallas_call(
-        functools.partial(image_up_kernel, fold),
+        functools.partial(image_up_kernel, fold, len(pieces)),
         grid=(FF // TILE,),
-        out_shape=jax.ShapeDtypeStruct((count, D), bf16),
+        out_shape=jax.ShapeDtypeStruct((images, D), bf16),
         in_specs=[
             fixed((rows, D)),
-            pl.BlockSpec((D, TILE), lambda i: (0, up_col // TILE + i)),
-            pl.BlockSpec((TILE // fold, fold * D), lambda i: (i, down_col // (fold * D))),
-            fixed((count, D)),
+            pl.BlockSpec((TILE // fold, fold * D), lambda i: (i, 0)),
+            fixed((images, D)),
         ]
+        + anywhere(pieces)
         + anywhere(after),
-        out_specs=fixed((count, D)),
-        scratch_shapes=[pltpu.VMEM((count, D), f32)],
+        out_specs=fixed((images, D)),
+        scratch_shapes=[
+            pltpu.VMEM((images, D), f32),
+            pltpu.VMEM((FF // TILE, D, TILE), bf16),
+            pltpu.SemaphoreType.DMA((FF // TILE, len(pieces))),
+        ],
         compiler_params=params(),
         cost_estimate=cost(2 * rows * D * FF, 4 * D * FF, 15 * rows * FF),
         name="image_up",
-    )(normed2, whole, whole, middle_sum, *after)
+    )(normed2, whole, middle_sum, *pieces, *after)
 
 
 def loss_parts(text_rows, pos, image_all):
@@ -962,14 +985,11 @@
     cap_local = matches.shape[0]
     total_images = matches.shape[1]
 
-    whole = lax.all_gather(
-        jnp.concatenate([img_up.reshape(per, FF), img_down.reshape(per, FF)], axis=1),
-        AXIS,
-        axis=0,
-        tiled=True,
-    )
+    whole = lax.all_gather(img_down.reshape(per, FF), AXIS, axis=0, tiled=True)
     small = peers == 32
-    shard = jnp.concatenate([img_qkv.reshape(per, 3 * D), img_out.reshape(per, D)], axis=1)
+    shard = jnp.concatenate(
+        [img_qkv.reshape(per, 3 * D), img_out.reshape(per, D), img_up.reshape(per, FF)], axis=1
+    )
     if small:
         line, perm = gathered_line(shard), row_order((1, 4, 2, 16, 8))
     else:
@@ -984,7 +1004,6 @@
         normed2, txt_up, txt_down, middle_sum, (line,)
     )
     text_unit, (beside, above) = in_turn(text_unit, (beside, above))
-    pieces = gathered_rows(line, beside, above) if small else [line]
 
     ends_at = jnp.cumsum(counts)
     slot_ids = lax.iota(jnp.int32, cap_local)
@@ -994,29 +1013,37 @@
     columns = lax.iota(jnp.int32, total_images)
     positive = ((matches > 0) | (owner[:, None] == columns[None, :])) & live[:, None]
 
-    own_pack = packed(text_unit, positive.astype(bf16), pieces[1:5] if small else ())
+    own_pack = packed(text_unit, positive.astype(bf16), ())
+    pieces = [line]
+    if small:
+        held = own_pack[None]
+        first, second = diagonal(beside, above)
+        other, first, second = lax.optimization_barrier((swapped(held, 16), first, second))
+        held = joined(held, other, 16)
+        pieces = [line, beside, above, first, second]
+        pieces = pieces + [swapped(piece, 1) for piece in pieces]
 
     normed_img, middle_img = image_front(
         images, pieces, perm, img_gain1, img_bias1, img_gain2, img_bias2
     )
     if small:
-        held = own_pack[None]
         scaled_sum = (hidden_sum * inverse[:, :1]).astype(bf16)
         normed_img, scaled_sum, other = lax.optimization_barrier(
-            (normed_img, scaled_sum, swapped(held, 16))
+            (normed_img, scaled_sum, swapped(held, 8))
         )
-        held = joined(held, other, 16)
+        held = joined(held, other, 8)
         hidden_cols = lax.all_to_all(scaled_sum, AXIS, split_axis=1, concat_axis=0, tiled=True)
-        whole, other = in_turn(whole, swapped(held, 8))
-        held = joined(held, other, 8)
         other = swapped(held, 4)
-    image_low = image_up(normed_img, whole, 0, FF, middle_img)
+    image_low = image_up(normed_img, pieces, whole, middle_img)
     if small:
         image_low, other, hidden_cols = lax.optimization_barrier((image_low, other, hidden_cols))
         held = joined(held, other, 4)
-        held = joined(held, swapped(held, 2), 2)
+        other = swapped(held, 2)
+    image_all = spread(image_low).reshape(total_images, D)
+    if small:
+        image_all, other = in_turn(image_all, other)
+        held = joined(held, other, 2)
         text_pack = joined(held, swapped(held, 1), 1).reshape(-1, D + total_images)
-    image_all = spread(image_low).reshape(total_images, D)
 
     order_a, order_b, tail = stage_orders()
     matrix_a, matrix_b = row_order(order_a + tail[::-1]), row_order(order_b + tail[::-1])

time: 323 us -> 354 us (1.096); the launches traced: 322 us -> 348 us
  Pallas kernels: 153 us -> 164 us
  waiting for transfers between devices: 57.6 us -> 66.2 us
  local copies, waits for them, and re-layouts: 29.5 us -> 35.8 us
    ppermute x35, waiting for transfers between devices: 48.6 us -> 66.1 us  [swapped(): return lax.ppermute(value, AXIS, [(i, i ^ mask) for i in range(peers)])]
    pallas_call x4, Pallas kernels: 16.1 us -> 25 us  [fold(): pl.pallas_call(fold_kernel, grid=(cols // tile,), out_shape=[jax.ShapeDty...]
    all_to_all x2, waiting for transfers between devices: 4.54 us -> 0.01 us  [spread(): return lax.all_to_all(copies, AXIS, split_axis=0, concat_axis=0, tiled=True)]
    all_gather x1, waiting for transfers between devices: 4.52 us -> 0.01 us  [local(): whole = lax.all_gather(img_down.reshape(per, FF), AXIS, axis=0, tiled=True)]
    unnamed x96 -> x85, local copies, waits for them, and re-layouts: 12 us -> 10.8 us
  transfers between devices with their start and end apart: 39 -> 39, of which waited for: 12 -> 11; matrix products, arithmetic and copies ran while one was open for 11% -> 11% of each run, Pallas kernels for 34% -> 33%
where the time goes in v2:
time: 354 us; the launch traced here: 348 us
  Pallas kernels  164 us (46%)
  waiting for transfers between devices  66.2 us (19%)
  starting transfers between devices  47.9 us (14%)
  local copies, waits for them, and re-layouts  35.8 us (10%)
  between operations  14.9 us (4%)
  other arithmetic  12.2 us (3%)
  matrix products  7.25 us (2%)
    ppermute x35, waiting for transfers between devices, swapped(): return lax.ppermute(value, AXIS, [(i, i ^ mask) for i in range(peers)])  66.1 us
    ppermute x35, starting transfers between devices, swapped(): return lax.ppermute(value, AXIS, [(i, i ^ mask) for i in range(peers)])  36.1 us
    pallas_call x4, Pallas kernels, fold(): pl.pallas_call(fold_kernel, grid=(cols // tile,), out_shape=[jax.ShapeDty...  25 us
    pallas_call x1, Pallas kernels, mlp_back(): pl.pallas_call(mlp_back_kernel, grid=(steps,), out_shape=[part] * 4 + [ja...  21.4 us
    pallas_call x1, Pallas kernels, text_front(): pl.pallas_call(text_front_kernel, out_shape=[jax.ShapeDtypeStruct(*item)...  18.1 us
    pallas_call x2, Pallas kernels, attention_back(): pl.pallas_call(attention_back_kernel, grid=(count,), out_shape=[jax.Shape...  16.8 us
    pallas_call x1, Pallas kernels, image_up(): pl.pallas_call(functools.partial(image_up_kernel, fold, len(pieces)), gri...  15.5 us
    pallas_call x1, Pallas kernels, image_front(): pl.pallas_call(functools.partial(image_front_kernel, windows), out_shape=...  14.9 us
  transfers between devices with their start and end apart: 39, of which 11 were waited for; matrix products, arithmetic and copies ran while one was open for 11% of the time, Pallas kernels for 33%

profile of v2, /device:TPU:0, one launch (start us, length us, event | category | flops | bytes accessed | tf_op | source)
XLA Modules:
  0.0 347.7 jit_solution(744820249089274951)
XLA Ops:
  11.8 5.1 %collective-permute-start.2 = (bf16[24,6144]{1,0:T(8,128)(2,1)S(1)}, bf16[24,6144]{1,0:T(8,128)(2,1)S(1)}, u32[]{:S(2)}, u32[]{:S(2)}) collective-permute-start(bf16[24,6144]{1,0:T(8,128)(2,1)S(1)} %constant_dynamic-update-slice_fusion), channel_id=1, source_target_pairs={{0,24},{1,25},{2,26},{3,27},{4,28},{5,29},{6,30},{7,31},{8,16},{9,... | collective-permute-start | bytes 884744 | tf_op jit(solution)/shard_map/ppermute | solution.py:26
  22.6 18.1 %text_front.1 = (bf16[640,768]{1,0:T(8,128)(2,1)}, bf16[640,2304]{1,0:T(8,128)(2,1)}, bf16[640,768]{1,0:T(8,128)(2,1)}, f32[640,768]{1,0:T(8,128)}, bf16[640,768...) custom-call(bf16[640,768]{1,0:T(8,128)(2,1)} %refs_3_.1, f32[1,768]{1,0:T(1,128)} %broadcast_in_dim.26.g1_ref.refs_4_, ...), custom_call_target="tpu_custom_call" | custom-call | flops 3019898880 | bytes 11599872 | tf_op jit(solution)/shard_map/text_front/pallas_call | solution.py:327
  40.7 4.5 %collective-permute-done.1 = bf16[24,6144]{1,0:T(8,128)(2,1)S(1)} collective-permute-done((bf16[24,6144]{1,0:T(8,128)(2,1)S(1)}, bf16[24,6144]{1,0:T(8,128)(2,1)S(1)}, u32[]{:S(2)}, u32[]{:S(2)}) %collective-permute-start.1) | collective-permute-done | bytes 294944 | tf_op jit(solution)/shard_map/ppermute | solution.py:26
  50.9 13.8 %text_up.1 = (bf16[640,3072]{1,0:T(8,128)(2,1)}, f32[40,3072]{1,0:T(8,128)}, f32[40,768]{1,0:T(8,128)}, f32[40,128]{1,0:T(8,128)}) custom-call(bf16[640,768]{1,0:T(8,128)(2,1)} %get-tuple-element.99.h2_ref, bf16[768,3072]{1,0:T(8,128)(2,1)} %wu_ref.3, bf16[3072,768]{1,0:T(8,128)(2,1)} %wd_ref.3, f32[40,768]{1,0:T(8,128)} %get-tuple-element.100.sum_ref, ...), custom_call_target="tpu_custom_call" | custom-call | flops 3019898880 | bytes 13369344 | tf_op jit(solution)/shard_map/text_up/pallas_call | solution.py:487
  64.8 21.1 %collective-permute-done.3.refs_1_ = bf16[96,6144]{1,0:T(8,128)(2,1)S(1)} collective-permute-done((bf16[96,6144]{1,0:T(8,128)(2,1)}, bf16[96,6144]{1,0:T(8,128)(2,1)S(1)}, u32[]{:S(2)}, u32[]{:S(2)}) %collective-permute-start.3) | collective-permute-done | bytes 1179680 | tf_op jit(solution)/shard_map/ppermute | solution.py:26
  93.4 5.1 %collective-permute-done.5 = bf16[1,40,1024]{2,1,0:T(8,128)(2,1)} collective-permute-done((bf16[1,40,1024]{2,1,0:T(8,128)(2,1)}, bf16[1,40,1024]{2,1,0:T(8,128)(2,1)}, u32[]{:S(2)}, u32[]{:S(2)}) %collective-permute-start.5) | collective-permute-done | bytes 81952 | tf_op jit(solution)/shard_map/ppermute | solution.py:26
  109.4 14.9 %image_front.1 = (bf16[400,768]{1,0:T(8,128)(2,1)}, f32[8,768]{1,0:T(8,128)}) custom-call(bf16[400,768]{1,0:T(8,128)(2,1)} %x_ref.3, bf16[768,768]{1,0:T(8,128)(2,1)} %fusion.5.perm_ref, bf16[1,768]{1,0:T(2,128)(2,1)} %broadcast_in_dim.22.g1_ref, bf16[1,768]{1,0:T(2,128)(2,1)} %broadcast_in_dim.23.b1_ref, bf16[1,768]{1,0:T(2,128)(2,1)} %broadcast_in_dim.24.g2_ref, ...), custom_call_target="tpu_custom_call" | custom-call | flops 2831155200 | bytes 4718592 | tf_op jit(solution)/shard_map/image_front/pallas_call | solution.py:392
  132.3 15.5 %image_up.1 = bf16[8,768]{1,0:T(8,128)(2,1)} custom-call(bf16[400,768]{1,0:T(8,128)(2,1)} %get-tuple-element.111.h2_ref, bf16[768,3072]{1,0:T(8,128)(2,1)} %all-gather.2.cloned.1.call-done.wd_ref, f32[8,768]{1,0:T(8,128)} %get-tuple-element.112.sum_ref, bf16[96,6144]{1,0:T(8,128)(2,1)} %pad_maximum_fusion.4.refs_0_, bf16[96,6144]{1,0:T(8,128)(2,1)} %copy-done.1, ...), custom_call_target="tpu_custom_call" | custom-call | flops 1887436800 | bytes 9437184 | tf_op jit(solution)/shard_map/image_up/pallas_call | solution.py:573
  149.4 4.9 %all-to-all-start.1 = ((bf16[32,8,768]{2,1,0:T(8,128)(2,1)}), bf16[32,8,768]{2,1,0:T(8,128)(2,1)S(1)}, u32[]{:S(2)}, u32[]{:S(2)}) async-start(bf16[32,8,768]{2,1,0:T(8,128)(2,1)} %broadcast_in_dim.60), calls=%async_computation.1 | async-start | bytes 786432 | tf_op jit(solution)/shard_map/all_to_all | solution.py:44
  156.4 18.9 %collective-permute-done.15 = bf16[8,40,1024]{2,1,0:T(8,128)(2,1)S(1)} collective-permute-done((bf16[8,40,1024]{2,1,0:T(8,128)(2,1)S(1)}, bf16[8,40,1024]{2,1,0:T(8,128)(2,1)S(1)}, u32[]{:S(2)}, u32[]{:S(2)}) %collective-permute-start.15) | collective-permute-done | bytes 655392 | tf_op jit(solution)/shard_map/ppermute | solution.py:26
  183.8 4.0 %loss_and_rows.1 = (f32[1,128]{1,0:T(1,128)}, f32[40,768]{1,0:T(8,128)}, bf16[40,768]{1,0:T(8,128)(2,1)}, f32[1,256]{1,0:T(1,128)}, f32[1,256]{1,0:T(1,128)}, /*index=5*/f32[1,128]{1,0:T(1,128)}) custom-call(bf16[1280,1024]{1,0:T(8,128)(2,1)} %bitcast.67, bf16[256,768]{1,0:T(8,128)(2,1)} %bitcast.70, bf16[40,1024]{1,0:T(8,128)(2,1)} %packed.1.own_ref, ...), custom_call_target="tpu_custom_call" | custom-call | flops 503316480 | bytes 2621440 | tf_op jit(solution)/shard_map/loss_and_rows/pallas_call | solution.py:667
  187.8 21.4 %mlp_back.1 = (bf16[384,1536]{1,0:T(8,128)(2,1)}, bf16[384,1536]{1,0:T(8,128)(2,1)}, bf16[384,1536]{1,0:T(8,128)(2,1)}, bf16[384,1536]{1,0:T(8,128)(2,1)}, f32[6...) custom-call(bf16[40,768]{1,0:T(8,128)(2,1)} %get-tuple-element.120.low_ref, bf16[3072,768]{1,0:T(8,128)(2,1)} %wd_ref.3, ...), custom_call_target="tpu_custom_call" | custom-call | flops 6039797760 | bytes 18087936 | tf_op jit(solution)/shard_map/mlp_back/pallas_call | solution.py:776
  211.1 7.2 %attention_back.2 = (bf16[256,768]{1,0:T(8,128)(2,1)}, bf16[256,2304]{1,0:T(8,128)(2,1)}) custom-call(f32[640,768]{1,0:T(8,128)} %get-tuple-element.124.grad_ref.refs_5_, bf16[768,768]{1,0:T(8,128)(2,1)} %wo_ref.5, bf16[640,2304]{1,0:T(8,128)(2,1)} %get-tuple-element.125.qkv_ref, f32[80,128]{1,0:T(8,128)} %get-tuple-element.126.lse_ref), custom_call_target="tpu_custom_call" | custom-call | flops 1509949440 | bytes 4325376 | tf_op jit(solution)/shard_map/attention_back/pallas_call | solution.py:831
  219.7 13.4 %fold.4 = (bf16[192,1536]{1,0:T(8,128)(2,1)}, bf16[192,1536]{1,0:T(8,128)(2,1)}, bf16[192,1536]{1,0:T(8,128)(2,1)}, bf16[192,1536]{1,0:T(8,128)(2,1)}) custom-call(bf16[384,1536]{1,0:T(8,128)(2,1)} %get-tuple-element.128.keep_a, bf16[384,1536]{1,0:T(8,128)(2,1)} %copy-done.8, bf16[384,1536]{1,0:T(8,128)(2,1)} %get-tuple-element.130.keep_b, ...), custom_call_target="tpu_custom_call" | custom-call | flops 1179648 | bytes 7077888 | tf_op jit(solution)/shard_map/fold/pallas_call | solution.py:193
  237.9 9.6 %attention_back.3 = (bf16[384,768]{1,0:T(8,128)(2,1)}, bf16[384,2304]{1,0:T(8,128)(2,1)}) custom-call(f32[640,768]{1,0:T(8,128)} %get-tuple-element.124.grad_ref.refs_5_, bf16[768,768]{1,0:T(8,128)(2,1)} %wo_ref.5, bf16[640,2304]{1,0:T(8,128)(2,1)} %get-tuple-element.125.qkv_ref, f32[80,128]{1,0:T(8,128)} %get-tuple-element.126.lse_ref, ...), custom_call_target="tpu_custom_call" | custom-call | flops 2264924160 | bytes 5898240 | tf_op jit(solution)/shard_map/attention_back/pallas_call | solution.py:831
  250.4 3.5 %fold.5 = (bf16[96,1536]{1,0:T(8,128)(2,1)}, bf16[96,1536]{1,0:T(8,128)(2,1)}, bf16[96,1536]{1,0:T(8,128)(2,1)}, bf16[96,1536]{1,0:T(8,128)(2,1)}) custom-call(bf16[192,1536]{1,0:T(8,128)(2,1)} %get-tuple-element.132.refs_0_.keep_a, bf16[192,1536]{1,0:T(8,128)(2,1)} %copy-done.19, bf16[192,1536]{1,0:T(8,128)(2,1)} %get-tuple-element.134.refs_2_.keep_b, ...), custom_call_target="tpu_custom_call" | custom-call | flops 589824 | bytes 3538944 | tf_op jit(solution)/shard_map/fold/pallas_call | solution.py:193
  258.7 4.8 %weight_back.2 = (bf16[384,1536]{1,0:T(8,128)(2,1)}, bf16[384,1536]{1,0:T(8,128)(2,1)}) custom-call(bf16[3,768,640]{2,1,0:T(8,128)(2,1)} %pad_maximum_fusion.lhs_ref, bf16[256,2304]{1,0:T(8,128)(2,1)} %get-tuple-element.127.refs_0_, bf16[384,2304]{1,0:T(8,128)(2,1)} %get-tuple-element.136.refs_0_.refs_1_, ...), custom_call_target="tpu_custom_call" | custom-call | flops 1509949440 | bytes 6094848 | tf_op jit(solution)/shard_map/weight_back/pallas_call | solution.py:883
  267.0 5.1 %weight_back.3 = (bf16[384,1536]{1,0:T(8,128)(2,1)}, bf16[384,1536]{1,0:T(8,128)(2,1)}) custom-call(bf16[3,768,640]{2,1,0:T(8,128)(2,1)} %pad_maximum_fusion.lhs_ref, bf16[256,2304]{1,0:T(8,128)(2,1)} %get-tuple-element.127.refs_0_, bf16[384,2304]{1,0:T(8,128)(2,1)} %get-tuple-element.136.refs_0_.refs_1_, bf16[256,768]{1,0:T(8,128)(2,1)} %get-tuple-element.145.refs_2_, ...), custom_call_target="tpu_custom_call" | custom-call | flops 1509949440 | bytes 6094848 | tf_op jit(solution)/shard_map/weight_back/pallas_call | solution.py:883
  276.3 4.6 %fold.6 = (bf16[192,1536]{1,0:T(8,128)(2,1)}, bf16[192,1536]{1,0:T(8,128)(2,1)}, bf16[192,1536]{1,0:T(8,128)(2,1)}, bf16[192,1536]{1,0:T(8,128)(2,1)}) custom-call(bf16[384,1536]{1,0:T(8,128)(2,1)} %get-tuple-element.143.keep_a, bf16[384,1536]{1,0:T(8,128)(2,1)} %copy-done.7, bf16[384,1536]{1,0:T(8,128)(2,1)} %get-tuple-element.148.keep_b, ...), custom_call_target="tpu_custom_call" | custom-call | flops 1179648 | bytes 7077888 | tf_op jit(solution)/shard_map/fold/pallas_call | solution.py:193
  286.9 10.4 %input_back.1 = (f32[640,768]{1,0:T(8,128)}, f32[1,768]{1,0:T(1,128)}, f32[1,768]{1,0:T(1,128)}) custom-call(bf16[256,2304]{1,0:T(8,128)(2,1)} %get-tuple-element.127.refs_0_, bf16[384,2304]{1,0:T(8,128)(2,1)} %get-tuple-element.136.refs_0_.refs_1_, bf16[768,2304]{1,0:T(8,128)(2,1)} %refs_2_.1, bf16[640,768]{1,0:T(8,128)(2,1)} %refs_3_.1, ...), custom_call_target="tpu_custom_call" | custom-call | flops 2264924160 | bytes 10420224 | tf_op jit(solution)/shard_map/input_back/pallas_call | solution.py:941
  306.4 3.8 %all-to-all-start.2 = ((f32[32,1,4,768]{3,2,1,0:T(4,128)}), f32[32,1,4,768]{3,2,1,0:T(4,128)S(1)}, u32[]{:S(2)}, u32[]{:S(2)}) async-start(f32[32,1,4,768]{3,2,1,0:T(4,128)} %broadcast_in_dim.61), calls=%async_computation.2 | async-start | bytes 786432 | tf_op jit(solution)/shard_map/all_to_all | solution.py:44
  310.2 7.9 %grad_of_down.1.refs_0_ = f32[96,768]{1,0:T(8,128)} custom-call(bf16[1280,1024]{1,0:T(8,128)(2,1)} %bitcast.68, bf16[256,768]{1,0:T(8,128)(2,1)} %bitcast.71, f32[1,256]{1,0:T(1,128)} %get-tuple-element.172.col_sum_ref, f32[1,256]{1,0:T(1,128)} %get-tuple-element.173.col_count_ref, f32[1,128]{1,0:T(1,128)} %get-tuple-element.174.live_ref, ...), custom_call_target="tpu_custom_call" | custom-call | flops 1006632960 | bytes 2621440 | tf_op jit(solution)/shard_map/grad_of_down/pallas_call | solution.py:699
  321.7 3.6 %collective-permute-start.34 = (bf16[24,3072]{1,0:T(8,128)(2,1)}, bf16[24,3072]{1,0:T(8,128)(2,1)S(1)}, u32[]{:S(2)}, u32[]{:S(2)}) collective-permute-start(bf16[24,3072]{1,0:T(8,128)(2,1)} %get-tuple-element.179), channel_id=1, source_target_pairs={{0,24},{1,25},{2,26},{3,27},{4,28},{5,29},{6,30},{7,31},{8,16},{9,... | collective-permute-start | bytes 442376 | tf_op jit(solution)/shard_map/ppermute | solution.py:26
  330.5 8.0 %collective-permute-done.33 = bf16[24,3072]{1,0:T(8,128)(2,1)S(1)} collective-permute-done((bf16[24,3072]{1,0:T(8,128)(2,1)}, bf16[24,3072]{1,0:T(8,128)(2,1)S(1)}, u32[]{:S(2)}, u32[]{:S(2)}) %collective-permute-start.33) | collective-permute-done | bytes 147488 | tf_op jit(solution)/shard_map/ppermute | solution.py:26
  (221 shorter events, 103.5 us)
Async XLA Ops:
  7.2 125.1 %all-gather.2.cloned.1.call-start = ((), (), s32[]{:S(2)}) async-start(), calls=%async_computation.3 | async-start | bytes 4866048 | tf_op jit(solution)/shard_map/all_gather | solution.py:988
  11.8 28.9 %collective-permute-start.2 = (bf16[24,6144]{1,0:T(8,128)(2,1)S(1)}, bf16[24,6144]{1,0:T(8,128)(2,1)S(1)}, u32[]{:S(2)}, u32[]{:S(2)}) collective-permute-start(bf16[24,6144]{1,0:T(8,128)(2,1)S(1)} %constant_dynamic-update-slice_fusion), channel_id=1, source_target_pairs={{0,24},{1,25},{2,26},{3,27},{4,28},{5,29},{6,30},{7,31},{8,16},{9,... | collective-permute-start | bytes 884744 | tf_op jit(solution)/shard_map/ppermute | solution.py:26
  16.9 28.3 %collective-permute-start.1 = (bf16[24,6144]{1,0:T(8,128)(2,1)S(1)}, bf16[24,6144]{1,0:T(8,128)(2,1)S(1)}, u32[]{:S(2)}, u32[]{:S(2)}) collective-permute-start(bf16[24,6144]{1,0:T(8,128)(2,1)S(1)} %constant_dynamic-update-slice_fusion), channel_id=1, source_target_pairs={{0,16},{1,17},{2,18},{3,19},{4,20},{5,21},{6,22},{7,23},{8,24},{9,... | collective-permute-start | bytes 884744 | tf_op jit(solution)/shard_map/ppermute | solution.py:26
  16.9 28.3 %collective-permute-start = (bf16[24,6144]{1,0:T(8,128)(2,1)S(1)}, bf16[24,6144]{1,0:T(8,128)(2,1)S(1)}, u32[]{:S(2)}, u32[]{:S(2)}) collective-permute-start(bf16[24,6144]{1,0:T(8,128)(2,1)S(1)} %constant_dynamic-update-slice_fusion), channel_id=1, source_target_pairs={{0,8},{1,9},{2,10},{3,11},{4,12},{5,13},{6,14},{7,15},{8,0},{9,1},... | collective-permute-start | bytes 884744 | tf_op jit(solution)/shard_map/ppermute | solution.py:26
  46.4 39.5 %collective-permute-start.3 = (bf16[96,6144]{1,0:T(8,128)(2,1)}, bf16[96,6144]{1,0:T(8,128)(2,1)S(1)}, u32[]{:S(2)}, u32[]{:S(2)}) collective-permute-start(bf16[96,6144]{1,0:T(8,128)(2,1)} %pad_maximum_fusion.4.refs_0_), channel_id=1, source_target_pairs={{0,2},{1,3},{2,0},{3,1},{4,6},{5,7},{6,4},{7,5},{8,10},{9,11},{10,... | collective-permute-start | bytes 3538952 | tf_op jit(solution)/shard_map/ppermute | solution.py:26
  47.8 38.1 %collective-permute-start.4 = (bf16[96,6144]{1,0:T(8,128)(2,1)}, bf16[96,6144]{1,0:T(8,128)(2,1)S(1)}, u32[]{:S(2)}, u32[]{:S(2)}) collective-permute-start(bf16[96,6144]{1,0:T(8,128)(2,1)} %pad_maximum_fusion.4.refs_0_), channel_id=1, source_target_pairs={{0,4},{1,5},{2,6},{3,7},{4,0},{5,1},{6,2},{7,3},{8,12},{9,13},{10,... | collective-permute-start | bytes 3538952 | tf_op jit(solution)/shard_map/ppermute | solution.py:26
  86.8 16.8 %collective-permute-start.6 = (bf16[48,6144]{1,0:T(8,128)(2,1)}, bf16[48,6144]{1,0:T(8,128)(2,1)}, u32[]{:S(2)}, u32[]{:S(2)}) collective-permute-start(bf16[48,6144]{1,0:T(8,128)(2,1)} %slice.39), channel_id=1, source_target_pairs={{0,4},{1,5},{2,6},{3,7},{4,0},{5,1},{6,2},{7,3},{8,12},{9,13},{10,... | collective-permute-start | bytes 1769480 | tf_op jit(solution)/shard_map/ppermute | solution.py:26
  89.1 14.5 %collective-permute-start.7 = (bf16[48,6144]{1,0:T(8,128)(2,1)}, bf16[48,6144]{1,0:T(8,128)(2,1)}, u32[]{:S(2)}, u32[]{:S(2)}) collective-permute-start(bf16[48,6144]{1,0:T(8,128)(2,1)} %slice.40), channel_id=1, source_target_pairs={{0,2},{1,3},{2,0},{3,1},{4,6},{5,7},{6,4},{7,5},{8,10},{9,11},{10,... | collective-permute-start | bytes 1769480 | tf_op jit(solution)/shard_map/ppermute | solution.py:26
  92.8 14.4 %collective-permute-start.8 = (bf16[96,6144]{1,0:T(8,128)(2,1)}, bf16[96,6144]{1,0:T(8,128)(2,1)S(1)}, u32[]{:S(2)}, u32[]{:S(2)}) collective-permute-start(bf16[96,6144]{1,0:T(8,128)(2,1)} %pad_maximum_fusion.4.refs_0_), channel_id=1, source_target_pairs={{0,1},{1,0},{2,3},{3,2},{4,5},{5,4},{6,7},{7,6},{8,9},{9,8},{10,11... | collective-permute-start | bytes 3538952 | tf_op jit(solution)/shard_map/ppermute | solution.py:26
  92.9 14.6 %collective-permute-start.9 = (bf16[96,6144]{1,0:T(8,128)(2,1)S(1)}, bf16[96,6144]{1,0:T(8,128)(2,1)}, u32[]{:S(2)}, u32[]{:S(2)}) collective-permute-start(bf16[96,6144]{1,0:T(8,128)(2,1)S(1)} %collective-permute-done.3.refs_1_), channel_id=1, source_target_pairs={{0,1},{1,0},{2,3},{3,2},{4,5},{5,4},{6,7},{7,6},{8,9},{9,8},{10,11... | collective-permute-start | bytes 3538952 | tf_op jit(solution)/shard_map/ppermute | solution.py:26
  107.1 17.2 %collective-permute-start.13 = (bf16[2,40,1024]{2,1,0:T(8,128)(2,1)S(1)}, bf16[2,40,1024]{2,1,0:T(8,128)(2,1)S(1)}, u32[]{:S(2)}, u32[]{:S(2)}) collective-permute-start(bf16[2,40,1024]{2,1,0:T(8,128)(2,1)S(1)} %maximum_bitcast_fusion), channel_id=1, source_target_pairs={{0,8},{1,9},{2,10},{3,11},{4,12},{5,13},{6,14},{7,15},{8,0},{9,1},... | collective-permute-start | bytes 491528 | tf_op jit(solution)/shard_map/ppermute | solution.py:26
  127.2 20.6 %all-to-all-start = ((bf16[40,32,96]{2,0,1:T(8,128)(2,1)}), bf16[40,32,96]{2,0,1:T(8,128)(2,1)S(1)}, u32[]{:S(2)}, u32[]{:S(2)}) async-start(bf16[40,32,96]{2,0,1:T(8,128)(2,1)} %copy.53), calls=%async_computation | async-start | bytes 655360 | tf_op jit(solution)/shard_map/all_to_all | solution.py:1035
  130.4 17.4 %collective-permute-start.14 = (bf16[4,40,1024]{2,1,0:T(8,128)(2,1)S(1)}, bf16[4,40,1024]{2,1,0:T(8,128)(2,1)S(1)}, u32[]{:S(2)}, u32[]{:S(2)}) collective-permute-start(bf16[4,40,1024]{2,1,0:T(8,128)(2,1)S(1)} %bitcast.74), channel_id=1, source_target_pairs={{0,4},{1,5},{2,6},{3,7},{4,0},{5,1},{6,2},{7,3},{8,12},{9,13},{10,... | collective-permute-start | bytes 983048 | tf_op jit(solution)/shard_map/ppermute | solution.py:26
  149.4 26.0 %all-to-all-start.1 = ((bf16[32,8,768]{2,1,0:T(8,128)(2,1)}), bf16[32,8,768]{2,1,0:T(8,128)(2,1)S(1)}, u32[]{:S(2)}, u32[]{:S(2)}) async-start(bf16[32,8,768]{2,1,0:T(8,128)(2,1)} %broadcast_in_dim.60), calls=%async_computation.1 | async-start | bytes 786432 | tf_op jit(solution)/shard_map/all_to_all | solution.py:44
  154.5 20.9 %collective-permute-start.15 = (bf16[8,40,1024]{2,1,0:T(8,128)(2,1)S(1)}, bf16[8,40,1024]{2,1,0:T(8,128)(2,1)S(1)}, u32[]{:S(2)}, u32[]{:S(2)}) collective-permute-start(bf16[8,40,1024]{2,1,0:T(8,128)(2,1)S(1)} %bitcast.72), channel_id=1, source_target_pairs={{0,2},{1,3},{2,0},{3,1},{4,6},{5,7},{6,4},{7,5},{8,10},{9,11},{10,... | collective-permute-start | bytes 1966088 | tf_op jit(solution)/shard_map/ppermute | solution.py:26
  233.2 16.0 %collective-permute-start.19 = (bf16[192,1536]{1,0:T(8,128)(2,1)}, bf16[192,1536]{1,0:T(8,128)(2,1)S(1)}, u32[]{:S(2)}, u32[]{:S(2)}) collective-permute-start(bf16[192,1536]{1,0:T(8,128)(2,1)} %get-tuple-element.133.refs_1_), channel_id=1, source_target_pairs={{0,2},{1,3},{2,0},{3,1},{4,6},{5,7},{6,4},{7,5},{8,10},{9,11},{10,... | collective-permute-start | bytes 1769480 | tf_op jit(solution)/shard_map/ppermute | solution.py:26
  234.0 15.6 %collective-permute-start.20 = (bf16[192,1536]{1,0:T(8,128)(2,1)}, bf16[192,1536]{1,0:T(8,128)(2,1)S(1)}, u32[]{:S(2)}, u32[]{:S(2)}) collective-permute-start(bf16[192,1536]{1,0:T(8,128)(2,1)} %get-tuple-element.135.refs_3_), channel_id=1, source_target_pairs={{0,4},{1,5},{2,6},{3,7},{4,0},{5,1},{6,2},{7,3},{8,12},{9,13},{10,... | collective-permute-start | bytes 1769480 | tf_op jit(solution)/shard_map/ppermute | solution.py:26
  280.9 17.7 %collective-permute-start.28 = (bf16[192,1536]{1,0:T(8,128)(2,1)}, bf16[192,1536]{1,0:T(8,128)(2,1)S(1)}, u32[]{:S(2)}, u32[]{:S(2)}) collective-permute-start(bf16[192,1536]{1,0:T(8,128)(2,1)} %get-tuple-element.160), channel_id=1, source_target_pairs={{0,2},{1,3},{2,0},{3,1},{4,6},{5,7},{6,4},{7,5},{8,10},{9,11},{10,... | collective-permute-start | bytes 1769480 | tf_op jit(solution)/shard_map/ppermute | solution.py:26
  281.6 17.0 %collective-permute-start.29 = (bf16[192,1536]{1,0:T(8,128)(2,1)}, bf16[192,1536]{1,0:T(8,128)(2,1)S(1)}, u32[]{:S(2)}, u32[]{:S(2)}) collective-permute-start(bf16[192,1536]{1,0:T(8,128)(2,1)} %get-tuple-element.162), channel_id=1, source_target_pairs={{0,4},{1,5},{2,6},{3,7},{4,0},{5,1},{6,2},{7,3},{8,12},{9,13},{10,... | collective-permute-start | bytes 1769480 | tf_op jit(solution)/shard_map/ppermute | solution.py:26
  282.5 14.8 %collective-permute-start.25 = (bf16[24,3072]{1,0:T(8,128)(2,1)S(1)}, bf16[24,3072]{1,0:T(8,128)(2,1)S(1)}, u32[]{:S(2)}, u32[]{:S(2)}) collective-permute-start(bf16[24,3072]{1,0:T(8,128)(2,1)S(1)} %copy-done.36), channel_id=1, source_target_pairs={{0,8},{1,9},{2,10},{3,11},{4,12},{5,13},{6,14},{7,15},{8,0},{9,1},... | collective-permute-start | bytes 442376 | tf_op jit(solution)/shard_map/ppermute | solution.py:26
  283.9 13.9 %collective-permute-start.26 = (bf16[24,3072]{1,0:T(8,128)(2,1)S(1)}, bf16[24,3072]{1,0:T(8,128)(2,1)S(1)}, u32[]{:S(2)}, u32[]{:S(2)}) collective-permute-start(bf16[24,3072]{1,0:T(8,128)(2,1)S(1)} %copy-done.35), channel_id=1, source_target_pairs={{0,16},{1,17},{2,18},{3,19},{4,20},{5,21},{6,22},{7,23},{8,24},{9,... | collective-permute-start | bytes 442376 | tf_op jit(solution)/shard_map/ppermute | solution.py:26
  303.1 15.1 %collective-permute-start.30 = (bf16[96,1536]{1,0:T(8,128)(2,1)}, bf16[96,1536]{1,0:T(8,128)(2,1)S(1)}, u32[]{:S(2)}, u32[]{:S(2)}) collective-permute-start(bf16[96,1536]{1,0:T(8,128)(2,1)} %get-tuple-element.169.refs_1_), channel_id=1, source_target_pairs={{0,4},{1,5},{2,6},{3,7},{4,0},{5,1},{6,2},{7,3},{8,12},{9,13},{10,... | collective-permute-start | bytes 884744 | tf_op jit(solution)/shard_map/ppermute | solution.py:26
  304.2 13.9 %collective-permute-start.31 = (bf16[96,1536]{1,0:T(8,128)(2,1)}, bf16[96,1536]{1,0:T(8,128)(2,1)S(1)}, u32[]{:S(2)}, u32[]{:S(2)}) collective-permute-start(bf16[96,1536]{1,0:T(8,128)(2,1)} %get-tuple-element.171.refs_3_), channel_id=1, source_target_pairs={{0,2},{1,3},{2,0},{3,1},{4,6},{5,7},{6,4},{7,5},{8,10},{9,11},{10,... | collective-permute-start | bytes 884744 | tf_op jit(solution)/shard_map/ppermute | solution.py:26
  306.4 33.5 %all-to-all-start.2 = ((f32[32,1,4,768]{3,2,1,0:T(4,128)}), f32[32,1,4,768]{3,2,1,0:T(4,128)S(1)}, u32[]{:S(2)}, u32[]{:S(2)}) async-start(f32[32,1,4,768]{3,2,1,0:T(4,128)} %broadcast_in_dim.61), calls=%async_computation.2 | async-start | bytes 786432 | tf_op jit(solution)/shard_map/all_to_all | solution.py:44
  (56 other events, 491.4 us)
Sparse Core Ops, SparseCore 0:
  11.5 81.7 all-gather.1

commit v3 on v1

--- a/solution.py
+++ b/solution.py
@@ -31,11 +31,13 @@
     return [1 << k for k in range(peers.bit_length() - 1)]
 
 
-def joined(held, other, mask):
+def joined(held, other, mask, outer=None):
     upper = (lax.axis_index(AXIS) & mask) > 0
     first = jnp.where(upper, other, held)
     second = jnp.where(upper, held, other)
-    return jnp.stack([first, second], axis=1).reshape((-1,) + held.shape[1:])
+    outer = held.shape[0] if outer is None else outer
+    parts = [part.reshape((outer, -1) + held.shape[1:]) for part in (first, second)]
+    return jnp.stack(parts, axis=1).reshape((-1,) + held.shape[1:])
 
 
 def spread(block):
@@ -71,10 +73,9 @@
     return jnp.concatenate([shard] + [swapped(shard, mask) for mask in (8, 16, 24)], axis=0)
 
 
-def gathered_rows(line, beside, above):
-    half = line.shape[0] // 2
-    pieces = [line, beside, above, swapped(beside[:half], 4), swapped(above[half:], 2)]
-    return pieces + [swapped(piece, 1) for piece in pieces]
+def diagonal(beside, above):
+    half = beside.shape[0] // 2
+    return swapped(beside[:half], 4), swapped(above[half:], 2)
 
 
 def in_turn(first, then):
@@ -347,14 +348,14 @@
     for copy in copies:
         copy.start()
 
-    def place_columns(src):
+    def place_columns(src, dst):
         @pl.loop(0, D // 256)
         def _(step):
             at = pl.ds(pl.multiple_of(step * 256, 256), 256)
-            placed_ref[:, at] = mul_bt(src[...], perm_ref[at, :]).astype(bf16)
+            dst[:, at] = mul_bt(src[...], perm_ref[at, :]).astype(bf16)
 
     norm_rows(x_ref, h1_ref, g1_ref[...].astype(f32), b1_ref[...].astype(f32), chunk)
-    place_columns(h1_ref)
+    place_columns(h1_ref, placed_ref)
     for copy in copies:
         copy.wait()
 
@@ -367,7 +368,7 @@
         one = same_sequence(count, row0, keys, key0, IMG_LEN)
         mask = jnp.concatenate([one, one], axis=0)
         attend_along(qkv_ref, att_ref, pl.ds(row0, count), pl.ds(key0, keys), mask)
-    place_columns(att_ref)
+    place_columns(att_ref, placed_ref)
 
     @pl.loop(0, D // 256)
     def _(step):
@@ -984,7 +985,6 @@
         normed2, txt_up, txt_down, middle_sum, (line,)
     )
     text_unit, (beside, above) = in_turn(text_unit, (beside, above))
-    pieces = gathered_rows(line, beside, above) if small else [line]
 
     ends_at = jnp.cumsum(counts)
     slot_ids = lax.iota(jnp.int32, cap_local)
@@ -994,29 +994,41 @@
     columns = lax.iota(jnp.int32, total_images)
     positive = ((matches > 0) | (owner[:, None] == columns[None, :])) & live[:, None]
 
-    own_pack = packed(text_unit, positive.astype(bf16), pieces[1:5] if small else ())
+    own_pack = packed(text_unit, positive.astype(bf16), ())
+    pieces = [line]
+    if small:
+        held = own_pack[None]
+        first, second = diagonal(beside, above)
+        other, first, second = lax.optimization_barrier((swapped(held, 16), first, second))
+        held = joined(held, other, 16)
+        pieces = [line, beside, above, first, second]
+        pieces = pieces + [swapped(piece, 1) for piece in pieces]
 
     normed_img, middle_img = image_front(
         images, pieces, perm, img_gain1, img_bias1, img_gain2, img_bias2
     )
     if small:
-        held = own_pack[None]
         scaled_sum = (hidden_sum * inverse[:, :1]).astype(bf16)
         normed_img, scaled_sum, other = lax.optimization_barrier(
-            (normed_img, scaled_sum, swapped(held, 16))
+            (normed_img, scaled_sum, swapped(held, 8))
         )
-        held = joined(held, other, 16)
+        held = joined(held, other, 8)
         hidden_cols = lax.all_to_all(scaled_sum, AXIS, split_axis=1, concat_axis=0, tiled=True)
-        whole, other = in_turn(whole, swapped(held, 8))
-        held = joined(held, other, 8)
-        other = swapped(held, 4)
+        beside, above = swapped(held, 2), swapped(held, 4)
+        whole, beside, above = lax.optimization_barrier((whole, beside, above))
+        first, second = diagonal(beside, above)
     image_low = image_up(normed_img, whole, 0, FF, middle_img)
     if small:
-        image_low, other, hidden_cols = lax.optimization_barrier((image_low, other, hidden_cols))
-        held = joined(held, other, 4)
-        held = joined(held, swapped(held, 2), 2)
-        text_pack = joined(held, swapped(held, 1), 1).reshape(-1, D + total_images)
+        image_low, first, second, hidden_cols = lax.optimization_barrier(
+            (image_low, first, second, hidden_cols)
+        )
+        across = jnp.concatenate([first, second], axis=0)
+        held = joined(joined(held, beside, 2), joined(above, across, 2), 4, 4)
+        other = swapped(held, 1)
     image_all = spread(image_low).reshape(total_images, D)
+    if small:
+        image_all, other = in_turn(image_all, other)
+        text_pack = joined(held, other, 1).reshape(-1, D + total_images)
 
     order_a, order_b, tail = stage_orders()
     matrix_a, matrix_b = row_order(order_a + tail[::-1]), row_order(order_b + tail[::-1])

time: 323 us -> 323 us (level); the launches traced: 322 us -> 318 us
  waiting for transfers between devices: 57.6 us -> 42.5 us
  Pallas kernels: 153 us -> 161 us
  starting transfers between devices: 46.4 us -> 52.4 us
    ppermute x35 -> x37, waiting for transfers between devices: 48.6 us -> 34.5 us  [swapped(): return lax.ppermute(value, AXIS, [(i, i ^ mask) for i in range(peers)])]
    pallas_call x4, Pallas kernels: 16.1 us -> 25 us  [fold(): pl.pallas_call(fold_kernel, grid=(cols // tile,), out_shape=[jax.ShapeDty...]
    all_gather x1, waiting for transfers between devices: 4.52 us -> 0.01 us  [local(): lax.all_gather(jnp.concatenate([img_up.reshape(per, FF), img_down.reshape...]
    all_to_all x2, starting transfers between devices: 6.35 us -> 10.1 us  [spread(): return lax.all_to_all(copies, AXIS, split_axis=0, concat_axis=0, tiled=True)]
    all_to_all x2, waiting for transfers between devices: 4.54 us -> 7.98 us  [spread(): return lax.all_to_all(copies, AXIS, split_axis=0, concat_axis=0, tiled=True)]
    ppermute x35 -> x37, starting transfers between devices: 37.2 us -> 38 us  [swapped(): return lax.ppermute(value, AXIS, [(i, i ^ mask) for i in range(peers)])]
    unnamed x96 -> x95, local copies, waits for them, and re-layouts: 12 us -> 11.2 us
  transfers between devices with their start and end apart: 39 -> 41, of which waited for: 12 -> 12; matrix products, arithmetic and copies ran while one was open for 11% -> 9% of each run, Pallas kernels for 34% -> 35%
where the time goes in v3:
time: 323 us; the launch traced here: 318 us
  Pallas kernels  161 us (50%)
  starting transfers between devices  52.4 us (16%)
  waiting for transfers between devices  42.5 us (13%)
  local copies, waits for them, and re-layouts  29.6 us (9%)
  between operations  15 us (5%)
  other arithmetic  10.3 us (3%)
  matrix products  7.25 us (2%)
    ppermute x37, starting transfers between devices, swapped(): return lax.ppermute(value, AXIS, [(i, i ^ mask) for i in range(peers)])  38 us
    ppermute x37, waiting for transfers between devices, swapped(): return lax.ppermute(value, AXIS, [(i, i ^ mask) for i in range(peers)])  34.5 us
    pallas_call x4, Pallas kernels, fold(): pl.pallas_call(fold_kernel, grid=(cols // tile,), out_shape=[jax.ShapeDty...  25 us
    pallas_call x1, Pallas kernels, mlp_back(): pl.pallas_call(mlp_back_kernel, grid=(steps,), out_shape=[part] * 4 + [ja...  21.5 us
    pallas_call x1, Pallas kernels, text_front(): pl.pallas_call(text_front_kernel, out_shape=[jax.ShapeDtypeStruct(*item)...  18.2 us
    pallas_call x2, Pallas kernels, attention_back(): pl.pallas_call(attention_back_kernel, grid=(count,), out_shape=[jax.Shape...  16.8 us
    pallas_call x1, Pallas kernels, image_up(): pl.pallas_call(functools.partial(image_up_kernel, fold), grid=(FF // TILE...  14.1 us
    pallas_call x1, Pallas kernels, image_front(): pl.pallas_call(functools.partial(image_front_kernel, windows), out_shape=...  13.8 us
  transfers between devices with their start and end apart: 41, of which 12 were waited for; matrix products, arithmetic and copies ran while one was open for 9% of the time, Pallas kernels for 35%

profile of v3, /device:TPU:0, one launch (start us, length us, event | category | flops | bytes accessed | tf_op | source)
XLA Modules:
  0.0 318.3 jit_solution(15118478436909090029)
XLA Ops:
  11.9 5.1 %collective-permute-start.2 = (bf16[24,3072]{1,0:T(8,128)(2,1)S(1)}, bf16[24,3072]{1,0:T(8,128)(2,1)S(1)}, u32[]{:S(2)}, u32[]{:S(2)}) collective-permute-start(bf16[24,3072]{1,0:T(8,128)(2,1)S(1)} %constant_dynamic-update-slice_fusion), channel_id=1, source_target_pairs={{0,24},{1,25},{2,26},{3,27},{4,28},{5,29},{6,30},{7,31},{8,16},{9,... | collective-permute-start | bytes 442376 | tf_op jit(solution)/shard_map/ppermute | solution.py:26
  21.6 18.2 %text_front.1 = (bf16[640,768]{1,0:T(8,128)(2,1)}, bf16[640,2304]{1,0:T(8,128)(2,1)}, bf16[640,768]{1,0:T(8,128)(2,1)}, f32[640,768]{1,0:T(8,128)}, bf16[640,768...) custom-call(bf16[640,768]{1,0:T(8,128)(2,1)} %refs_3_.1, f32[1,768]{1,0:T(1,128)} %broadcast_in_dim.26.g1_ref.refs_4_, ...), custom_call_target="tpu_custom_call" | custom-call | flops 3019898880 | bytes 11599872 | tf_op jit(solution)/shard_map/text_front/pallas_call | solution.py:329
  47.5 13.8 %text_up.1 = (bf16[640,3072]{1,0:T(8,128)(2,1)}, f32[40,3072]{1,0:T(8,128)}, f32[40,768]{1,0:T(8,128)}, f32[40,128]{1,0:T(8,128)}) custom-call(bf16[640,768]{1,0:T(8,128)(2,1)} %get-tuple-element.103.h2_ref, bf16[768,3072]{1,0:T(8,128)(2,1)} %wu_ref.3, bf16[3072,768]{1,0:T(8,128)(2,1)} %wd_ref.3, f32[40,768]{1,0:T(8,128)} %get-tuple-element.104.sum_ref, ...), custom_call_target="tpu_custom_call" | custom-call | flops 3019898880 | bytes 13369344 | tf_op jit(solution)/shard_map/text_up/pallas_call | solution.py:488
  74.7 9.3 %collective-permute-done.6.refs_3_ = bf16[48,3072]{1,0:T(8,128)(2,1)S(1)} collective-permute-done((bf16[48,3072]{1,0:T(8,128)(2,1)S(1)}, bf16[48,3072]{1,0:T(8,128)(2,1)S(1)}, u32[]{:S(2)}, u32[]{:S(2)}) %collective-permute-start.6) | collective-permute-done | bytes 294944 | tf_op jit(solution)/shard_map/ppermute | solution.py:26
  90.9 13.8 %image_front.1 = (bf16[400,768]{1,0:T(8,128)(2,1)}, f32[8,768]{1,0:T(8,128)}) custom-call(bf16[400,768]{1,0:T(8,128)(2,1)} %x_ref.3, bf16[768,768]{1,0:T(8,128)(2,1)} %fusion.5.perm_ref, bf16[1,768]{1,0:T(2,128)(2,1)} %broadcast_in_dim.22.g1_ref, bf16[1,768]{1,0:T(2,128)(2,1)} %broadcast_in_dim.23.b1_ref, bf16[1,768]{1,0:T(2,128)(2,1)} %broadcast_in_dim.24.g2_ref, ...), custom_call_target="tpu_custom_call" | custom-call | flops 2831155200 | bytes 4718592 | tf_op jit(solution)/shard_map/image_front/pallas_call | solution.py:393
  108.2 4.3 %all-to-all-start = ((bf16[40,32,96]{2,0,1:T(8,128)(2,1)}), bf16[40,32,96]{2,0,1:T(8,128)(2,1)S(1)}, u32[]{:S(2)}, u32[]{:S(2)}) async-start(bf16[40,32,96]{2,0,1:T(8,128)(2,1)} %copy.60), calls=%async_computation | async-start | bytes 655360 | tf_op jit(solution)/shard_map/all_to_all | solution.py:1016
  117.0 14.1 %image_up.1 = bf16[8,768]{1,0:T(8,128)(2,1)} custom-call(bf16[400,768]{1,0:T(8,128)(2,1)} %get-tuple-element.115.h2_ref, bf16[768,6144]{1,0:T(8,128)(2,1)} %all-gather.2.cloned.1.call-done.wu_ref.wd_ref, bf16[768,6144]{1,0:T(8,128)(2,1)} %all-gather.2.cloned.1.call-done.wu_ref.wd_ref, f32[8,768]{1,0:T(8,128)} %get-tuple-element.118.sum_ref), custom_call_target="tpu_custom_call" | custom-call | flops 1887436800 | bytes 9437184 | tf_op jit(solution)/shard_map/image_up/pallas_call | solution.py:555
  133.5 6.8 %all-to-all-start.1 = ((bf16[32,8,768]{2,1,0:T(8,128)(2,1)}), bf16[32,8,768]{2,1,0:T(8,128)(2,1)S(1)}, u32[]{:S(2)}, u32[]{:S(2)}) async-start(bf16[32,8,768]{2,1,0:T(8,128)(2,1)} %broadcast_in_dim.60), calls=%async_computation.1 | async-start | bytes 786432 | tf_op jit(solution)/shard_map/all_to_all | solution.py:46
  145.5 8.0 %all-to-all-done.1 = bf16[32,8,768]{2,1,0:T(8,128)(2,1)S(1)} async-done(((bf16[32,8,768]{2,1,0:T(8,128)(2,1)}), bf16[32,8,768]{2,1,0:T(8,128)(2,1)S(1)}, u32[]{:S(2)}, u32[]{:S(2)}) %all-to-all-start.1) | async-done | bytes 393248 | tf_op jit(solution)/shard_map/all_to_all | solution.py:46
  156.3 4.0 %loss_and_rows.1 = (f32[1,128]{1,0:T(1,128)}, f32[40,768]{1,0:T(8,128)}, bf16[40,768]{1,0:T(8,128)(2,1)}, f32[1,256]{1,0:T(1,128)}, f32[1,256]{1,0:T(1,128)}, /*index=5*/f32[1,128]{1,0:T(1,128)}) custom-call(bf16[1280,1024]{1,0:T(8,128)(2,1)} %bitcast.80, bf16[256,768]{1,0:T(8,128)(2,1)} %bitcast.83, bf16[40,1024]{1,0:T(8,128)(2,1)} %packed.1.own_ref, ...), custom_call_target="tpu_custom_call" | custom-call | flops 503316480 | bytes 2621440 | tf_op jit(solution)/shard_map/loss_and_rows/pallas_call | solution.py:645
  160.4 21.5 %mlp_back.1 = (bf16[384,1536]{1,0:T(8,128)(2,1)}, bf16[384,1536]{1,0:T(8,128)(2,1)}, bf16[384,1536]{1,0:T(8,128)(2,1)}, bf16[384,1536]{1,0:T(8,128)(2,1)}, f32[6...) custom-call(bf16[40,768]{1,0:T(8,128)(2,1)} %get-tuple-element.128.low_ref, bf16[3072,768]{1,0:T(8,128)(2,1)} %wd_ref.3, ...), custom_call_target="tpu_custom_call" | custom-call | flops 6039797760 | bytes 18087936 | tf_op jit(solution)/shard_map/mlp_back/pallas_call | solution.py:754
  183.7 7.2 %attention_back.2 = (bf16[256,768]{1,0:T(8,128)(2,1)}, bf16[256,2304]{1,0:T(8,128)(2,1)}) custom-call(f32[640,768]{1,0:T(8,128)} %get-tuple-element.132.grad_ref.refs_5_, bf16[768,768]{1,0:T(8,128)(2,1)} %wo_ref.5, bf16[640,2304]{1,0:T(8,128)(2,1)} %get-tuple-element.133.qkv_ref, f32[80,128]{1,0:T(8,128)} %get-tuple-element.134.lse_ref), custom_call_target="tpu_custom_call" | custom-call | flops 1509949440 | bytes 4325376 | tf_op jit(solution)/shard_map/attention_back/pallas_call | solution.py:809
  192.4 13.5 %fold.4 = (bf16[192,1536]{1,0:T(8,128)(2,1)}, bf16[192,1536]{1,0:T(8,128)(2,1)}, bf16[192,1536]{1,0:T(8,128)(2,1)}, bf16[192,1536]{1,0:T(8,128)(2,1)}) custom-call(bf16[384,1536]{1,0:T(8,128)(2,1)} %get-tuple-element.136.keep_a, bf16[384,1536]{1,0:T(8,128)(2,1)} %copy-done.5, bf16[384,1536]{1,0:T(8,128)(2,1)} %get-tuple-element.138.keep_b, ...), custom_call_target="tpu_custom_call" | custom-call | flops 1179648 | bytes 7077888 | tf_op jit(solution)/shard_map/fold/pallas_call | solution.py:195
  210.3 9.6 %attention_back.3 = (bf16[384,768]{1,0:T(8,128)(2,1)}, bf16[384,2304]{1,0:T(8,128)(2,1)}) custom-call(f32[640,768]{1,0:T(8,128)} %get-tuple-element.132.grad_ref.refs_5_, bf16[768,768]{1,0:T(8,128)(2,1)} %wo_ref.5, bf16[640,2304]{1,0:T(8,128)(2,1)} %get-tuple-element.133.qkv_ref, f32[80,128]{1,0:T(8,128)} %get-tuple-element.134.lse_ref, ...), custom_call_target="tpu_custom_call" | custom-call | flops 2264924160 | bytes 5898240 | tf_op jit(solution)/shard_map/attention_back/pallas_call | solution.py:809
  222.9 3.5 %fold.5 = (bf16[96,1536]{1,0:T(8,128)(2,1)}, bf16[96,1536]{1,0:T(8,128)(2,1)}, bf16[96,1536]{1,0:T(8,128)(2,1)}, bf16[96,1536]{1,0:T(8,128)(2,1)}) custom-call(bf16[192,1536]{1,0:T(8,128)(2,1)} %get-tuple-element.140.refs_0_.keep_a, bf16[192,1536]{1,0:T(8,128)(2,1)} %copy-done.12, bf16[192,1536]{1,0:T(8,128)(2,1)} %get-tuple-element.142.refs_2_.keep_b, ...), custom_call_target="tpu_custom_call" | custom-call | flops 589824 | bytes 3538944 | tf_op jit(solution)/shard_map/fold/pallas_call | solution.py:195
  230.4 4.7 %weight_back.2 = (bf16[384,1536]{1,0:T(8,128)(2,1)}, bf16[384,1536]{1,0:T(8,128)(2,1)}) custom-call(bf16[3,768,640]{2,1,0:T(8,128)(2,1)} %pad_maximum_fusion.lhs_ref, bf16[256,2304]{1,0:T(8,128)(2,1)} %get-tuple-element.135.refs_0_, bf16[384,2304]{1,0:T(8,128)(2,1)} %get-tuple-element.144.refs_0_.refs_1_, ...), custom_call_target="tpu_custom_call" | custom-call | flops 1509949440 | bytes 6094848 | tf_op jit(solution)/shard_map/weight_back/pallas_call | solution.py:861
  238.7 5.0 %weight_back.3 = (bf16[384,1536]{1,0:T(8,128)(2,1)}, bf16[384,1536]{1,0:T(8,128)(2,1)}) custom-call(bf16[3,768,640]{2,1,0:T(8,128)(2,1)} %pad_maximum_fusion.lhs_ref, bf16[256,2304]{1,0:T(8,128)(2,1)} %get-tuple-element.135.refs_0_, bf16[384,2304]{1,0:T(8,128)(2,1)} %get-tuple-element.144.refs_0_.refs_1_, bf16[256,768]{1,0:T(8,128)(2,1)} %get-tuple-element.153.refs_2_, ...), custom_call_target="tpu_custom_call" | custom-call | flops 1509949440 | bytes 6094848 | tf_op jit(solution)/shard_map/weight_back/pallas_call | solution.py:861
  248.0 4.6 %fold.6 = (bf16[192,1536]{1,0:T(8,128)(2,1)}, bf16[192,1536]{1,0:T(8,128)(2,1)}, bf16[192,1536]{1,0:T(8,128)(2,1)}, bf16[192,1536]{1,0:T(8,128)(2,1)}) custom-call(bf16[384,1536]{1,0:T(8,128)(2,1)} %get-tuple-element.151.keep_a, bf16[384,1536]{1,0:T(8,128)(2,1)} %copy-done.4, bf16[384,1536]{1,0:T(8,128)(2,1)} %get-tuple-element.156.keep_b, ...), custom_call_target="tpu_custom_call" | custom-call | flops 1179648 | bytes 7077888 | tf_op jit(solution)/shard_map/fold/pallas_call | solution.py:195
  258.9 10.4 %input_back.1 = (f32[640,768]{1,0:T(8,128)}, f32[1,768]{1,0:T(1,128)}, f32[1,768]{1,0:T(1,128)}) custom-call(bf16[256,2304]{1,0:T(8,128)(2,1)} %get-tuple-element.135.refs_0_, bf16[384,2304]{1,0:T(8,128)(2,1)} %get-tuple-element.144.refs_0_.refs_1_, bf16[768,2304]{1,0:T(8,128)(2,1)} %refs_2_.1, bf16[640,768]{1,0:T(8,128)(2,1)} %refs_3_.1, ...), custom_call_target="tpu_custom_call" | custom-call | flops 2264924160 | bytes 10420224 | tf_op jit(solution)/shard_map/input_back/pallas_call | solution.py:919
  271.1 3.5 %fold.7 = (bf16[96,1536]{1,0:T(8,128)(2,1)}, bf16[96,1536]{1,0:T(8,128)(2,1)}, bf16[96,1536]{1,0:T(8,128)(2,1)}, bf16[96,1536]{1,0:T(8,128)(2,1)}) custom-call(bf16[192,1536]{1,0:T(8,128)(2,1)} %get-tuple-element.158.refs_6_.keep_a, bf16[192,1536]{1,0:T(8,128)(2,1)} %copy-done.10, bf16[192,1536]{1,0:T(8,128)(2,1)} %get-tuple-element.169.keep_b, ...), custom_call_target="tpu_custom_call" | custom-call | flops 589824 | bytes 3538944 | tf_op jit(solution)/shard_map/fold/pallas_call | solution.py:195
  277.6 3.2 %all-to-all-start.2 = ((f32[32,1,4,768]{3,2,1,0:T(4,128)}), f32[32,1,4,768]{3,2,1,0:T(4,128)S(1)}, u32[]{:S(2)}, u32[]{:S(2)}) async-start(f32[32,1,4,768]{3,2,1,0:T(4,128)} %broadcast_in_dim.61), calls=%async_computation.2 | async-start | bytes 786432 | tf_op jit(solution)/shard_map/all_to_all | solution.py:46
  280.8 7.9 %grad_of_down.1.refs_0_ = f32[96,768]{1,0:T(8,128)} custom-call(bf16[1280,1024]{1,0:T(8,128)(2,1)} %bitcast.81, bf16[256,768]{1,0:T(8,128)(2,1)} %bitcast.84, f32[1,256]{1,0:T(1,128)} %get-tuple-element.180.col_sum_ref, f32[1,256]{1,0:T(1,128)} %get-tuple-element.181.col_count_ref, f32[1,128]{1,0:T(1,128)} %get-tuple-element.182.live_ref, ...), custom_call_target="tpu_custom_call" | custom-call | flops 1006632960 | bytes 2621440 | tf_op jit(solution)/shard_map/grad_of_down/pallas_call | solution.py:677
  292.3 3.6 %collective-permute-start.36 = (bf16[24,3072]{1,0:T(8,128)(2,1)}, bf16[24,3072]{1,0:T(8,128)(2,1)S(1)}, u32[]{:S(2)}, u32[]{:S(2)}) collective-permute-start(bf16[24,3072]{1,0:T(8,128)(2,1)} %get-tuple-element.187), channel_id=1, source_target_pairs={{0,24},{1,25},{2,26},{3,27},{4,28},{5,29},{6,30},{7,31},{8,16},{9,... | collective-permute-start | bytes 442376 | tf_op jit(solution)/shard_map/ppermute | solution.py:26
  301.1 8.0 %collective-permute-done.35 = bf16[24,3072]{1,0:T(8,128)(2,1)S(1)} collective-permute-done((bf16[24,3072]{1,0:T(8,128)(2,1)}, bf16[24,3072]{1,0:T(8,128)(2,1)S(1)}, u32[]{:S(2)}, u32[]{:S(2)}) %collective-permute-start.35) | collective-permute-done | bytes 147488 | tf_op jit(solution)/shard_map/ppermute | solution.py:26
  (239 shorter events, 99.7 us)
Async XLA Ops:
  7.2 109.0 %all-gather.2.cloned.1.call-start = ((), (), s32[]{:S(2)}) async-start(), calls=%async_computation.3 | async-start | bytes 9732096 | tf_op jit(solution)/shard_map/all_gather | solution.py:966
  11.9 28.6 %collective-permute-start.2 = (bf16[24,3072]{1,0:T(8,128)(2,1)S(1)}, bf16[24,3072]{1,0:T(8,128)(2,1)S(1)}, u32[]{:S(2)}, u32[]{:S(2)}) collective-permute-start(bf16[24,3072]{1,0:T(8,128)(2,1)S(1)} %constant_dynamic-update-slice_fusion), channel_id=1, source_target_pairs={{0,24},{1,25},{2,26},{3,27},{4,28},{5,29},{6,30},{7,31},{8,16},{9,... | collective-permute-start | bytes 442376 | tf_op jit(solution)/shard_map/ppermute | solution.py:26
  17.0 23.5 %collective-permute-start.1 = (bf16[24,3072]{1,0:T(8,128)(2,1)S(1)}, bf16[24,3072]{1,0:T(8,128)(2,1)S(1)}, u32[]{:S(2)}, u32[]{:S(2)}) collective-permute-start(bf16[24,3072]{1,0:T(8,128)(2,1)S(1)} %constant_dynamic-update-slice_fusion), channel_id=1, source_target_pairs={{0,16},{1,17},{2,18},{3,19},{4,20},{5,21},{6,22},{7,23},{8,24},{9,... | collective-permute-start | bytes 442376 | tf_op jit(solution)/shard_map/ppermute | solution.py:26
  17.0 23.5 %collective-permute-start = (bf16[24,3072]{1,0:T(8,128)(2,1)S(1)}, bf16[24,3072]{1,0:T(8,128)(2,1)S(1)}, u32[]{:S(2)}, u32[]{:S(2)}) collective-permute-start(bf16[24,3072]{1,0:T(8,128)(2,1)S(1)} %constant_dynamic-update-slice_fusion), channel_id=1, source_target_pairs={{0,8},{1,9},{2,10},{3,11},{4,12},{5,13},{6,14},{7,15},{8,0},{9,1},... | collective-permute-start | bytes 442376 | tf_op jit(solution)/shard_map/ppermute | solution.py:26
  40.6 23.1 %collective-permute-start.3 = (bf16[96,3072]{1,0:T(8,128)(2,1)S(1)}, bf16[96,3072]{1,0:T(8,128)(2,1)S(1)}, u32[]{:S(2)}, u32[]{:S(2)}) collective-permute-start(bf16[96,3072]{1,0:T(8,128)(2,1)S(1)} %pad_maximum_fusion.6.refs_0_), channel_id=1, source_target_pairs={{0,2},{1,3},{2,0},{3,1},{4,6},{5,7},{6,4},{7,5},{8,10},{9,11},{10,... | collective-permute-start | bytes 1769480 | tf_op jit(solution)/shard_map/ppermute | solution.py:26
  42.3 21.4 %collective-permute-start.4 = (bf16[96,3072]{1,0:T(8,128)(2,1)S(1)}, bf16[96,3072]{1,0:T(8,128)(2,1)}, u32[]{:S(2)}, u32[]{:S(2)}) collective-permute-start(bf16[96,3072]{1,0:T(8,128)(2,1)S(1)} %pad_maximum_fusion.6.refs_0_), channel_id=1, source_target_pairs={{0,4},{1,5},{2,6},{3,7},{4,0},{5,1},{6,2},{7,3},{8,12},{9,13},{10,... | collective-permute-start | bytes 1769480 | tf_op jit(solution)/shard_map/ppermute | solution.py:26
  47.5 39.7 %collective-permute-start.8 = (bf16[96,3072]{1,0:T(8,128)(2,1)S(1)}, bf16[96,3072]{1,0:T(8,128)(2,1)S(1)}, u32[]{:S(2)}, u32[]{:S(2)}) collective-permute-start(bf16[96,3072]{1,0:T(8,128)(2,1)S(1)} %pad_maximum_fusion.6.refs_0_), channel_id=1, source_target_pairs={{0,1},{1,0},{2,3},{3,2},{4,5},{5,4},{6,7},{7,6},{8,9},{9,8},{10,11... | collective-permute-start | bytes 1769480 | tf_op jit(solution)/shard_map/ppermute | solution.py:26
  68.4 20.6 %collective-permute-start.9 = (bf16[96,3072]{1,0:T(8,128)(2,1)S(1)}, bf16[96,3072]{1,0:T(8,128)(2,1)S(1)}, u32[]{:S(2)}, u32[]{:S(2)}) collective-permute-start(bf16[96,3072]{1,0:T(8,128)(2,1)S(1)} %collective-permute-done.3.refs_1_), channel_id=1, source_target_pairs={{0,1},{1,0},{2,3},{3,2},{4,5},{5,4},{6,7},{7,6},{8,9},{9,8},{10,11... | collective-permute-start | bytes 1769480 | tf_op jit(solution)/shard_map/ppermute | solution.py:26
  69.5 19.5 %collective-permute-start.10 = (bf16[96,3072]{1,0:T(8,128)(2,1)}, bf16[96,3072]{1,0:T(8,128)(2,1)S(1)}, u32[]{:S(2)}, u32[]{:S(2)}) collective-permute-start(bf16[96,3072]{1,0:T(8,128)(2,1)} %collective-permute-done.4.refs_2_), channel_id=1, source_target_pairs={{0,1},{1,0},{2,3},{3,2},{4,5},{5,4},{6,7},{7,6},{8,9},{9,8},{10,11... | collective-permute-start | bytes 1769480 | tf_op jit(solution)/shard_map/ppermute | solution.py:26
  72.2 14.4 %collective-permute-start.7 = (bf16[48,3072]{1,0:T(8,128)(2,1)S(1)}, bf16[48,3072]{1,0:T(8,128)(2,1)S(1)}, u32[]{:S(2)}, u32[]{:S(2)}) collective-permute-start(bf16[48,3072]{1,0:T(8,128)(2,1)S(1)} %slice.46), channel_id=1, source_target_pairs={{0,2},{1,3},{2,0},{3,1},{4,6},{5,7},{6,4},{7,5},{8,10},{9,11},{10,... | collective-permute-start | bytes 884744 | tf_op jit(solution)/shard_map/ppermute | solution.py:26
  87.2 17.6 %collective-permute-start.13 = (bf16[2,40,1024]{2,1,0:T(8,128)(2,1)S(1)}, bf16[2,40,1024]{2,1,0:T(8,128)(2,1)S(1)}, u32[]{:S(2)}, u32[]{:S(2)}) collective-permute-start(bf16[2,40,1024]{2,1,0:T(8,128)(2,1)S(1)} %maximum_bitcast_fusion), channel_id=1, source_target_pairs={{0,8},{1,9},{2,10},{3,11},{4,12},{5,13},{6,14},{7,15},{8,0},{9,1},... | collective-permute-start | bytes 491528 | tf_op jit(solution)/shard_map/ppermute | solution.py:26
  108.2 22.9 %all-to-all-start = ((bf16[40,32,96]{2,0,1:T(8,128)(2,1)}), bf16[40,32,96]{2,0,1:T(8,128)(2,1)S(1)}, u32[]{:S(2)}, u32[]{:S(2)}) async-start(bf16[40,32,96]{2,0,1:T(8,128)(2,1)} %copy.60), calls=%async_computation | async-start | bytes 655360 | tf_op jit(solution)/shard_map/all_to_all | solution.py:1016
  116.2 14.8 %collective-permute-start.16 = (bf16[2,40,1024]{2,1,0:T(8,128)(2,1)S(1)}, bf16[2,40,1024]{2,1,0:T(8,128)(2,1)S(1)}, u32[]{:S(2)}, u32[]{:S(2)}) collective-permute-start(bf16[2,40,1024]{2,1,0:T(8,128)(2,1)S(1)} %slice.48), channel_id=1, source_target_pairs={{0,4},{1,5},{2,6},{3,7},{4,0},{5,1},{6,2},{7,3},{8,12},{9,13},{10,... | collective-permute-start | bytes 491528 | tf_op jit(solution)/shard_map/ppermute | solution.py:26
  116.6 14.5 %collective-permute-start.17 = (bf16[2,40,1024]{2,1,0:T(8,128)(2,1)S(1)}, bf16[2,40,1024]{2,1,0:T(8,128)(2,1)S(1)}, u32[]{:S(2)}, u32[]{:S(2)}) collective-permute-start(bf16[2,40,1024]{2,1,0:T(8,128)(2,1)S(1)} %slice.49), channel_id=1, source_target_pairs={{0,2},{1,3},{2,0},{3,1},{4,6},{5,7},{6,4},{7,5},{8,10},{9,11},{10,... | collective-permute-start | bytes 491528 | tf_op jit(solution)/shard_map/ppermute | solution.py:26
  132.2 21.3 %collective-permute-start.18 = (bf16[16,40,1024]{2,1,0:T(8,128)(2,1)S(1)}, bf16[16,40,1024]{2,1,0:T(8,128)(2,1)S(1)}, u32[]{:S(2)}, u32[]{:S(2)}) collective-permute-start(bf16[16,40,1024]{2,1,0:T(8,128)(2,1)S(1)} %bitcast.82), channel_id=1, source_target_pairs={{0,1},{1,0},{2,3},{3,2},{4,5},{5,4},{6,7},{7,6},{8,9},{9,8},{10,11... | collective-permute-start | bytes 3932168 | tf_op jit(solution)/shard_map/ppermute | solution.py:26
  133.5 20.0 %all-to-all-start.1 = ((bf16[32,8,768]{2,1,0:T(8,128)(2,1)}), bf16[32,8,768]{2,1,0:T(8,128)(2,1)S(1)}, u32[]{:S(2)}, u32[]{:S(2)}) async-start(bf16[32,8,768]{2,1,0:T(8,128)(2,1)} %broadcast_in_dim.60), calls=%async_computation.1 | async-start | bytes 786432 | tf_op jit(solution)/shard_map/all_to_all | solution.py:46
  205.8 15.6 %collective-permute-start.21 = (bf16[192,1536]{1,0:T(8,128)(2,1)}, bf16[192,1536]{1,0:T(8,128)(2,1)S(1)}, u32[]{:S(2)}, u32[]{:S(2)}) collective-permute-start(bf16[192,1536]{1,0:T(8,128)(2,1)} %get-tuple-element.141.refs_1_), channel_id=1, source_target_pairs={{0,2},{1,3},{2,0},{3,1},{4,6},{5,7},{6,4},{7,5},{8,10},{9,11},{10,... | collective-permute-start | bytes 1769480 | tf_op jit(solution)/shard_map/ppermute | solution.py:26
  206.4 15.6 %collective-permute-start.22 = (bf16[192,1536]{1,0:T(8,128)(2,1)}, bf16[192,1536]{1,0:T(8,128)(2,1)S(1)}, u32[]{:S(2)}, u32[]{:S(2)}) collective-permute-start(bf16[192,1536]{1,0:T(8,128)(2,1)} %get-tuple-element.143.refs_3_), channel_id=1, source_target_pairs={{0,4},{1,5},{2,6},{3,7},{4,0},{5,1},{6,2},{7,3},{8,12},{9,13},{10,... | collective-permute-start | bytes 1769480 | tf_op jit(solution)/shard_map/ppermute | solution.py:26
  252.6 17.5 %collective-permute-start.30 = (bf16[192,1536]{1,0:T(8,128)(2,1)}, bf16[192,1536]{1,0:T(8,128)(2,1)S(1)}, u32[]{:S(2)}, u32[]{:S(2)}) collective-permute-start(bf16[192,1536]{1,0:T(8,128)(2,1)} %get-tuple-element.168), channel_id=1, source_target_pairs={{0,2},{1,3},{2,0},{3,1},{4,6},{5,7},{6,4},{7,5},{8,10},{9,11},{10,... | collective-permute-start | bytes 1769480 | tf_op jit(solution)/shard_map/ppermute | solution.py:26
  253.6 16.5 %collective-permute-start.31 = (bf16[192,1536]{1,0:T(8,128)(2,1)}, bf16[192,1536]{1,0:T(8,128)(2,1)S(1)}, u32[]{:S(2)}, u32[]{:S(2)}) collective-permute-start(bf16[192,1536]{1,0:T(8,128)(2,1)} %get-tuple-element.170), channel_id=1, source_target_pairs={{0,4},{1,5},{2,6},{3,7},{4,0},{5,1},{6,2},{7,3},{8,12},{9,13},{10,... | collective-permute-start | bytes 1769480 | tf_op jit(solution)/shard_map/ppermute | solution.py:26
  254.6 14.8 %collective-permute-start.27 = (bf16[24,3072]{1,0:T(8,128)(2,1)S(1)}, bf16[24,3072]{1,0:T(8,128)(2,1)S(1)}, u32[]{:S(2)}, u32[]{:S(2)}) collective-permute-start(bf16[24,3072]{1,0:T(8,128)(2,1)S(1)} %copy-done.41), channel_id=1, source_target_pairs={{0,8},{1,9},{2,10},{3,11},{4,12},{5,13},{6,14},{7,15},{8,0},{9,1},... | collective-permute-start | bytes 442376 | tf_op jit(solution)/shard_map/ppermute | solution.py:26
  255.2 14.1 %collective-permute-start.28 = (bf16[24,3072]{1,0:T(8,128)(2,1)S(1)}, bf16[24,3072]{1,0:T(8,128)(2,1)S(1)}, u32[]{:S(2)}, u32[]{:S(2)}) collective-permute-start(bf16[24,3072]{1,0:T(8,128)(2,1)S(1)} %copy-done.40), channel_id=1, source_target_pairs={{0,16},{1,17},{2,18},{3,19},{4,20},{5,21},{6,22},{7,23},{8,24},{9,... | collective-permute-start | bytes 442376 | tf_op jit(solution)/shard_map/ppermute | solution.py:26
  274.6 14.1 %collective-permute-start.32 = (bf16[96,1536]{1,0:T(8,128)(2,1)}, bf16[96,1536]{1,0:T(8,128)(2,1)S(1)}, u32[]{:S(2)}, u32[]{:S(2)}) collective-permute-start(bf16[96,1536]{1,0:T(8,128)(2,1)} %get-tuple-element.177.refs_1_), channel_id=1, source_target_pairs={{0,4},{1,5},{2,6},{3,7},{4,0},{5,1},{6,2},{7,3},{8,12},{9,13},{10,... | collective-permute-start | bytes 884744 | tf_op jit(solution)/shard_map/ppermute | solution.py:26
  277.6 33.0 %all-to-all-start.2 = ((f32[32,1,4,768]{3,2,1,0:T(4,128)}), f32[32,1,4,768]{3,2,1,0:T(4,128)S(1)}, u32[]{:S(2)}, u32[]{:S(2)}) async-start(f32[32,1,4,768]{3,2,1,0:T(4,128)} %broadcast_in_dim.61), calls=%async_computation.2 | async-start | bytes 786432 | tf_op jit(solution)/shard_map/all_to_all | solution.py:46
  (63 other events, 515.9 us)
Sparse Core Ops, SparseCore 0:
  11.0 98.9 all-gather.1
